TPU v7x, 32 devices: a whole 2x2x4 slice. The times are simulated.
32 devices in a mesh: fsdp: 8 (over z, y), seq: 4 (over x, core).
Axes of the slice: x: 2, y: 2, z: 4, core: 2. Of those that a mesh axis runs over, the one named last changes fastest.
Arguments:
- hidden_in: bfloat16 [3, 4096, 768], P(None, ('fsdp', 'seq')), may hold values from -6 to 6
- row_types: int32 [3, 4096], P(None, ('fsdp', 'seq')), may hold values from 0 to 159, as said below
- lengths: int32 [3, 8, 8], P(None, 'fsdp'), may hold values from 1 to 384, as said below
- noise_time: float32 [3, 8, 8], P(None, 'fsdp'), may hold values from 0 to 1
- coords: float32 [3, 3, 4096], P(None, None, 'fsdp'), may hold values from -15 to 15
- residue_table: bfloat16 [32, 768], P(None, 'fsdp'), may hold values from -6 to 6
- atom_table: bfloat16 [128, 768], P(None, 'fsdp'), may hold values from -6 to 6
- time_weight: bfloat16 [768, 768], P('fsdp'), may hold values from -0.21875 to 0.21875
- first_gain: bfloat16 [768], P('fsdp'), may hold values from 0.25 to 1.75
- query_weight: bfloat16 [768, 768], P('fsdp'), may hold values from -0.21875 to 0.21875
- key_weight: bfloat16 [768, 768], P('fsdp'), may hold values from -0.21875 to 0.21875
- value_weight: bfloat16 [768, 768], P('fsdp'), may hold values from -0.21875 to 0.21875
- output_weight: bfloat16 [768, 768], P('fsdp'), may hold values from -1.75 to 1.75
- kernel_mean: bfloat16 [128], P('fsdp'), may hold values from 0.5 to 12
- kernel_width: bfloat16 [128], P('fsdp'), may hold values from 0.5 to 3
- pair_weight: bfloat16 [128, 32], P('fsdp'), may hold values from -12 to 12
- second_gain: bfloat16 [768], P('fsdp'), may hold values from 0.25 to 1.75
- up_weight: bfloat16 [768, 3072], P('fsdp'), may hold values from -0.21875 to 0.21875
- down_weight: bfloat16 [3072, 768], P('fsdp'), may hold values from -0.109375 to 0.109375
- force_weight: bfloat16 [3, 768], P(None, 'fsdp'), may hold values from -0.21875 to 0.21875
- layer_cot: bfloat16 [3, 4096, 768], P(None, ('fsdp', 'seq')), may hold values from -6 to 6
- force_cot: float32 [3, 3, 4096], P(None, None, ('fsdp', 'seq')), may hold values from -6 to 6
Outputs:
- layer_out: bfloat16 [3, 4096, 768], P(None, ('fsdp', 'seq'))
- forces: float32 [3, 3, 4096], P(None, None, ('fsdp', 'seq'))
- input_grad: float32 [3, 4096, 768], P(None, ('fsdp', 'seq'))
- residue_table_grad: float32 [32, 768], P(None, 'fsdp')
- atom_table_grad: float32 [128, 768], P(None, 'fsdp')
- time_weight_grad: float32 [768, 768], P('fsdp')
- first_gain_grad: float32 [768], P('fsdp')
- query_weight_grad: float32 [768, 768], P('fsdp')
- key_weight_grad: float32 [768, 768], P('fsdp')
- value_weight_grad: float32 [768, 768], P('fsdp')
- output_weight_grad: float32 [768, 768], P('fsdp')
- kernel_mean_grad: float32 [128], P('fsdp')
- kernel_width_grad: float32 [128], P('fsdp')
- pair_weight_grad: float32 [128, 32], P('fsdp')
- second_gain_grad: float32 [768], P('fsdp')
- up_weight_grad: float32 [768, 3072], P('fsdp')
- down_weight_grad: float32 [3072, 768], P('fsdp')
- force_weight_grad: float32 [3, 768], P(None, 'fsdp')
Inputs may be any that keep to these rules, and one draw needn't show every extreme that they name: In each group, document 1 is a protein of exactly 384 rows, document 0 ends before row 128 of the group, all documents have at least one row, and the lengths of a group sum to 512. `row_types`: rows of document 1 hold a residue type below 32; all other rows hold 32 plus an atom type below 128.
All inputs are finite; a program needn't handle non-finite values.
Results may differ from a plain program's by a relative error of at most 0.019.
Values may be sent and summed in bfloat16 or wider, within the bound.
No kernel may reach another device: no remote copies, remote signals or barrier semaphores. Data moves between devices by JAX's collectives and lax.ppermute only.
A program may use at most 192 MiB of HBM per device.

v0:
```python
import math

import jax
import jax.numpy as jnp
from jax import lax
from jax.sharding import PartitionSpec as P

NORM_EPS = 1e-05
EXACT_PRECISION = lax.Precision.HIGHEST


def dot_wide(left, right):
    return jnp.dot(left, right, preferred_element_type=jnp.float32)


def sinus_embed(stamps, model_width):
    half_width = model_width // 2
    frequency = jnp.exp(
        -math.log(10000.0) * jnp.arange(half_width).astype(jnp.float32) / half_width
    )
    angles = 1000.0 * stamps[:, None] * frequency[None, :]
    return jnp.concatenate([jnp.sin(angles), jnp.cos(angles)], axis=1)


def norm_forward(value, norm_gain):
    centre = value - jnp.mean(value, axis=-1, keepdims=True)
    inv_std = lax.rsqrt(jnp.mean(centre * centre, axis=-1, keepdims=True) + NORM_EPS)
    normed = centre * inv_std
    return (normed * norm_gain, normed, inv_std)


def norm_backward(grad_out, normed, inv_std, norm_gain):
    scaled = grad_out * norm_gain
    grad_in = inv_std * (
        scaled
        - jnp.mean(scaled, axis=-1, keepdims=True)
        - normed * jnp.mean(scaled * normed, axis=-1, keepdims=True)
    )
    return (grad_in, jnp.sum(grad_out * normed, axis=0))


def gaussians(query_pos, key_pos, kernel_mean, kernel_width):
    delta_pos = query_pos[:, :, None] - key_pos[:, None, :]
    distance = jnp.sqrt(jnp.sum(delta_pos * delta_pos, axis=0))
    standard = (distance[:, :, None] - kernel_mean) / kernel_width
    return (
        jnp.exp(-0.5 * standard * standard) / (math.sqrt(2.0 * math.pi) * kernel_width),
        standard,
    )


def pair_bias(query_pos, key_pos, kernel_mean, kernel_width, pair_weight):
    group_rows = key_pos.shape[1]
    block_rows = min(128, group_rows)
    blocks = group_rows // block_rows

    def one_block(block_index):
        offset = block_index * block_rows
        density, _ = gaussians(
            query_pos,
            lax.dynamic_slice_in_dim(key_pos, offset, block_rows, 1),
            kernel_mean,
            kernel_width,
        )
        return jnp.einsum(
            "ijk,kh->hij",
            density.astype(jnp.bfloat16),
            pair_weight,
            preferred_element_type=jnp.float32,
        )

    pieces = lax.map(one_block, jnp.arange(blocks, dtype=jnp.int32))
    return jnp.moveaxis(pieces, 0, 2).reshape(pair_weight.shape[1], query_pos.shape[1], group_rows)


def pair_grads(query_pos, key_pos, kernel_mean, kernel_width, pair_weight, score_low):
    group_rows = key_pos.shape[1]
    block_rows = min(128, group_rows)
    blocks = group_rows // block_rows

    def one_block(carry, block_index):
        offset = block_index * block_rows
        density, standard = gaussians(
            query_pos,
            lax.dynamic_slice_in_dim(key_pos, offset, block_rows, 1),
            kernel_mean,
            kernel_width,
        )
        piece = lax.dynamic_slice_in_dim(score_low, offset, block_rows, 2)
        weight_grad = carry[0] + jnp.einsum(
            "ijk,hij->kh", density.astype(jnp.bfloat16), piece, preferred_element_type=jnp.float32
        )
        dens_grad = (
            jnp.einsum("hij,kh->ijk", piece, pair_weight, preferred_element_type=jnp.float32)
            * density
        )
        mean_grad = carry[1] + jnp.sum(dens_grad * standard, axis=(0, 1)) / kernel_width
        width_grad = (
            carry[2] + jnp.sum(dens_grad * (standard * standard - 1.0), axis=(0, 1)) / kernel_width
        )
        return ((weight_grad, mean_grad, width_grad), None)

    kernels = pair_weight.shape[0]
    start_carry = (
        jnp.zeros(pair_weight.shape, jnp.float32),
        jnp.zeros((kernels,), jnp.float32),
        jnp.zeros((kernels,), jnp.float32),
    )
    result, _ = lax.scan(one_block, start_carry, jnp.arange(blocks, dtype=jnp.int32))
    return result


def attention_scores(queries, keys_all, bias_full, same_doc, head_count):
    query_rows, model_width = queries.shape
    head_dim = model_width // head_count
    scores = jnp.einsum(
        "ihd,jhd->hij",
        queries.reshape(query_rows, head_count, head_dim),
        keys_all.reshape(-1, head_count, head_dim),
        preferred_element_type=jnp.float32,
    ) * head_dim ** (-0.5)
    return jnp.where(same_doc[None], scores + bias_full, -1000000000.0)


def full_shape(piece, split_axis, factor):
    return tuple(
        (
            extent * factor if axis_no == split_axis else extent
            for axis_no, extent in enumerate(piece.shape)
        )
    )


def body(
    hidden_in,
    row_types,
    lengths,
    noise_time,
    coords,
    residue_table,
    atom_table,
    time_weight,
    first_gain,
    query_weight,
    key_weight,
    value_weight,
    output_weight,
    kernel_mean,
    kernel_width,
    pair_weight,
    second_gain,
    up_weight,
    down_weight,
    force_weight,
    layer_cot,
    force_cot,
):
    seq_count = lax.axis_size("seq")
    fsdp_count = lax.axis_size("fsdp")
    seq_index = lax.axis_index("seq")
    micro_count, tok_rows, model_width = hidden_in.shape
    group_rows = tok_rows * seq_count
    head_count = pair_weight.shape[1]
    head_dim = model_width // head_count
    inv_root = head_dim ** (-0.5)
    shards = (
        residue_table,
        atom_table,
        time_weight,
        first_gain,
        query_weight,
        key_weight,
        value_weight,
        output_weight,
        kernel_mean,
        kernel_width,
        pair_weight,
        second_gain,
        up_weight,
        down_weight,
        force_weight,
    )
    split_axes = (1, 1, 0, 0, 0, 0, 0, 0, 0, 0, 0, 0, 0, 0, 1)
    grad_totals = tuple(
        (
            jnp.zeros(full_shape(piece, split_axis, fsdp_count), jnp.float32)
            for piece, split_axis in zip(shards, split_axes)
        )
    )
    all_rows = jnp.arange(group_rows, dtype=jnp.int32)
    offset = seq_index * tok_rows
    out_list = []
    force_list = []
    grad_list = []
    for micro_index in range(micro_count):
        (
            residue_full,
            atom_full,
            time_full,
            gain_one,
            query_full,
            key_full,
            value_full,
            output_full,
            mean_full,
            width_full,
            pair_full,
            gain_two,
            up_full,
            down_full,
            force_full,
        ) = (
            lax.all_gather(residue_table, "fsdp", axis=1, tiled=True),
            lax.all_gather(atom_table, "fsdp", axis=1, tiled=True),
            lax.all_gather(time_weight, "fsdp", axis=0, tiled=True),
            lax.all_gather(first_gain, "fsdp", axis=0, tiled=True),
            lax.all_gather(query_weight, "fsdp", axis=0, tiled=True),
            lax.all_gather(key_weight, "fsdp", axis=0, tiled=True),
            lax.all_gather(value_weight, "fsdp", axis=0, tiled=True),
            lax.all_gather(output_weight, "fsdp", axis=0, tiled=True),
            lax.all_gather(kernel_mean, "fsdp", axis=0, tiled=True),
            lax.all_gather(kernel_width, "fsdp", axis=0, tiled=True),
            lax.all_gather(pair_weight, "fsdp", axis=0, tiled=True),
            lax.all_gather(second_gain, "fsdp", axis=0, tiled=True),
            lax.all_gather(up_weight, "fsdp", axis=0, tiled=True),
            lax.all_gather(down_weight, "fsdp", axis=0, tiled=True),
            lax.all_gather(force_weight, "fsdp", axis=1, tiled=True),
        )
        mean_wide = mean_full.astype(jnp.float32)
        width_wide = width_full.astype(jnp.float32)
        doc_lengths = lengths[micro_index, 0]
        stamps = noise_time[micro_index, 0]
        positions = coords[micro_index]
        bounds = jnp.cumsum(doc_lengths)
        key_doc = jnp.sum((all_rows[:, None] >= bounds[None, :]).astype(jnp.int32), axis=1)
        query_doc = lax.dynamic_slice_in_dim(key_doc, offset, tok_rows)
        query_pos = lax.dynamic_slice_in_dim(positions, offset, tok_rows, 1)
        same_doc = query_doc[:, None] == key_doc[None, :]
        row_kinds = row_types[micro_index]
        doc_hot = (
            query_doc[:, None] == jnp.arange(doc_lengths.shape[0], dtype=jnp.int32)[None, :]
        ).astype(jnp.float32)
        residue_hot = (
            row_kinds[:, None] == jnp.arange(residue_full.shape[0], dtype=jnp.int32)[None, :]
        ).astype(jnp.bfloat16)
        atom_hot = (
            (row_kinds - residue_full.shape[0])[:, None]
            == jnp.arange(atom_full.shape[0], dtype=jnp.int32)[None, :]
        ).astype(jnp.bfloat16)
        time_low = sinus_embed(stamps, model_width).astype(jnp.bfloat16)
        time_proj = dot_wide(time_low, time_full)
        start_state = (
            hidden_in[micro_index].astype(jnp.float32)
            + dot_wide(residue_hot, residue_full)
            + dot_wide(atom_hot, atom_full)
            + jnp.dot(doc_hot, time_proj, precision=EXACT_PRECISION)
        )
        normed_in, normed_one, inv_one = norm_forward(start_state, gain_one.astype(jnp.float32))
        attn_in = normed_in.astype(jnp.bfloat16)
        queries = dot_wide(attn_in, query_full).astype(jnp.bfloat16)
        keys_all, values_all = (
            lax.all_gather(
                dot_wide(attn_in, key_full).astype(jnp.bfloat16), "seq", axis=0, tiled=True
            ),
            lax.all_gather(
                dot_wide(attn_in, value_full).astype(jnp.bfloat16), "seq", axis=0, tiled=True
            ),
        )
        bias_full = pair_bias(query_pos, positions, mean_wide, width_wide, pair_full)
        scores = attention_scores(queries, keys_all, bias_full, same_doc, head_count)
        maximum = jnp.max(scores, axis=-1, keepdims=True)
        log_total = maximum + jnp.log(jnp.sum(jnp.exp(scores - maximum), axis=-1, keepdims=True))
        probs_low = jnp.exp(scores - log_total).astype(jnp.bfloat16)
        values_heads = values_all.reshape(group_rows, head_count, head_dim)
        attended = (
            jnp.einsum("hij,jhd->ihd", probs_low, values_heads, preferred_element_type=jnp.float32)
            .reshape(tok_rows, model_width)
            .astype(jnp.bfloat16)
        )
        mid_state = start_state + dot_wide(attended, output_full)
        normed_mid, normed_two, inv_two = norm_forward(mid_state, gain_two.astype(jnp.float32))
        ffn_in = normed_mid.astype(jnp.bfloat16)
        up_state = dot_wide(ffn_in, up_full)
        gelu_low = jax.nn.gelu(up_state, approximate=True).astype(jnp.bfloat16)
        layer_out = (mid_state + dot_wide(gelu_low, down_full)).astype(jnp.bfloat16)
        out_wide = layer_out.astype(jnp.float32)
        force_wide = force_full.astype(jnp.float32)
        out_list.append(layer_out)
        force_list.append(jnp.einsum("cd,id->ci", force_wide, out_wide, precision=EXACT_PRECISION))
        (
            residue_full,
            atom_full,
            time_full,
            gain_one,
            query_full,
            key_full,
            value_full,
            output_full,
            mean_full,
            width_full,
            pair_full,
            gain_two,
            up_full,
            down_full,
            force_full,
        ) = (
            lax.all_gather(residue_table, "fsdp", axis=1, tiled=True),
            lax.all_gather(atom_table, "fsdp", axis=1, tiled=True),
            lax.all_gather(time_weight, "fsdp", axis=0, tiled=True),
            lax.all_gather(first_gain, "fsdp", axis=0, tiled=True),
            lax.all_gather(query_weight, "fsdp", axis=0, tiled=True),
            lax.all_gather(key_weight, "fsdp", axis=0, tiled=True),
            lax.all_gather(value_weight, "fsdp", axis=0, tiled=True),
            lax.all_gather(output_weight, "fsdp", axis=0, tiled=True),
            lax.all_gather(kernel_mean, "fsdp", axis=0, tiled=True),
            lax.all_gather(kernel_width, "fsdp", axis=0, tiled=True),
            lax.all_gather(pair_weight, "fsdp", axis=0, tiled=True),
            lax.all_gather(second_gain, "fsdp", axis=0, tiled=True),
            lax.all_gather(up_weight, "fsdp", axis=0, tiled=True),
            lax.all_gather(down_weight, "fsdp", axis=0, tiled=True),
            lax.all_gather(force_weight, "fsdp", axis=1, tiled=True),
        )
        force_wide = force_full.astype(jnp.float32)
        mean_wide = mean_full.astype(jnp.float32)
        width_wide = width_full.astype(jnp.float32)
        forces_cot = force_cot[micro_index]
        out_grad = layer_cot[micro_index].astype(jnp.float32) + jnp.einsum(
            "ci,cd->id", forces_cot, force_wide, precision=EXACT_PRECISION
        )
        force_w_grad = jnp.einsum("ci,id->cd", forces_cot, out_wide, precision=EXACT_PRECISION)
        branch_low = out_grad.astype(jnp.bfloat16)
        down_w_grad = jnp.einsum(
            "if,id->fd", gelu_low, branch_low, preferred_element_type=jnp.float32
        )
        gelu_grad = jnp.einsum(
            "id,fd->if", branch_low, down_full, preferred_element_type=jnp.float32
        )
        _, gelu_pull = jax.vjp(lambda inner: jax.nn.gelu(inner, approximate=True), up_state)
        up_low = gelu_pull(gelu_grad)[0].astype(jnp.bfloat16)
        up_w_grad = jnp.einsum("id,if->df", ffn_in, up_low, preferred_element_type=jnp.float32)
        ffn_in_grad = jnp.einsum("if,df->id", up_low, up_full, preferred_element_type=jnp.float32)
        norm_part, gain_two_grad = norm_backward(
            ffn_in_grad, normed_two, inv_two, gain_two.astype(jnp.float32)
        )
        mid_grad = out_grad + norm_part
        attn_low = mid_grad.astype(jnp.bfloat16)
        output_w_grad = jnp.einsum(
            "id,ie->de", attended, attn_low, preferred_element_type=jnp.float32
        )
        attended_grad = (
            jnp.einsum("ie,de->id", attn_low, output_full, preferred_element_type=jnp.float32)
            .astype(jnp.bfloat16)
            .reshape(tok_rows, head_count, head_dim)
        )
        scores = attention_scores(queries, keys_all, bias_full, same_doc, head_count)
        probs = jnp.exp(scores - log_total)
        prob_grad = jnp.einsum(
            "ihd,jhd->hij", attended_grad, values_heads, preferred_element_type=jnp.float32
        )
        value_part = jnp.einsum(
            "hij,ihd->jhd",
            probs.astype(jnp.bfloat16),
            attended_grad,
            preferred_element_type=jnp.float32,
        ).reshape(group_rows, model_width)
        score_low = (
            probs * (prob_grad - jnp.sum(probs * prob_grad, axis=-1, keepdims=True))
        ).astype(jnp.bfloat16)
        query_low = (
            (
                jnp.einsum(
                    "hij,jhd->ihd",
                    score_low,
                    keys_all.reshape(group_rows, head_count, head_dim),
                    preferred_element_type=jnp.float32,
                )
                * inv_root
            )
            .reshape(tok_rows, model_width)
            .astype(jnp.bfloat16)
        )
        key_part = (
            jnp.einsum(
                "hij,ihd->jhd",
                score_low,
                queries.reshape(tok_rows, head_count, head_dim),
                preferred_element_type=jnp.float32,
            )
            * inv_root
        ).reshape(group_rows, model_width)
        key_sum, value_sum = (
            lax.psum_scatter(
                key_part.astype(jnp.bfloat16), "seq", scatter_dimension=0, tiled=True
            ).astype(jnp.float32),
            lax.psum_scatter(
                value_part.astype(jnp.bfloat16), "seq", scatter_dimension=0, tiled=True
            ).astype(jnp.float32),
        )
        key_low = key_sum.astype(jnp.bfloat16)
        value_low = value_sum.astype(jnp.bfloat16)
        query_w_grad = jnp.einsum(
            "id,ie->de", attn_in, query_low, preferred_element_type=jnp.float32
        )
        key_w_grad = jnp.einsum("id,ie->de", attn_in, key_low, preferred_element_type=jnp.float32)
        value_w_grad = jnp.einsum(
            "id,ie->de", attn_in, value_low, preferred_element_type=jnp.float32
        )
        attn_in_grad = (
            jnp.einsum("ie,de->id", query_low, query_full, preferred_element_type=jnp.float32)
            + jnp.einsum("ie,de->id", key_low, key_full, preferred_element_type=jnp.float32)
            + jnp.einsum("ie,de->id", value_low, value_full, preferred_element_type=jnp.float32)
        )
        norm_part_one, gain_one_grad = norm_backward(
            attn_in_grad, normed_one, inv_one, gain_one.astype(jnp.float32)
        )
        input_grad = mid_grad + norm_part_one
        grad_list.append(input_grad)
        residue_grad = jnp.einsum(
            "ir,id->rd", residue_hot.astype(jnp.float32), input_grad, precision=EXACT_PRECISION
        )
        atom_grad = jnp.einsum(
            "ir,id->rd", atom_hot.astype(jnp.float32), input_grad, precision=EXACT_PRECISION
        )
        time_grad_low = jnp.einsum(
            "in,id->nd", doc_hot, input_grad, precision=EXACT_PRECISION
        ).astype(jnp.bfloat16)
        time_w_grad = jnp.einsum(
            "nd,ne->de", time_low, time_grad_low, preferred_element_type=jnp.float32
        )
        pair_w_grad, mean_grad, width_grad = pair_grads(
            query_pos, positions, mean_wide, width_wide, pair_full, score_low
        )
        step_grads = (
            residue_grad,
            atom_grad,
            time_w_grad,
            gain_one_grad,
            query_w_grad,
            key_w_grad,
            value_w_grad,
            output_w_grad,
            mean_grad,
            width_grad,
            pair_w_grad,
            gain_two_grad,
            up_w_grad,
            down_w_grad,
            force_w_grad,
        )
        grad_totals = jax.tree.map(jnp.add, grad_totals, step_grads)
    reduced = (
        lax.psum_scatter(grad_totals[0], "fsdp", scatter_dimension=1, tiled=True),
        lax.psum_scatter(grad_totals[1], "fsdp", scatter_dimension=1, tiled=True),
        lax.psum_scatter(grad_totals[2], "fsdp", scatter_dimension=0, tiled=True),
        lax.psum_scatter(grad_totals[3], "fsdp", scatter_dimension=0, tiled=True),
        lax.psum_scatter(grad_totals[4], "fsdp", scatter_dimension=0, tiled=True),
        lax.psum_scatter(grad_totals[5], "fsdp", scatter_dimension=0, tiled=True),
        lax.psum_scatter(grad_totals[6], "fsdp", scatter_dimension=0, tiled=True),
        lax.psum_scatter(grad_totals[7], "fsdp", scatter_dimension=0, tiled=True),
        lax.psum_scatter(grad_totals[8], "fsdp", scatter_dimension=0, tiled=True),
        lax.psum_scatter(grad_totals[9], "fsdp", scatter_dimension=0, tiled=True),
        lax.psum_scatter(grad_totals[10], "fsdp", scatter_dimension=0, tiled=True),
        lax.psum_scatter(grad_totals[11], "fsdp", scatter_dimension=0, tiled=True),
        lax.psum_scatter(grad_totals[12], "fsdp", scatter_dimension=0, tiled=True),
        lax.psum_scatter(grad_totals[13], "fsdp", scatter_dimension=0, tiled=True),
        lax.psum_scatter(grad_totals[14], "fsdp", scatter_dimension=1, tiled=True),
    )
    summed = (
        lax.psum(reduced[0].astype(jnp.bfloat16), "seq").astype(jnp.float32),
        lax.psum(reduced[1].astype(jnp.bfloat16), "seq").astype(jnp.float32),
        lax.psum(reduced[2].astype(jnp.bfloat16), "seq").astype(jnp.float32),
        lax.psum(reduced[3].astype(jnp.bfloat16), "seq").astype(jnp.float32),
        lax.psum(reduced[4].astype(jnp.bfloat16), "seq").astype(jnp.float32),
        lax.psum(reduced[5].astype(jnp.bfloat16), "seq").astype(jnp.float32),
        lax.psum(reduced[6].astype(jnp.bfloat16), "seq").astype(jnp.float32),
        lax.psum(reduced[7].astype(jnp.bfloat16), "seq").astype(jnp.float32),
        lax.psum(reduced[8].astype(jnp.bfloat16), "seq").astype(jnp.float32),
        lax.psum(reduced[9].astype(jnp.bfloat16), "seq").astype(jnp.float32),
        lax.psum(reduced[10].astype(jnp.bfloat16), "seq").astype(jnp.float32),
        lax.psum(reduced[11].astype(jnp.bfloat16), "seq").astype(jnp.float32),
        lax.psum(reduced[12].astype(jnp.bfloat16), "seq").astype(jnp.float32),
        lax.psum(reduced[13].astype(jnp.bfloat16), "seq").astype(jnp.float32),
        lax.psum(reduced[14].astype(jnp.bfloat16), "seq").astype(jnp.float32),
    )
    return (
        jnp.stack(out_list),
        jnp.stack(force_list),
        jnp.stack(grad_list),
        summed[0],
        summed[1],
        summed[2],
        summed[3],
        summed[4],
        summed[5],
        summed[6],
        summed[7],
        summed[8],
        summed[9],
        summed[10],
        summed[11],
        summed[12],
        summed[13],
        summed[14],
    )


def solution(mesh):
    return jax.shard_map(
        body,
        mesh=mesh,
        in_specs=(
            P(None, ("fsdp", "seq"), None),
            P(None, ("fsdp", "seq")),
            P(None, "fsdp", None),
            P(None, "fsdp", None),
            P(None, None, "fsdp"),
            P(None, "fsdp"),
            P(None, "fsdp"),
            P("fsdp", None),
            P("fsdp"),
            P("fsdp", None),
            P("fsdp", None),
            P("fsdp", None),
            P("fsdp", None),
            P("fsdp"),
            P("fsdp"),
            P("fsdp", None),
            P("fsdp"),
            P("fsdp", None),
            P("fsdp", None),
            P(None, "fsdp"),
            P(None, ("fsdp", "seq"), None),
            P(None, None, ("fsdp", "seq")),
        ),
        out_specs=(
            P(None, ("fsdp", "seq"), None),
            P(None, None, ("fsdp", "seq")),
            P(None, ("fsdp", "seq"), None),
            P(None, "fsdp"),
            P(None, "fsdp"),
            P("fsdp", None),
            P("fsdp"),
            P("fsdp", None),
            P("fsdp", None),
            P("fsdp", None),
            P("fsdp", None),
            P("fsdp"),
            P("fsdp"),
            P("fsdp", None),
            P("fsdp"),
            P("fsdp", None),
            P("fsdp", None),
            P(None, "fsdp"),
        ),
        check_vma=False,
    )
```

profile of v0, /device:TPU:0, one launch (start us, length us, event | category | flops | bytes accessed | tf_op | source)
XLA Modules:
  0.0 1695.0 jit_solution(3282775199643666342)
XLA Ops:
  15.2 35.2 %all_gather.43 = bf16[128,768]{0,1:T(8,128)(2,1)} all-gather(bf16[128,96]{0,1:T(8,128)(2,1)} %param.40), channel_id=1, replica_groups=mesh['fsdp'=8,'seq'=4] {'fsdp'}, dimensions={1}, use_global_device_ids=true | all-gather | bytes 221184 | tf_op jit(solution)/shard_map/all_gather | solution.py:214
  62.0 22.2 %all-reduce.9 = (bf16[128]{0:T(256)(128)(2,1)S(1)}, bf16[128]{0:T(256)(128)(2,1)S(1)}, bf16[768]{0:T(1024)(128)(2,1)}, bf16[768]{0:T(1024)(128)(2,1)}) all-reduce(bf16[128]{0:T(256)(128)(2,1)S(1)} %dynamic-update-slice.1, bf16[128]{0:T(256)(128)(2,1)S(1)} %dynamic-update-slice.2, ...), channel_id=1, replica_groups=mesh['fsdp'=8,'seq'=4] {'fsdp'}, use_global_device_ids=true, to_apply=%add.1 | all-reduce | flops 1792 | bytes 7168
  84.3 30.7 %all_gather.53 = bf16[128,32]{1,0:T(8,128)(2,1)S(1)} all-gather(bf16[16,32]{1,0:T(8,128)(2,1)} %param.49), channel_id=1, replica_groups=mesh['fsdp'=8,'seq'=4] {'fsdp'}, dimensions={0}, use_global_device_ids=true | all-gather | bytes 9216 | tf_op jit(solution)/shard_map/all_gather | solution.py:223
  119.4 27.2 %while.81 = (s32[]{:T(128)}, f32[4,32,128,128]{3,1,2,0:T(8,128)}, f32[3,128]{1,0:T(4,128)S(1)}, s32[4]{0:T(128)S(1)}, f32[3,512]{1,0:T(4,128)S(1)}, /*index=5*/f...) while((s32[]{:T(128)}, f32[4,32,128,128]{3,1,2,0:T(8,128)}, ...), condition=%wide.region_6.7_spmd, body=%wide.region_4.6_spmd.sunk | while | flops 146931840 | bytes 2376383 | solution.py:72
  153.9 29.8 %while.83 = (s32[]{:T(128)}, f32[4,32,128,128]{3,1,2,0:T(8,128)}, f32[3,128]{1,0:T(4,128)S(1)}, s32[4]{0:T(128)S(1)}, f32[3,512]{1,0:T(4,128)}, /*index=5*/f32[1...) while((s32[]{:T(128)}, f32[4,32,128,128]{3,1,2,0:T(8,128)}, ...), condition=%wide.region_28.29_spmd, body=%wide.region_26.28_spmd.sunk | while | flops 146931840 | bytes 2376383 | solution.py:72
  188.9 29.9 %while.82 = (s32[]{:T(128)}, f32[4,32,128,128]{3,1,2,0:T(8,128)}, f32[3,128]{1,0:T(4,128)S(1)}, s32[4]{0:T(128)S(1)}, f32[3,512]{1,0:T(4,128)}, /*index=5*/f32[1...) while((s32[]{:T(128)}, f32[4,32,128,128]{3,1,2,0:T(8,128)}, ...), condition=%wide.region_17.18_spmd, body=%wide.region_15.17_spmd.sunk | while | flops 146931840 | bytes 2376383 | solution.py:72
  220.4 30.8 %all-gather = bf16[8,96,32]{1,2,0:T(8,128)(2,1)S(1)} all-gather(bf16[1,96,32]{1,2,0:T(8,128)(2,1)S(1)} %bitcast.472), channel_id=1, replica_groups=mesh['fsdp'=8,'seq'=4] {'fsdp'}, dimensions={0}, use_global_device_ids=true | all-gather | bytes 55296 | tf_op jit(solution)/shard_map/all_gather | solution.py:213
  251.3 16.8 all-gather.1
  268.3 12.1 copy.188
  431.5 24.2 %reduce-scatter.54.cloned.1.call-done = bf16[128,768]{1,0:T(8,128)(2,1)} async-done(((bf16[512,768]{1,0:T(8,128)(2,1)}), bf16[128,768]{1,0:T(8,128)(2,1)}) %reduce-scatter.54.cloned.1.call-update) | async-done | bytes 196624
  653.6 23.6 %reduce-scatter.62.cloned.1.call-done = bf16[128,768]{1,0:T(8,128)(2,1)} async-done(((bf16[512,768]{1,0:T(8,128)(2,1)}), bf16[128,768]{1,0:T(8,128)(2,1)}) %reduce-scatter.62.cloned.1.call-update) | async-done | bytes 196624
  689.6 51.9 %while.84 = (s32[]{:T(128)}, f32[128,32]{0,1:T(8,128)S(1)}, f32[128]{0:T(128)S(1)}, f32[128]{0:T(128)S(1)}, f32[3,128]{1,0:T(4,128)S(1)}, /*index=5*/s32[4]{0:T(...) while((s32[]{:T(128)}, f32[128,32]{0,1:T(8,128)S(1)}, ...), condition=%wide.region_77.78_spmd.clone, body=%wide.region_73.77_spmd.clone.sunk | while | flops 306324096 | bytes 4578018 | solution.py:109
  794.8 51.9 %while.86 = (s32[]{:T(128)}, f32[128,32]{0,1:T(8,128)S(1)}, f32[128]{0:T(128)S(1)}, f32[128]{0:T(128)S(1)}, f32[3,128]{1,0:T(4,128)S(1)}, /*index=5*/s32[4]{0:T(...) while((s32[]{:T(128)}, f32[128,32]{0,1:T(8,128)S(1)}, ...), condition=%wide.region_87.88_spmd.clone, body=%wide.region_83.87_spmd.clone.sunk | while | flops 306324096 | bytes 4578018 | solution.py:109
  847.6 52.0 %while.85 = (s32[]{:T(128)}, f32[128,32]{0,1:T(8,128)S(1)}, f32[128]{0:T(128)S(1)}, f32[128]{0:T(128)S(1)}, f32[3,128]{1,0:T(4,128)S(1)}, /*index=5*/s32[4]{0:T(...) while((s32[]{:T(128)}, f32[128,32]{0,1:T(8,128)S(1)}, ...), condition=%wide.region_82.83_spmd.clone, body=%wide.region_78.82_spmd.clone.sunk | while | flops 306324096 | bytes 4610814 | solution.py:109
  911.2 53.2 %reduce-scatter.42.cloned.1.call-done = f32[96,768]{1,0:T(8,128)} async-done(((f32[768,768]{1,0:T(8,128)}), f32[96,768]{1,0:T(8,128)}) %reduce-scatter.42.cloned.1.call-update) | async-done | bytes 294928 | tf_op jit(solution)/shard_map/reduce_scatter | solution.py:457
  966.0 69.8 %reduce-scatter.44.cloned.1.call-done = f32[96,768]{1,0:T(8,128)} async-done(((f32[768,768]{1,0:T(8,128)}), f32[96,768]{1,0:T(8,128)}) %reduce-scatter.44.cloned.1.call-update) | async-done | bytes 294928 | tf_op jit(solution)/shard_map/reduce_scatter | solution.py:458
  1037.5 164.5 %reduce-scatter.48.cloned.1.call-done = f32[96,3072]{1,0:T(8,128)} async-done(((f32[768,3072]{1,0:T(8,128)}), f32[96,3072]{1,0:T(8,128)}) %reduce-scatter.48.cloned.1.call-update) | async-done | bytes 1179664 | tf_op jit(solution)/shard_map/reduce_scatter | solution.py:464
  1204.1 163.9 %reduce-scatter.50.cloned.1.call-done = f32[384,768]{1,0:T(8,128)} async-done(((f32[3072,768]{1,0:T(8,128)}), f32[384,768]{1,0:T(8,128)}) %reduce-scatter.50.cloned.1.call-update) | async-done | bytes 1179664 | tf_op jit(solution)/shard_map/reduce_scatter | solution.py:465
  1371.7 60.6 %reduce-scatter.68.cloned.1.call-done = f32[96,3]{1,0:T(8,128)} async-done(((f32[768,3]{1,0:T(8,128)}), f32[96,3]{1,0:T(8,128)}) %reduce-scatter.68.cloned.1.call-update) | async-done | bytes 1168
  1433.2 62.9 %reduce-scatter.66.cloned.1.call-done = f32[16,32]{1,0:T(8,128)} async-done(((f32[128,32]{1,0:T(8,128)}), f32[16,32]{1,0:T(8,128)}) %reduce-scatter.66.cloned.1.call-update) | async-done | bytes 2064
  1496.9 35.2 %all-reduce.8 = (bf16[768]{0:T(1024)(128)(2,1)S(1)}, bf16[128]{0:T(256)(128)(2,1)S(1)}, bf16[128]{0:T(256)(128)(2,1)S(1)}, bf16[768]{0:T(1024)(128)(2,1)S(1)}) all-reduce(f32[768]{0:T(1024)S(1)} %add_add_fusion.9, f32[128]{0:T(128)S(1)} %add_add_fusion.11, ...), channel_id=11, replica_groups=mesh['fsdp'=8,'seq'=4] {'fsdp'}, use_global_device_ids=true, to_apply=%region_63.64.clone | all-reduce | flops 1792 | bytes 10752
  1533.5 26.3 %reduce-scatter.64.cloned.1.call-done = f32[96,32]{1,0:T(8,128)} async-done(((f32[768,32]{1,0:T(8,128)}), f32[96,32]{1,0:T(8,128)}) %reduce-scatter.64.cloned.1.call-update) | async-done | bytes 12304
  1560.7 62.7 %reduce-scatter.36.cloned.1.call-done = f32[128,96]{0,1:T(8,128)} async-done(((f32[128,768]{0,1:T(8,128)}), f32[128,96]{0,1:T(8,128)}) %reduce-scatter.36.cloned.1.call-update) | async-done | bytes 49168 | tf_op jit(solution)/shard_map/reduce_scatter | solution.py:453
  1639.3 37.4 %all-reduce.14.cloned.1.call-done = (bf16[96,768]{1,0:T(8,128)(2,1)}, bf16[96,768]{1,0:T(8,128)(2,1)}, bf16[96,768]{1,0:T(8,128)(2,1)}, bf16[96,768]{1,0:T(8,128...) async-done(((bf16[96,768]{1,0:T(8,128)(2,1)}, bf16[96,768]{1,0:T(8,128)(2,1)}, bf16[96,768]{1,0:T(8,128)(2,1)}, ...) | async-done | bytes 1916944 | tf_op jit(solution)/shard_map/psum | solution.py:471
  (1013 shorter events, 726.0 us)
Async XLA Ops:
  7.2 335.7 %all-gather.10.cloned.1.call-start = ((), (), s32[]{:S(2)}) async-start(), calls=%async_computation.17 | async-start | bytes 1327104 | tf_op jit(solution)/shard_map/all_gather | solution.py:215
  7.9 337.7 %all-gather.12.cloned.1.call-start = ((), (), s32[]{:S(2)}) async-start(), calls=%async_computation.18 | async-start | bytes 1327104 | tf_op jit(solution)/shard_map/all_gather | solution.py:219
  8.7 347.5 %all-gather.14.cloned.1.call-start = ((), (), s32[]{:S(2)}) async-start(), calls=%async_computation.19 | async-start | bytes 1327104 | tf_op jit(solution)/shard_map/all_gather | solution.py:217
  9.4 348.9 %all-gather.16.cloned.1.call-start = ((), (), s32[]{:S(2)}) async-start(), calls=%async_computation.20 | async-start | bytes 1327104 | tf_op jit(solution)/shard_map/all_gather | solution.py:218
  10.0 370.1 %all-gather.18.cloned.1.call-start = ((), (), s32[]{:S(2)}) async-start(), calls=%async_computation.21 | async-start | bytes 1327104 | tf_op jit(solution)/shard_map/all_gather | solution.py:220
  10.6 373.0 %all-gather.20.cloned.1.call-start = ((), (), s32[]{:S(2)}) async-start(), calls=%async_computation.22 | async-start | bytes 5308416 | tf_op jit(solution)/shard_map/all_gather | solution.py:225
  11.1 375.6 %all-gather.22.cloned.1.call-start = ((), (), s32[]{:S(2)}) async-start(), calls=%async_computation.23 | async-start | bytes 5308416 | tf_op jit(solution)/shard_map/all_gather | solution.py:226
  11.9 417.2 %reduce-scatter.52.cloned.1.call-start = ((), (), s32[]{:S(2)}) async-start(), calls=%async_computation.32 | async-start | bytes 983040
  415.2 221.7 %reduce-scatter.56.cloned.1.call-start = ((), (), s32[]{:S(2)}) async-start(), calls=%async_computation.34 | async-start | bytes 983040
  575.2 64.1 %reduce-scatter.58.cloned.1.call-start = ((), (), s32[]{:S(2)}) async-start(), calls=%async_computation.35 | async-start | bytes 983040
  590.1 61.1 %reduce-scatter.60.cloned.1.call-start = ((), (), s32[]{:S(2)}) async-start(), calls=%async_computation.36 | async-start | bytes 983040
  605.0 72.3 %reduce-scatter.62.cloned.1.call-start = ((), (), s32[]{:S(2)}) async-start(), calls=%async_computation.37 | async-start | bytes 983040
  613.2 292.9 %reduce-scatter.40.cloned.1.call-start = ((), (), s32[]{:S(2)}) async-start(), calls=%async_computation.26 | async-start | bytes 2654208 | tf_op jit(solution)/shard_map/reduce_scatter | solution.py:456
  623.0 284.8 %reduce-scatter.46.cloned.1.call-start = ((), (), s32[]{:S(2)}) async-start(), calls=%async_computation.29 | async-start | bytes 2654208 | tf_op jit(solution)/shard_map/reduce_scatter | solution.py:459
  628.3 281.2 %reduce-scatter.38.cloned.1.call-start = ((), (), s32[]{:S(2)}) async-start(), calls=%async_computation.25 | async-start | bytes 2654208 | tf_op jit(solution)/shard_map/reduce_scatter | solution.py:454
  686.0 278.3 %reduce-scatter.42.cloned.1.call-start = ((), (), s32[]{:S(2)}) async-start(), calls=%async_computation.27 | async-start | bytes 2654208 | tf_op jit(solution)/shard_map/reduce_scatter | solution.py:457
  689.4 346.4 %reduce-scatter.44.cloned.1.call-start = ((), (), s32[]{:S(2)}) async-start(), calls=%async_computation.28 | async-start | bytes 2654208 | tf_op jit(solution)/shard_map/reduce_scatter | solution.py:458
  749.8 452.1 %reduce-scatter.48.cloned.1.call-start = ((), (), s32[]{:S(2)}) async-start(), calls=%async_computation.30 | async-start | bytes 10616832 | tf_op jit(solution)/shard_map/reduce_scatter | solution.py:464
  782.0 586.0 %reduce-scatter.50.cloned.1.call-start = ((), (), s32[]{:S(2)}) async-start(), calls=%async_computation.31 | async-start | bytes 10616832 | tf_op jit(solution)/shard_map/reduce_scatter | solution.py:465
  847.4 584.9 %reduce-scatter.68.cloned.1.call-start = ((), (), s32[]{:S(2)}) async-start(), calls=%async_computation.40 | async-start | bytes 442368
  899.7 596.3 %reduce-scatter.66.cloned.1.call-start = ((), (), s32[]{:S(2)}) async-start(), calls=%async_computation.39 | async-start | bytes 73728
  900.5 659.3 %reduce-scatter.64.cloned.1.call-start = ((), (), s32[]{:S(2)}) async-start(), calls=%async_computation.38 | async-start | bytes 442368
  902.8 720.5 %reduce-scatter.36.cloned.1.call-start = ((), (), s32[]{:S(2)}) async-start(), calls=%async_computation.24 | async-start | bytes 442368 | tf_op jit(solution)/shard_map/reduce_scatter | solution.py:453
  904.2 772.5 %all-reduce.14.cloned.1.call-start = ((), (), s32[]{:S(2)}) async-start(), calls=%async_computation.41 | async-start | bytes 3833856 | tf_op jit(solution)/shard_map/psum | solution.py:471
  (244 other events, 8533.3 us)
Sparse Core Ops, SparseCore 0:
  10.2 44.4 all-gather.9
  56.9 40.3 all-gather.11
  99.4 39.9 all-gather.13
  141.5 39.7 all-gather.15
  183.3 39.9 all-gather.17
  225.3 78.8 all-gather.19
  306.4 78.1 all-gather.21
  432.4 23.2 reduce-scatter.53
  575.3 23.6 reduce-scatter.55
  601.7 23.2 reduce-scatter.57
  628.0 23.2 reduce-scatter.59
  653.9 23.2 reduce-scatter.61
  680.6 69.0 reduce-scatter.39
  753.1 68.1 reduce-scatter.45
  824.7 68.2 reduce-scatter.37
  896.3 68.0 reduce-scatter.41
  967.7 68.0 reduce-scatter.43
  1039.4 162.4 reduce-scatter.47
  1205.4 162.5 reduce-scatter.49
  1371.8 60.4 reduce-scatter.67
  1435.7 60.3 reduce-scatter.65
  1499.3 60.4 reduce-scatter.63
  1562.9 60.3 reduce-scatter.35
  1628.0 48.6 all-reduce.13
  (1 shorter events, 21.6 us)
where the time goes:
time: 1700 us; the launch traced here: 1690 us
  waiting for transfers between devices  768 us (45%)
  matrix products  394 us (23%)
  blocking collectives  235 us (14%)
  local copies, waits for them, and re-layouts  195 us (11%)
  other arithmetic  63.4 us (4%)
  between operations  20 us (1%)
    unnamed x34, waiting for transfers between devices  217 us
    reduce_scatter x1, waiting for transfers between devices, body(): lax.psum_scatter(grad_totals[12], 'fsdp', scatter_dimension=0, tiled=True)  164 us
    reduce_scatter x1, waiting for transfers between devices, body(): lax.psum_scatter(grad_totals[13], 'fsdp', scatter_dimension=0, tiled=True)  164 us
    dot_general x12, matrix products, one_block(): jnp.einsum('hij,kh->ijk', piece, pair_weight, preferred_element_type=jnp....  81.5 us
    reduce_scatter x1, waiting for transfers between devices, body(): lax.psum_scatter(grad_totals[6], 'fsdp', scatter_dimension=0, tiled=True)  69.8 us
    dot_general x12, matrix products, one_block(): jnp.einsum('ijk,kh->hij', density.astype(jnp.bfloat16), pair_weight, pref...  64.5 us
    reduce_scatter x1, waiting for transfers between devices, body(): lax.psum_scatter(grad_totals[1], 'fsdp', scatter_dimension=1, tiled=True)  62.7 us
    unnamed x2, blocking collectives  57.5 us
  transfers between devices with their start and end apart: 25, of which 13 were waited for; matrix products, arithmetic and copies ran while one was open for 31% of the time, Pallas kernels for 0%

commit v1 on v0

v1 whole, which is shorter than its diff:
```python
import functools
import math

import jax
import jax.numpy as jnp
from jax import lax
from jax.experimental import pallas as pl
from jax.experimental.pallas import tpu as pltpu
from jax.sharding import PartitionSpec as P

NORM_EPS = 1e-05
PROTEIN_ROWS = 384
LANES = 128
HEAD_PAD = 32
TILE_ROWS = 8
LOG2E = math.log2(math.e)
VMEM_LIMIT = 56 * 2**20
EXACT = lax.Precision.HIGHEST
bf16 = jnp.bfloat16
f32 = jnp.float32


def dot_wide(left, right):
    return jnp.dot(left, right, preferred_element_type=f32)


def dot_tn(left, right):
    return lax.dot_general(left, right, (((0,), (0,)), ((), ())), preferred_element_type=f32)


def dot_nt(left, right):
    return lax.dot_general(left, right, (((1,), (1,)), ((), ())), preferred_element_type=f32)


def sinus_embed(stamps, model_width):
    half_width = model_width // 2
    frequency = jnp.exp(-math.log(10000.0) * jnp.arange(half_width).astype(f32) / half_width)
    angles = 1000.0 * stamps[..., None] * frequency
    return jnp.concatenate([jnp.sin(angles), jnp.cos(angles)], axis=-1)


def norm_forward(value, norm_gain):
    centre = value - jnp.mean(value, axis=-1, keepdims=True)
    inv_std = lax.rsqrt(jnp.mean(centre * centre, axis=-1, keepdims=True) + NORM_EPS)
    normed = centre * inv_std
    return normed * norm_gain, normed, inv_std


def norm_backward(grad_out, normed, inv_std, norm_gain):
    scaled = grad_out * norm_gain
    grad_in = inv_std * (
        scaled
        - jnp.mean(scaled, axis=-1, keepdims=True)
        - normed * jnp.mean(scaled * normed, axis=-1, keepdims=True)
    )
    return grad_in, jnp.sum(grad_out * normed, axis=0)


def density_rows(spans, mean_ref, coef_ref, powers):
    kernels = mean_ref.shape[0]
    tiles = spans[0].shape[1] // LANES
    parts = [[] for _ in range(powers)]
    for start in range(0, kernels, 16):
        mean = mean_ref[start : start + 16, :]
        coef = coef_ref[start : start + 16, :]
        pieces = [[] for _ in range(powers)]
        for span in spans:
            for tile in range(tiles):
                shift = span[:, tile * LANES : (tile + 1) * LANES] - mean
                dens = jnp.exp2(shift * shift * coef).astype(bf16)
                pieces[0].append(dens)
                if powers > 1:
                    low = shift.astype(bf16)
                    once = dens * low
                    pieces[1].append(once)
                    pieces[2].append(once * low)
        for power in range(powers):
            parts[power].append(jnp.concatenate(pieces[power], axis=1))
    return jnp.concatenate([piece for part in parts for piece in part], axis=0)


def bias_kernel(flag_ref, dist_ref, mask_ref, mean_ref, coef_ref, weight_ref, out_ref):
    micro = pl.program_id(0)
    row_count, columns = dist_ref.shape
    heads = weight_ref.shape[0]
    long_tiles = PROTEIN_ROWS // LANES
    all_tiles = columns // LANES

    def fill(base, first, tiles):
        empty = jnp.full((TILE_ROWS, LANES), -1e30, f32)
        for tile in range(first, first + tiles):
            for head in range(heads):
                out_ref[tile, pl.ds(head * row_count + base, TILE_ROWS), :] = empty

    def compute(base, first, tiles, batch):
        span = slice(first * LANES, (first + tiles) * LANES)
        dist = dist_ref[pl.ds(base, TILE_ROWS), span]
        mask = mask_ref[pl.ds(base, TILE_ROWS), span]
        for start in range(0, TILE_ROWS, batch):
            rows = range(start, start + batch)
            dens = density_rows([dist[row : row + 1] for row in rows], mean_ref, coef_ref, 1)
            bias = dot_wide(weight_ref[...], dens)
            for row in rows:
                for tile in range(tiles):
                    at = ((row - start) * tiles + tile) * LANES
                    out_ref[first + tile, pl.ds(base + row, heads, stride=row_count), :] = (
                        bias[:, at : at + LANES]
                        + mask[row : row + 1, tile * LANES : (tile + 1) * LANES]
                    )

    def one_tile(tile_index, carry):
        base = pl.multiple_of(tile_index * TILE_ROWS, TILE_ROWS)
        flag = flag_ref[micro, tile_index]

        @pl.when(flag != 1)
        def _():
            compute(base, 0, long_tiles, 2)

        @pl.when(flag == 1)
        def _():
            fill(base, 0, long_tiles)

        @pl.when(flag != 0)
        def _():
            compute(base, long_tiles, all_tiles - long_tiles, TILE_ROWS)

        @pl.when(flag == 0)
        def _():
            fill(base, long_tiles, all_tiles - long_tiles)

        return carry

    lax.fori_loop(0, row_count // TILE_ROWS, one_tile, 0)


def pair_bias(flags, dist, mask, mean_wide, coef_wide, weight):
    micro_count, row_count, columns = dist.shape
    heads, kernels = weight.shape
    block = pl.BlockSpec((None, row_count, columns), lambda m: (m, 0, 0))
    wide = pl.BlockSpec((kernels, LANES), lambda m: (0, 0))
    return pl.pallas_call(
        bias_kernel,
        grid=(micro_count,),
        in_specs=[
            pl.BlockSpec(memory_space=pltpu.SMEM),
            block,
            block,
            wide,
            wide,
            pl.BlockSpec((heads, kernels), lambda m: (0, 0)),
        ],
        out_specs=pl.BlockSpec(
            (None, columns // LANES, heads * row_count, LANES), lambda m: (m, 0, 0, 0)
        ),
        out_shape=jax.ShapeDtypeStruct(
            (micro_count, columns // LANES, heads * row_count, LANES), f32
        ),
        compiler_params=pltpu.CompilerParams(vmem_limit_bytes=VMEM_LIMIT),
        name="pair_bias",
    )(flags, dist, mask, mean_wide, coef_wide, weight)


def pair_grad_kernel(flag_ref, dist_ref, score_ref, mean_ref, coef_ref, out_ref):
    micro = pl.program_id(0)
    row_count, columns = dist_ref.shape
    heads = score_ref.shape[1] // row_count
    long_tiles = PROTEIN_ROWS // LANES
    all_tiles = columns // LANES
    out_ref[...] = jnp.zeros_like(out_ref)

    def compute(base, first, tiles, batch):
        total = out_ref[...]
        span = slice(first * LANES, (first + tiles) * LANES)
        dist = dist_ref[pl.ds(base, TILE_ROWS), span]
        for start in range(0, TILE_ROWS, batch):
            rows = range(start, start + batch)
            dens = density_rows([dist[row : row + 1] for row in rows], mean_ref, coef_ref, 3)
            score = jnp.concatenate(
                [
                    score_ref[first + tile, pl.ds(base + row, heads, stride=row_count), :]
                    for row in rows
                    for tile in range(tiles)
                ],
                axis=1,
            ).astype(bf16)
            total = total + dot_nt(score, dens)
        out_ref[...] = total

    def one_tile(tile_index, carry):
        base = pl.multiple_of(tile_index * TILE_ROWS, TILE_ROWS)
        flag = flag_ref[micro, tile_index]

        @pl.when(flag != 1)
        def _():
            compute(base, 0, long_tiles, 2)

        @pl.when(flag != 0)
        def _():
            compute(base, long_tiles, all_tiles - long_tiles, TILE_ROWS)

        return carry

    lax.fori_loop(0, row_count // TILE_ROWS, one_tile, 0)


def pair_grads(flags, dist, score_cot, mean_wide, coef_wide):
    micro_count, row_count, columns = dist.shape
    kernels = mean_wide.shape[0]
    heads = score_cot.shape[2] // row_count
    wide = pl.BlockSpec((kernels, LANES), lambda m: (0, 0))
    return pl.pallas_call(
        pair_grad_kernel,
        grid=(micro_count,),
        in_specs=[
            pl.BlockSpec(memory_space=pltpu.SMEM),
            pl.BlockSpec((None, row_count, columns), lambda m: (m, 0, 0)),
            pl.BlockSpec((None,) + score_cot.shape[1:], lambda m: (m, 0, 0, 0)),
            wide,
            wide,
        ],
        out_specs=pl.BlockSpec((None, heads, 3 * kernels), lambda m: (m, 0, 0)),
        out_shape=jax.ShapeDtypeStruct((micro_count, heads, 3 * kernels), f32),
        compiler_params=pltpu.CompilerParams(vmem_limit_bytes=VMEM_LIMIT),
        name="pair_grads",
    )(flags, dist, score_cot, mean_wide, coef_wide)


def head_stack(tile):
    lane_head = lax.broadcasted_iota(jnp.int32, (1, LANES), 1) // HEAD_PAD
    return jnp.concatenate(
        [
            jnp.where(lane_head == head, tile, jnp.zeros_like(tile))
            for head in range(LANES // HEAD_PAD)
        ],
        axis=0,
    )


def head_merge(stacked, row_count):
    lane_head = lax.broadcasted_iota(jnp.int32, (1, LANES), 1) // HEAD_PAD
    merged = stacked[:row_count]
    for head in range(1, LANES // HEAD_PAD):
        merged = jnp.where(
            lane_head == head, stacked[head * row_count : (head + 1) * row_count], merged
        )
    return merged


def attend_kernel(scale, query_ref, key_ref, value_ref, bias_ref, prob_ref, out_ref):
    row_count = query_ref.shape[0]
    tiles = bias_ref.shape[0]
    scores = dot_nt(head_stack(query_ref[...]), key_ref[...]) * scale
    scores = scores + jnp.concatenate([bias_ref[tile] for tile in range(tiles)], axis=1)
    exps = jnp.exp2(scores - jnp.max(scores, axis=1, keepdims=True))
    probs = (exps * (1.0 / jnp.sum(exps, axis=1, keepdims=True))).astype(bf16)
    prob_ref[...] = probs
    out_ref[...] = head_merge(dot_wide(probs, value_ref[...]), row_count).astype(bf16)


def attend(query, key, value, bias, scale):
    micro_count, row_count, width = query.shape
    columns = key.shape[1]
    groups = width // LANES
    stack = (LANES // HEAD_PAD) * row_count
    own = pl.BlockSpec((None, row_count, LANES), lambda m, g: (m, 0, g))
    whole = pl.BlockSpec((None, columns, LANES), lambda m, g: (m, 0, g))
    return pl.pallas_call(
        functools.partial(attend_kernel, scale),
        grid=(micro_count, groups),
        in_specs=[
            own,
            whole,
            whole,
            pl.BlockSpec((None, columns // LANES, stack, LANES), lambda m, g: (m, 0, g, 0)),
        ],
        out_specs=[pl.BlockSpec((None, stack, columns), lambda m, g: (m, g, 0)), own],
        out_shape=[
            jax.ShapeDtypeStruct((micro_count, groups * stack, columns), bf16),
            jax.ShapeDtypeStruct((micro_count, row_count, width), bf16),
        ],
        compiler_params=pltpu.CompilerParams(vmem_limit_bytes=VMEM_LIMIT),
        name="attend",
    )(query, key, value, bias)


def attend_back_kernel(
    scale,
    query_ref,
    key_ref,
    value_ref,
    cot_ref,
    prob_ref,
    score_ref,
    query_cot_ref,
    key_cot_ref,
    value_cot_ref,
):
    row_count = query_ref.shape[0]
    tiles = score_ref.shape[0]
    cot_stack = head_stack(cot_ref[...])
    query_stack = head_stack(query_ref[...])
    low_probs = prob_ref[...]
    probs = low_probs.astype(f32)
    prob_cot = dot_nt(cot_stack, value_ref[...])
    weighted = probs * prob_cot
    score_cot = weighted - probs * jnp.sum(weighted, axis=1, keepdims=True)
    for tile in range(tiles):
        score_ref[tile] = score_cot[:, tile * LANES : (tile + 1) * LANES]
    low = score_cot.astype(bf16)
    query_cot_ref[...] = (head_merge(dot_wide(low, key_ref[...]), row_count) * scale).astype(bf16)
    key_cot_ref[...] = (dot_tn(low, query_stack) * scale).astype(bf16)
    value_cot_ref[...] = dot_tn(low_probs, cot_stack).astype(bf16)


def attend_back(query, key, value, cot, probs, scale):
    micro_count, row_count, width = query.shape
    columns = key.shape[1]
    groups = width // LANES
    stack = (LANES // HEAD_PAD) * row_count
    own = pl.BlockSpec((None, row_count, LANES), lambda m, g: (m, 0, g))
    whole = pl.BlockSpec((None, columns, LANES), lambda m, g: (m, 0, g))
    return pl.pallas_call(
        functools.partial(attend_back_kernel, scale),
        grid=(micro_count, groups),
        in_specs=[
            own,
            whole,
            whole,
            own,
            pl.BlockSpec((None, stack, columns), lambda m, g: (m, g, 0)),
        ],
        out_specs=[
            pl.BlockSpec((None, columns // LANES, stack, LANES), lambda m, g: (m, 0, g, 0)),
            own,
            whole,
            whole,
        ],
        out_shape=[
            jax.ShapeDtypeStruct((micro_count, columns // LANES, groups * stack, LANES), f32),
            jax.ShapeDtypeStruct((micro_count, row_count, width), bf16),
            jax.ShapeDtypeStruct((micro_count, columns, width), bf16),
            jax.ShapeDtypeStruct((micro_count, columns, width), bf16),
        ],
        compiler_params=pltpu.CompilerParams(vmem_limit_bytes=VMEM_LIMIT),
        name="attend_back",
    )(query, key, value, cot, probs)


def place_matrix(source, piece, padded):
    index = jnp.arange(source, dtype=jnp.int32)
    target = (index // piece) * padded + index % piece
    spots = jnp.arange(source // piece * padded, dtype=jnp.int32)
    return (target[:, None] == spots[None, :]).astype(bf16)


def dot_low(left, right):
    return jnp.dot(left, right, preferred_element_type=f32).astype(bf16)


def roll_rows(value, shift, axis):
    size = value.shape[axis]
    twice = jnp.concatenate([value, value], axis=axis)
    return lax.dynamic_slice_in_dim(twice, shift, size, axis)


def gather_shards(shard):
    return lax.all_gather(shard, "fsdp", axis=0, tiled=True)


def reduce_shards(grad):
    part = lax.psum_scatter(grad, "fsdp", scatter_dimension=0, tiled=True)
    return lax.psum(part, "seq").astype(f32)[0]


def body(
    hidden_in,
    row_types,
    lengths,
    noise_time,
    coords,
    residue_table,
    atom_table,
    time_weight,
    first_gain,
    query_weight,
    key_weight,
    value_weight,
    output_weight,
    kernel_mean,
    kernel_width,
    pair_weight,
    second_gain,
    up_weight,
    down_weight,
    force_weight,
    layer_cot,
    force_cot,
):
    seq_count = lax.axis_size("seq")
    fsdp_count = lax.axis_size("fsdp")
    seq_index = lax.axis_index("seq")
    micro_count, tok_rows, model_width = hidden_in.shape
    group_rows = tok_rows * seq_count
    own_kernels, head_count = pair_weight.shape
    kernels = own_kernels * fsdp_count
    head_dim = model_width // head_count
    inv_root = head_dim ** (-0.5)
    wide_heads = head_count * HEAD_PAD
    total_rows = micro_count * tok_rows
    residues, own_width = residue_table.shape
    types = residues + atom_table.shape[0]
    offset = seq_index * tok_rows

    small_rows = types + 16
    small = jnp.concatenate(
        [
            residue_table,
            atom_table,
            force_weight,
            first_gain[None],
            second_gain[None],
            jnp.zeros((small_rows - types - 5, own_width), bf16),
        ],
        axis=0,
    )
    small = jnp.pad(small, ((0, 0), (0, LANES - own_width)))
    kernel_rows = jnp.concatenate([pair_weight, kernel_mean[:, None], kernel_width[:, None]], axis=1)
    kernel_rows = jnp.pad(kernel_rows, ((0, 0), (0, LANES - head_count - 2)))
    small_all = lax.all_gather(jnp.concatenate([small, kernel_rows], axis=0), "fsdp", axis=0)
    kernel_all = small_all[:, small_rows:].reshape(kernels, LANES)
    pair_full = kernel_all[:, :head_count].astype(f32)
    mean_full = kernel_all[:, head_count].astype(f32)
    width_full = kernel_all[:, head_count + 1].astype(f32)
    spread = place_matrix(model_width, own_width, LANES)
    tables = dot_low(
        small_all[:, :small_rows].transpose(1, 0, 2).reshape(small_rows, fsdp_count * LANES),
        spread.T,
    )
    type_table = tables[:types]
    force_wide = tables[types : types + 3].astype(f32)
    gain_one = tables[types + 3].astype(f32)
    gain_two = tables[types + 4].astype(f32)

    time_full = gather_shards(time_weight)
    query_full = gather_shards(query_weight)
    key_full = gather_shards(key_weight)
    value_full = gather_shards(value_weight)
    output_full = gather_shards(output_weight)
    up_full = gather_shards(up_weight)
    down_full = gather_shards(down_weight)

    doc_lengths = lengths[:, 0]
    bounds = jnp.cumsum(doc_lengths, axis=1)
    first_len = doc_lengths[:, 0]
    all_rows = jnp.arange(group_rows, dtype=jnp.int32)
    key_doc = jnp.sum((all_rows[None, :, None] >= bounds[:, None, :]).astype(jnp.int32), axis=2)
    query_doc = lax.dynamic_slice_in_dim(key_doc, offset, tok_rows, 1)
    query_pos = lax.dynamic_slice_in_dim(coords, offset, tok_rows, 2)
    roll_index = (all_rows[None, :] + first_len[:, None]) % group_rows
    rolled_doc = jnp.sum(
        (roll_index[:, :, None] >= bounds[:, None, :]).astype(jnp.int32), axis=2
    )
    rolled_pos = jnp.stack([roll_rows(coords[m], first_len[m], 1) for m in range(micro_count)])
    same_doc = query_doc[:, :, None] == rolled_doc[:, None, :]
    mask = jnp.where(same_doc, 0.0, -1e30).astype(f32)
    delta = query_pos[:, :, :, None] - rolled_pos[:, :, None, :]
    dist = jnp.sqrt(jnp.sum(delta * delta, axis=1))
    long_row = (query_doc == 1).reshape(micro_count, tok_rows // TILE_ROWS, TILE_ROWS)
    flags = jnp.where(
        jnp.all(long_row, axis=2), 0, jnp.where(jnp.any(long_row, axis=2), 2, 1)
    ).astype(jnp.int32)

    scale_k = 1.0 / (math.sqrt(2.0 * math.pi) * width_full)
    coef = (-0.5 * LOG2E) / (width_full * width_full)
    mean_wide = jnp.broadcast_to(mean_full[:, None], (kernels, LANES))
    coef_wide = jnp.broadcast_to(coef[:, None], (kernels, LANES))
    bias_weight = (pair_full * (scale_k * LOG2E)[:, None]).T.astype(bf16)
    bias = pair_bias(flags, dist, mask, mean_wide, coef_wide, bias_weight)

    doc_hot = (
        query_doc[:, :, None] == jnp.arange(doc_lengths.shape[1], dtype=jnp.int32)
    ).astype(f32)
    type_hot = (
        row_types.reshape(total_rows)[:, None] == jnp.arange(types, dtype=jnp.int32)
    ).astype(bf16)
    time_low = sinus_embed(noise_time[:, 0], model_width).astype(bf16)
    time_proj = dot_wide(time_low.reshape(-1, model_width), time_full).reshape(
        micro_count, -1, model_width
    )
    start_state = (
        hidden_in.astype(f32)
        + dot_wide(type_hot, type_table).reshape(hidden_in.shape)
        + jnp.einsum("min,mnd->mid", doc_hot, time_proj, precision=EXACT)
    ).reshape(total_rows, model_width)
    normed_in, normed_one, inv_one = norm_forward(start_state, gain_one)
    attn_in = normed_in.astype(bf16)

    head_place = place_matrix(model_width, head_dim, HEAD_PAD)
    query_pad = dot_low(query_full, head_place)
    key_pad = dot_low(key_full, head_place)
    value_pad = dot_low(value_full, head_place)
    output_pad = dot_low(head_place.T, output_full)
    attn_all = lax.all_gather(
        attn_in.reshape(micro_count, tok_rows, model_width), "seq", axis=1, tiled=True
    )
    attn_all = jnp.concatenate(
        [roll_rows(attn_all[m], first_len[m], 0) for m in range(micro_count)], axis=0
    )
    queries = dot_low(attn_in, query_pad).reshape(micro_count, tok_rows, wide_heads)
    keys = dot_low(attn_all, key_pad).reshape(micro_count, group_rows, wide_heads)
    values = dot_low(attn_all, value_pad).reshape(micro_count, group_rows, wide_heads)
    probs, attended = attend(queries, keys, values, bias, inv_root * LOG2E)
    attended = attended.reshape(total_rows, wide_heads)

    mid_state = start_state + dot_wide(attended, output_pad)
    normed_mid, normed_two, inv_two = norm_forward(mid_state, gain_two)
    ffn_in = normed_mid.astype(bf16)
    up_state = dot_wide(ffn_in, up_full)
    gelu_low = jax.nn.gelu(up_state, approximate=True).astype(bf16)
    layer_out = (mid_state + dot_wide(gelu_low, down_full)).astype(bf16)
    forces = dot_nt(force_wide.astype(bf16), layer_out)
    forces = forces.reshape(3, micro_count, tok_rows).transpose(1, 0, 2)

    forces_cot = force_cot.transpose(1, 0, 2).reshape(3, total_rows)
    out_grad = layer_cot.reshape(total_rows, model_width).astype(f32)
    for axis in range(3):
        out_grad = out_grad + forces_cot[axis][:, None] * force_wide[axis][None, :]
    force_w_grad = jnp.dot(forces_cot, layer_out.astype(f32), precision=EXACT)
    branch_low = out_grad.astype(bf16)
    down_w_grad = dot_tn(gelu_low, branch_low)
    gelu_grad = dot_nt(branch_low, down_full)
    _, gelu_pull = jax.vjp(lambda inner: jax.nn.gelu(inner, approximate=True), up_state)
    up_low = gelu_pull(gelu_grad)[0].astype(bf16)
    up_w_grad = dot_tn(ffn_in, up_low)
    ffn_in_grad = dot_nt(up_low, up_full)
    norm_part, gain_two_grad = norm_backward(ffn_in_grad, normed_two, inv_two, gain_two)
    mid_grad = out_grad + norm_part
    attn_low = mid_grad.astype(bf16)
    output_w_grad = dot_low(head_place, dot_tn(attended, attn_low).astype(bf16))
    attended_grad = dot_nt(attn_low, output_pad).astype(bf16)

    score_cot, query_low, key_part, value_part = attend_back(
        queries,
        keys,
        values,
        attended_grad.reshape(micro_count, tok_rows, wide_heads),
        probs,
        inv_root,
    )
    query_low = query_low.reshape(total_rows, wide_heads)
    key_part = key_part.reshape(-1, wide_heads)
    value_part = value_part.reshape(-1, wide_heads)
    all_part = (dot_nt(key_part, key_pad) + dot_nt(value_part, value_pad)).astype(bf16)
    all_part = all_part.reshape(micro_count, group_rows, model_width)
    all_part = jnp.stack(
        [roll_rows(all_part[m], group_rows - first_len[m], 0) for m in range(micro_count)]
    )
    own_part = lax.psum_scatter(all_part, "seq", scatter_dimension=1, tiled=True)
    query_w_grad = dot_low(dot_tn(attn_in, query_low).astype(bf16), head_place.T)
    key_w_grad = dot_low(dot_tn(attn_all, key_part).astype(bf16), head_place.T)
    value_w_grad = dot_low(dot_tn(attn_all, value_part).astype(bf16), head_place.T)
    attn_in_grad = dot_nt(query_low, query_pad) + own_part.reshape(
        total_rows, model_width
    ).astype(f32)
    norm_part_one, gain_one_grad = norm_backward(attn_in_grad, normed_one, inv_one, gain_one)
    input_grad = mid_grad + norm_part_one

    input_low = input_grad.astype(bf16)
    type_grad = dot_tn(type_hot, input_low)
    time_cot = jnp.einsum(
        "min,mid->mnd",
        doc_hot.astype(bf16),
        input_low.reshape(micro_count, tok_rows, model_width),
        preferred_element_type=f32,
    ).astype(bf16)
    time_w_grad = dot_tn(
        time_low.reshape(-1, model_width), time_cot.reshape(-1, model_width)
    ).astype(bf16)

    sums = jnp.sum(pair_grads(flags, dist, score_cot, mean_wide, coef_wide), axis=0)
    plain, once, twice = (sums[:, k * kernels : (k + 1) * kernels].T for k in range(3))
    pair_w_grad = plain * scale_k[:, None]
    inv_width = 1.0 / width_full
    mean_grad = jnp.sum(pair_full * once, axis=1) * scale_k * inv_width * inv_width
    width_grad = (
        jnp.sum(pair_full * (twice * (inv_width * inv_width)[:, None] - plain), axis=1)
        * scale_k
        * inv_width
    )

    def by_shard(grad):
        return grad.reshape(fsdp_count, -1, grad.shape[-1]).astype(bf16)

    small_grad = jnp.concatenate(
        [
            type_grad,
            force_w_grad,
            gain_one_grad[None],
            gain_two_grad[None],
            jnp.zeros((small_rows - types - 5, model_width), f32),
        ],
        axis=0,
    )
    small_grad = dot_low(small_grad.astype(bf16), spread)
    small_grad = small_grad.reshape(small_rows, fsdp_count, LANES).transpose(1, 0, 2)
    kernel_grad = jnp.concatenate(
        [pair_w_grad, mean_grad[:, None], width_grad[:, None]], axis=1
    ).astype(bf16)
    kernel_grad = jnp.pad(kernel_grad, ((0, 0), (0, LANES - head_count - 2)))
    small_grad = jnp.concatenate(
        [small_grad, kernel_grad.reshape(fsdp_count, own_kernels, LANES)], axis=1
    )
    down_sum = reduce_shards(by_shard(down_w_grad))
    up_sum = reduce_shards(by_shard(up_w_grad))
    output_sum = reduce_shards(by_shard(output_w_grad))
    query_sum = reduce_shards(by_shard(query_w_grad))
    key_sum = reduce_shards(by_shard(key_w_grad))
    value_sum = reduce_shards(by_shard(value_w_grad))
    time_sum = reduce_shards(by_shard(time_w_grad))
    small_sum = reduce_shards(small_grad)
    kernel_sum = small_sum[small_rows:]
    row_sum = small_sum[:small_rows, :own_width]
    return (
        layer_out.reshape(hidden_in.shape),
        forces,
        input_grad.reshape(hidden_in.shape),
        row_sum[:residues],
        row_sum[residues:types],
        time_sum,
        row_sum[types + 3],
        query_sum,
        key_sum,
        value_sum,
        output_sum,
        kernel_sum[:, head_count],
        kernel_sum[:, head_count + 1],
        kernel_sum[:, :head_count],
        row_sum[types + 4],
        up_sum,
        down_sum,
        row_sum[types : types + 3],
    )


def solution(mesh):
    rows = ("fsdp", "seq")
    return jax.shard_map(
        body,
        mesh=mesh,
        in_specs=(
            P(None, rows, None),
            P(None, rows),
            P(None, "fsdp", None),
            P(None, "fsdp", None),
            P(None, None, "fsdp"),
            P(None, "fsdp"),
            P(None, "fsdp"),
            P("fsdp", None),
            P("fsdp"),
            P("fsdp", None),
            P("fsdp", None),
            P("fsdp", None),
            P("fsdp", None),
            P("fsdp"),
            P("fsdp"),
            P("fsdp", None),
            P("fsdp"),
            P("fsdp", None),
            P("fsdp", None),
            P(None, "fsdp"),
            P(None, rows, None),
            P(None, None, rows),
        ),
        out_specs=(
            P(None, rows, None),
            P(None, None, rows),
            P(None, rows, None),
            P(None, "fsdp"),
            P(None, "fsdp"),
            P("fsdp", None),
            P("fsdp"),
            P("fsdp", None),
            P("fsdp", None),
            P("fsdp", None),
            P("fsdp", None),
            P("fsdp"),
            P("fsdp"),
            P("fsdp", None),
            P("fsdp"),
            P("fsdp", None),
            P("fsdp", None),
            P(None, "fsdp"),
        ),
        check_vma=False,
    )
```

time: 1700 us -> 1180 us (0.69)
  matrix products: 394 us -> 117 us
  blocking collectives: 235 us -> 45 us
  local copies, waits for them, and re-layouts: 195 us -> 22.4 us
  Pallas kernels: 0 us -> 139 us
  other arithmetic: 63.4 us -> 38.3 us
  waiting for transfers between devices: 768 us -> 786 us
    dot_general x141 -> x31, matrix products: 394 us -> 117 us  [the longest x13 56.2 us: dot_low(): return jnp.dot(left, right, preferred_element_type=f32).astype(bf16)]
    all_gather x7 -> x8, waiting for transfers between devices: 0.09 us -> 226 us  [the longest x7 205 us: gather_shards(): return lax.all_gather(shard, 'fsdp', axis=0, tiled=True)]
    unnamed x34 -> x18, waiting for transfers between devices: 217 us -> 4.69 us
    pallas_call x0 -> x4, Pallas kernels: none -> 139 us  [the longest x1 41.1 us: pair_grads(): pl.pallas_call(pair_grad_kernel, grid=(micro_count,), in_specs=[pl.BlockS...]
    all_gather x10 -> x1, blocking collectives: 167 us -> 33.4 us  [body(): lax.all_gather(jnp.concatenate([small, kernel_rows], axis=0), 'fsdp', axi...]
    unnamed x2 -> x0, blocking collectives: 57.5 us -> none
    dynamic_slice x65 -> x1, local copies, waits for them, and re-layouts: 46.6 us -> 0.01 us  [body(): query_pos = lax.dynamic_slice_in_dim(coords, offset, tok_rows, 2)]
    unnamed x506 -> x147, local copies, waits for them, and re-layouts: 45.8 us -> 6.41 us
  transfers between devices with their start and end apart: 25 -> 18, of which waited for: 13 -> 16; matrix products, arithmetic and copies ran while one was open for 31% -> 12% of each run, Pallas kernels for 0% -> 9%
where the time goes in v1:
time: 1180 us; the launch traced here: 1170 us
  waiting for transfers between devices  786 us (67%)
  Pallas kernels  139 us (12%)
  matrix products  117 us (10%)
  blocking collectives  45 us (4%)
  other arithmetic  38.3 us (3%)
  between operations  25.4 us (2%)
  local copies, waits for them, and re-layouts  22.4 us (2%)
    reduce_scatter x8, waiting for transfers between devices, reduce_shards(): part = lax.psum_scatter(grad, 'fsdp', scatter_dimension=0, tiled=True)  513 us
    all_gather x7, waiting for transfers between devices, gather_shards(): return lax.all_gather(shard, 'fsdp', axis=0, tiled=True)  205 us
    dot_general x13, matrix products, dot_low(): return jnp.dot(left, right, preferred_element_type=f32).astype(bf16)  56.2 us
    pallas_call x1, Pallas kernels, pair_grads(): pl.pallas_call(pair_grad_kernel, grid=(micro_count,), in_specs=[pl.BlockS...  41.1 us
    psum x1, waiting for transfers between devices, reduce_shards(): return lax.psum(part, 'seq').astype(f32)[0]  37.1 us
    pallas_call x1, Pallas kernels, attend_back(): pl.pallas_call(functools.partial(attend_back_kernel, scale), grid=(micro_...  35.3 us
    all_gather x1, blocking collectives, body(): lax.all_gather(jnp.concatenate([small, kernel_rows], axis=0), 'fsdp', axi...  33.4 us
    pallas_call x1, Pallas kernels, pair_bias(): pl.pallas_call(bias_kernel, grid=(micro_count,), in_specs=[pl.BlockSpec(m...  32 us
  transfers between devices with their start and end apart: 18, of which 16 were waited for; matrix products, arithmetic and copies ran while one was open for 12% of the time, Pallas kernels for 9%

profile of v1, /device:TPU:0, one launch (start us, length us, event | category | flops | bytes accessed | tf_op | source)
XLA Modules:
  0.0 1173.5 jit_solution(12520789726809224686)
XLA Ops:
  17.1 33.4 %all-gather = bf16[1536,128]{1,0:T(8,128)(2,1)S(1)} all-gather(bf16[192,128]{1,0:T(8,128)(2,1)S(1)} %fusion.85), channel_id=2, replica_groups=mesh['fsdp'=8,'seq'=4] {'fsdp'}, dimensions={0}, use_global_device_ids=true | all-gather | bytes 442368 | tf_op jit(solution)/shard_map/all_gather | solution.py:429
  77.4 32.0 %pair_bias.1.bias_ref = f32[3,4,4096,128]{3,2,1,0:T(8,128)} custom-call(s32[3,16]{1,0:T(4,128)} %select_select_fusion.flag_ref, f32[3,128,512]{2,1,0:T(8,128)} %sqrt.3.dist_ref, f32[3,128,512]{2,1,0:T(8,128)} %compare_select_fusion.mask_ref, f32[128,128]{1,0:T(8,128)} %broadcast_in_dim.111.mean_ref, f32[128,128]{1,0:T(8,128)} %broadcast_in_dim.113.coef_ref, ...), custom_call_target="tpu_custom_call" | custom-call | tf_op jit(solution)/shard_map/pair_bias/pallas_call | solution.py:141
  117.4 22.3 %all-gather.20.cloned.1.call-done = bf16[768,768]{1,0:T(8,128)(2,1)} async-done(((bf16[96,768]{1,0:T(8,128)(2,1)}), bf16[768,768]{1,0:T(8,128)(2,1)}) %all-gather.20.cloned.1.call-update) | async-done | bytes 1179664 | tf_op jit(solution)/shard_map/all_gather | solution.py:367
  143.8 37.7 %all-gather.18.cloned.1.call-done = bf16[768,768]{1,0:T(8,128)(2,1)} async-done(((bf16[96,768]{1,0:T(8,128)(2,1)}), bf16[768,768]{1,0:T(8,128)(2,1)}) %all-gather.18.cloned.1.call-update) | async-done | bytes 1179664 | tf_op jit(solution)/shard_map/all_gather | solution.py:367
  185.6 37.8 %all-gather.16.cloned.1.call-done = bf16[768,768]{1,0:T(8,128)(2,1)} async-done(((bf16[96,768]{1,0:T(8,128)(2,1)}), bf16[768,768]{1,0:T(8,128)(2,1)}) %all-gather.16.cloned.1.call-update) | async-done | bytes 1179664 | tf_op jit(solution)/shard_map/all_gather | solution.py:367
  227.5 20.8 %all-gather.14.cloned.1.call-done = bf16[3,512,768]{2,1,0:T(8,128)(2,1)} async-done(((bf16[3,128,768]{2,1,0:T(8,128)(2,1)}), bf16[3,512,768]{2,1,0:T(8,128)(2,1)}) %all-gather.14.cloned.1.call-update) | async-done | bytes 2359312 | tf_op jit(solution)/shard_map/all_gather | solution.py:503
  266.1 30.1 %attend.1 = (bf16[3,4096,512]{2,1,0:T(8,128)(2,1)}, bf16[3,128,1024]{2,1,0:T(8,128)(2,1)}) custom-call(bf16[3,128,1024]{2,1,0:T(8,128)(2,1)} %bitcast.230, bf16[3,512,1024]{2,1,0:T(8,128)(2,1)} %bitcast.226, bf16[3,512,1024]{2,1,0:T(8,128)(2,1)} %bitcast.224, f32[3,4,4096,128]{3,2,1,0:T(8,128)} %pair_bias.1.bias_ref), custom_call_target="tpu_custom_call" | custom-call | tf_op jit(solution)/shard_map/attend/pallas_call | solution.py:267
  299.7 30.7 %all-gather.24.cloned.1.call-done = bf16[3072,768]{1,0:T(8,128)(2,1)} async-done(((bf16[384,768]{1,0:T(8,128)(2,1)}), bf16[3072,768]{1,0:T(8,128)(2,1)}) %all-gather.24.cloned.1.call-update) | async-done | bytes 4718608 | tf_op jit(solution)/shard_map/all_gather | solution.py:367
  336.9 73.8 %all-gather.22.cloned.1.call-done = bf16[768,3072]{1,0:T(8,128)(2,1)} async-done(((bf16[96,3072]{1,0:T(8,128)(2,1)}), bf16[768,3072]{1,0:T(8,128)(2,1)}) %all-gather.22.cloned.1.call-update) | async-done | bytes 4718608 | tf_op jit(solution)/shard_map/all_gather | solution.py:367
  410.7 10.2 fusion.6
  427.0 35.3 %attend_back.1 = (f32[3,4,4096,128]{3,2,1,0:T(8,128)}, bf16[3,128,1024]{2,1,0:T(8,128)(2,1)}, bf16[3,512,1024]{2,1,0:T(8,128)(2,1)}, bf16[3,512,1024]{2,1,0:T(8,128)(2,1)}) custom-call(bf16[3,128,1024]{2,1,0:T(8,128)(2,1)} %bitcast.231, bf16[3,512,1024]{2,1,0:T(8,128)(2,1)} %bitcast.227, bf16[3,512,1024]{2,1,0:T(8,128)(2,1)} %bitcast.225, ...), custom_call_target="tpu_custom_call" | custom-call | tf_op jit(solution)/shard_map/attend_back/pallas_call | solution.py:322
  485.8 7.8 fusion.51
  493.7 7.8 fusion.53
  538.3 41.1 %pair_grads.1 = f32[3,32,384]{2,1,0:T(8,128)} custom-call(s32[3,16]{1,0:T(4,128)} %select_select_fusion.flag_ref, f32[3,128,512]{2,1,0:T(8,128)} %sqrt.3.dist_ref, f32[3,4,4096,128]{3,2,1,0:T(8,128)} %get-tuple-element.29.score_ref, f32[128,128]{1,0:T(8,128)} %broadcast_in_dim.111.mean_ref, f32[128,128]{1,0:T(8,128)} %broadcast_in_dim.113.coef_ref), custom_call_target="tpu_custom_call" | custom-call | tf_op jit(solution)/shard_map/pair_grads/pallas_call | solution.py:211
  580.6 6.6 fusion.55
  590.2 51.9 %reduce-scatter.16.cloned.1.call-done = bf16[1,96,768]{2,1,0:T(8,128)(2,1)} async-done(((bf16[8,96,768]{2,1,0:T(8,128)(2,1)}), bf16[1,96,768]{2,1,0:T(8,128)(2,1)}) %reduce-scatter.16.cloned.1.call-update) | async-done | bytes 147472 | tf_op jit(solution)/shard_map/reduce_scatter | solution.py:371
  642.1 66.7 %reduce-scatter.20.cloned.1.call-done = bf16[1,96,768]{2,1,0:T(8,128)(2,1)} async-done(((bf16[8,96,768]{2,1,0:T(8,128)(2,1)}), bf16[1,96,768]{2,1,0:T(8,128)(2,1)}) %reduce-scatter.20.cloned.1.call-update) | async-done | bytes 147472 | tf_op jit(solution)/shard_map/reduce_scatter | solution.py:371
  708.8 66.9 %reduce-scatter.18.cloned.1.call-done = bf16[1,96,768]{2,1,0:T(8,128)(2,1)} async-done(((bf16[8,96,768]{2,1,0:T(8,128)(2,1)}), bf16[1,96,768]{2,1,0:T(8,128)(2,1)}) %reduce-scatter.18.cloned.1.call-update) | async-done | bytes 147472 | tf_op jit(solution)/shard_map/reduce_scatter | solution.py:371
  775.7 67.3 %reduce-scatter.14.cloned.1.call-done = bf16[1,96,768]{2,1,0:T(8,128)(2,1)} async-done(((bf16[8,96,768]{2,1,0:T(8,128)(2,1)}), bf16[1,96,768]{2,1,0:T(8,128)(2,1)}) %reduce-scatter.14.cloned.1.call-update) | async-done | bytes 147472 | tf_op jit(solution)/shard_map/reduce_scatter | solution.py:371
  843.0 98.3 %reduce-scatter.24.cloned.1.call-done = bf16[1,96,3072]{2,1,0:T(8,128)(2,1)} async-done(((bf16[8,96,3072]{2,1,0:T(8,128)(2,1)}), bf16[1,96,3072]{2,1,0:T(8,128)(2,1)}) %reduce-scatter.24.cloned.1.call-update) | async-done | bytes 589840 | tf_op jit(solution)/shard_map/reduce_scatter | solution.py:371
  941.3 99.1 %reduce-scatter.26.cloned.1.call-done = bf16[1,384,768]{2,1,0:T(8,128)(2,1)} async-done(((bf16[8,384,768]{2,1,0:T(8,128)(2,1)}), bf16[1,384,768]{2,1,0:T(8,128)(2,1)}) %reduce-scatter.26.cloned.1.call-update) | async-done | bytes 589840 | tf_op jit(solution)/shard_map/reduce_scatter | solution.py:371
  1042.0 63.0 %reduce-scatter.12.cloned.1.call-done = bf16[1,192,128]{2,1,0:T(8,128)(2,1)} async-done(((bf16[8,192,128]{2,1,0:T(8,128)(2,1)}), bf16[1,192,128]{2,1,0:T(8,128)(2,1)}) %reduce-scatter.12.cloned.1.call-update) | async-done | bytes 49168 | tf_op jit(solution)/shard_map/reduce_scatter | solution.py:371
  1105.0 11.6 psum.56
  1119.7 37.1 %all-reduce.6.cloned.1.call-done = (bf16[96,768]{1,0:T(8,128)(2,1)}, bf16[96,768]{1,0:T(8,128)(2,1)}, bf16[96,768]{1,0:T(8,128)(2,1)}, bf16[96,768]{1,0:T(8,128)...) async-done(((bf16[96,768]{1,0:T(8,128)(2,1)}, bf16[96,768]{1,0:T(8,128)(2,1)}, bf16[96,768]{1,0:T(8,128)(2,1)}, ...) | async-done | bytes 1916944 | tf_op jit(solution)/shard_map/psum | solution.py:372
  (305 shorter events, 158.9 us)
Async XLA Ops:
  7.2 48.1 %all-gather.10.cloned.1.call-start = ((), (), s32[]{:S(2)}) async-start(), calls=%async_computation.9 | async-start | bytes 1327104 | tf_op jit(solution)/shard_map/all_gather | solution.py:367
  7.9 103.7 %all-gather.12.cloned.1.call-start = ((), (), s32[]{:S(2)}) async-start(), calls=%async_computation.10 | async-start | bytes 1327104 | tf_op jit(solution)/shard_map/all_gather | solution.py:367
  8.7 131.0 %all-gather.20.cloned.1.call-start = ((), (), s32[]{:S(2)}) async-start(), calls=%async_computation.14 | async-start | bytes 1327104 | tf_op jit(solution)/shard_map/all_gather | solution.py:367
  9.4 172.1 %all-gather.18.cloned.1.call-start = ((), (), s32[]{:S(2)}) async-start(), calls=%async_computation.13 | async-start | bytes 1327104 | tf_op jit(solution)/shard_map/all_gather | solution.py:367
  10.0 213.5 %all-gather.16.cloned.1.call-start = ((), (), s32[]{:S(2)}) async-start(), calls=%async_computation.12 | async-start | bytes 1327104 | tf_op jit(solution)/shard_map/all_gather | solution.py:367
  10.6 237.7 %all-gather.14.cloned.1.call-start = ((), (), s32[]{:S(2)}) async-start(), calls=%async_computation.11 | async-start | bytes 2949120 | tf_op jit(solution)/shard_map/all_gather | solution.py:503
  57.7 53.7 %copy-start.27 = (f32[384]{0:T(512)}, f32[384]{0:T(512)S(1)}, u32[]{:S(2)}) copy-start(f32[384]{0:T(512)S(1)} %get-tuple-element.162) | copy-start | bytes 4612
  58.0 53.4 %copy-start.30 = (f32[384]{0:T(512)}, f32[384]{0:T(512)S(1)}, u32[]{:S(2)}) copy-start(f32[384]{0:T(512)S(1)} %get-tuple-element.161) | copy-start | bytes 4612
  59.0 271.4 %all-gather.24.cloned.1.call-start = ((), (), s32[]{:S(2)}) async-start(), calls=%async_computation.16 | async-start | bytes 5308416 | tf_op jit(solution)/shard_map/all_gather | solution.py:367
  59.8 350.9 %all-gather.22.cloned.1.call-start = ((), (), s32[]{:S(2)}) async-start(), calls=%async_computation.15 | async-start | bytes 5308416 | tf_op jit(solution)/shard_map/all_gather | solution.py:367
  60.6 446.2 %reduce-scatter.10.cloned.1.call-start = ((), (), s32[]{:S(2)}) async-start(), calls=%async_computation.17 | async-start | bytes 2949120 | tf_op jit(solution)/shard_map/reduce_scatter | solution.py:558
  109.4 114.0 %copy-start.55 = (s32[768]{0:T(1024)}, s32[768]{0:T(1024)S(1)}, u32[]{:S(2)}) copy-start(s32[768]{0:T(1024)S(1)} %fusion.121) | copy-start | bytes 9220
  475.4 114.8 %reduce-scatter.22.cloned.1.call-start = ((), (), s32[]{:S(2)}) async-start(), calls=%async_computation.23 | async-start | bytes 1327104 | tf_op jit(solution)/shard_map/reduce_scatter | solution.py:371
  480.9 161.2 %reduce-scatter.16.cloned.1.call-start = ((), (), s32[]{:S(2)}) async-start(), calls=%async_computation.20 | async-start | bytes 1327104 | tf_op jit(solution)/shard_map/reduce_scatter | solution.py:371
  485.8 223.0 %reduce-scatter.20.cloned.1.call-start = ((), (), s32[]{:S(2)}) async-start(), calls=%async_computation.22 | async-start | bytes 1327104 | tf_op jit(solution)/shard_map/reduce_scatter | solution.py:371
  493.7 282.0 %reduce-scatter.18.cloned.1.call-start = ((), (), s32[]{:S(2)}) async-start(), calls=%async_computation.21 | async-start | bytes 1327104 | tf_op jit(solution)/shard_map/reduce_scatter | solution.py:371
  501.6 341.4 %reduce-scatter.14.cloned.1.call-start = ((), (), s32[]{:S(2)}) async-start(), calls=%async_computation.19 | async-start | bytes 1327104 | tf_op jit(solution)/shard_map/reduce_scatter | solution.py:371
  514.2 427.0 %reduce-scatter.24.cloned.1.call-start = ((), (), s32[]{:S(2)}) async-start(), calls=%async_computation.24 | async-start | bytes 5308416 | tf_op jit(solution)/shard_map/reduce_scatter | solution.py:371
  520.7 519.7 %reduce-scatter.26.cloned.1.call-start = ((), (), s32[]{:S(2)}) async-start(), calls=%async_computation.25 | async-start | bytes 5308416 | tf_op jit(solution)/shard_map/reduce_scatter | solution.py:371
  537.6 567.4 %reduce-scatter.12.cloned.1.call-start = ((), (), s32[]{:S(2)}) async-start(), calls=%async_computation.18 | async-start | bytes 442368 | tf_op jit(solution)/shard_map/reduce_scatter | solution.py:371
  538.3 42.1 %copy-start.60 = (f32[128,1]{0,1:T(1,128)S(1)}, f32[128,1]{0,1:T(1,128)}, u32[]{:S(2)}) copy-start(f32[128,1]{0,1:T(1,128)} %get-tuple-element.134) | copy-start | bytes 1540
  587.3 453.2 %copy-start.4 = (bf16[384,768]{1,0:T(8,128)(2,1)}, bf16[384,768]{1,0:T(8,128)(2,1)S(1)}, u32[]{:S(2)}) copy-start(bf16[384,768]{1,0:T(8,128)(2,1)S(1)} %fusion.55) | copy-start | bytes 1769476
  590.1 566.7 %all-reduce.6.cloned.1.call-start = ((), (), s32[]{:S(2)}) async-start(), calls=%async_computation.26 | async-start | bytes 3833856 | tf_op jit(solution)/shard_map/psum | solution.py:372
  1118.5 46.9 %copy-start.15 = (f32[16,128]{1,0:T(8,128)}, f32[16,128]{1,0:T(8,128)S(1)}, u32[]{:S(2)}) copy-start(f32[16,128]{1,0:T(8,128)S(1)} %slice_bitcast_fusion.5) | copy-start | bytes 24580
  (63 other events, 558.2 us)
Sparse Core Ops, SparseCore 0:
  10.2 45.0 all-gather.9
  57.4 40.0 all-gather.11
  99.7 39.9 all-gather.19
  141.7 39.8 all-gather.17
  183.6 39.8 all-gather.15
  225.4 22.8 all-gather.13
  250.5 79.8 all-gather.23
  332.6 78.0 all-gather.21
  475.5 31.1 reduce-scatter.9
  510.4 64.1 reduce-scatter.21
  579.0 63.0 reduce-scatter.15
  645.7 63.0 reduce-scatter.19
  712.6 63.0 reduce-scatter.17
  779.9 63.0 reduce-scatter.13
  846.9 94.3 reduce-scatter.23
  945.2 95.1 reduce-scatter.25
  1043.9 61.0 reduce-scatter.11
  1108.0 48.7 all-reduce.5

commit v2 on v1

v2 whole, which is shorter than its diff:
```python
import functools
import math

import jax
import jax.numpy as jnp
from jax import lax
from jax.experimental import pallas as pl
from jax.experimental.pallas import tpu as pltpu
from jax.sharding import PartitionSpec as P

NORM_EPS = 1e-05
PROTEIN_ROWS = 384
LANES = 128
HEAD_PAD = 32
TILE_ROWS = 8
ROW_BLOCK = 32
CENTRE = 6.0
PER_STEP = 4
LOG2E = math.log2(math.e)
VMEM_LIMIT = 56 * 2**20
EXACT = lax.Precision.HIGHEST
bf16 = jnp.bfloat16
f32 = jnp.float32


def dot_wide(left, right):
    return jnp.dot(left, right, preferred_element_type=f32)


def dot_tn(left, right):
    return lax.dot_general(left, right, (((0,), (0,)), ((), ())), preferred_element_type=f32)


def dot_nt(left, right):
    return lax.dot_general(left, right, (((1,), (1,)), ((), ())), preferred_element_type=f32)


def cost(micros):
    return pl.CostEstimate(flops=int(micros * 0.04e9), bytes_accessed=0, transcendentals=0)


def sinus_columns(stamps, model_width, first, columns):
    half_width = model_width // 2
    index = first + jnp.arange(columns, dtype=jnp.int32)
    step = (index % half_width).astype(f32)
    frequency = jnp.exp(-math.log(10000.0) * step / half_width)
    angles = 1000.0 * stamps[..., None] * frequency
    return jnp.where(index < half_width, jnp.sin(angles), jnp.cos(angles)).astype(bf16)


def norm_forward(value, norm_gain):
    centre = value - jnp.mean(value, axis=-1, keepdims=True)
    inv_std = lax.rsqrt(jnp.mean(centre * centre, axis=-1, keepdims=True) + NORM_EPS)
    normed = centre * inv_std
    return normed * norm_gain, normed, inv_std


def norm_backward(grad_out, normed, inv_std, norm_gain):
    scaled = grad_out * norm_gain
    grad_in = inv_std * (
        scaled
        - jnp.mean(scaled, axis=-1, keepdims=True)
        - normed * jnp.mean(scaled * normed, axis=-1, keepdims=True)
    )
    return grad_in, jnp.sum(grad_out * normed, axis=0)


def density_rows(spans, mean_ref, coef_ref, base_ref):
    kernels = mean_ref.shape[0]
    tiles = spans[0].shape[1] // LANES
    parts = []
    for start in range(0, kernels, 16):
        mean = mean_ref[start : start + 16, :]
        coef = coef_ref[start : start + 16, :]
        pieces = []
        for span in spans:
            for tile in range(tiles):
                shift = span[:, tile * LANES : (tile + 1) * LANES] - mean
                power = shift * shift * coef
                if base_ref is not None:
                    power = power + base_ref[start : start + 16, :]
                pieces.append(jnp.exp2(power).astype(bf16))
        parts.append(jnp.concatenate(pieces, axis=1))
    return jnp.concatenate(parts, axis=0)


def bias_kernel(
    micro, flag_ref, dist_ref, mask_ref, mean_ref, coef_ref, base_ref, weight_ref, *rest
):
    out_ref = rest[-1]
    row_count, columns = dist_ref.shape
    heads = weight_ref.shape[0]
    long_tiles = PROTEIN_ROWS // LANES
    all_tiles = columns // LANES

    def fill(base, first, tiles):
        empty = jnp.full((TILE_ROWS, LANES), -1e30, f32)
        for tile in range(first, first + tiles):
            for head in range(heads):
                out_ref[tile, pl.ds(head * row_count + base, TILE_ROWS), :] = empty

    def compute(base, first, tiles, batch):
        span = slice(first * LANES, (first + tiles) * LANES)
        dist = dist_ref[pl.ds(base, TILE_ROWS), span]
        mask = mask_ref[pl.ds(base, TILE_ROWS), span]
        for start in range(0, TILE_ROWS, batch):
            rows = range(start, start + batch)
            dens = density_rows(
                [dist[row : row + 1] for row in rows], mean_ref, coef_ref, base_ref
            )
            bias = dot_wide(weight_ref[...], dens) * LOG2E
            for row in rows:
                for tile in range(tiles):
                    at = ((row - start) * tiles + tile) * LANES
                    out_ref[first + tile, pl.ds(base + row, heads, stride=row_count), :] = (
                        bias[:, at : at + LANES]
                        + mask[row : row + 1, tile * LANES : (tile + 1) * LANES]
                    )

    def one_tile(tile_index, carry):
        base = pl.multiple_of(tile_index * TILE_ROWS, TILE_ROWS)
        flag = flag_ref[micro, pl.program_id(0) * (row_count // TILE_ROWS) + tile_index]

        @pl.when(flag != 1)
        def _():
            compute(base, 0, long_tiles, 2)

        @pl.when(flag == 1)
        def _():
            fill(base, 0, long_tiles)

        @pl.when(flag != 0)
        def _():
            compute(base, long_tiles, all_tiles - long_tiles, TILE_ROWS)

        @pl.when(flag == 0)
        def _():
            fill(base, long_tiles, all_tiles - long_tiles)

        return carry

    lax.fori_loop(0, row_count // TILE_ROWS, one_tile, 0)


def pair_bias(micro, earlier, flags, dist, mask, mean_wide, coef_wide, base_wide, weight):
    micro_count, row_count, columns = dist.shape
    heads, kernels = weight.shape
    blocks = row_count // ROW_BLOCK
    block = pl.BlockSpec((None, ROW_BLOCK, columns), lambda i: (micro, i, 0))
    wide = pl.BlockSpec((kernels, LANES), lambda i: (0, 0))
    shape = (micro_count, blocks, columns // LANES, heads * ROW_BLOCK, LANES)
    operands = [flags, dist, mask, mean_wide, coef_wide, base_wide, weight]
    specs = [
        pl.BlockSpec(memory_space=pltpu.SMEM),
        block,
        block,
        wide,
        wide,
        wide,
        pl.BlockSpec((heads, kernels), lambda i: (0, 0)),
    ]
    if earlier is not None:
        operands.append(earlier)
        specs.append(pl.BlockSpec(memory_space=pl.ANY))
    return pl.pallas_call(
        functools.partial(bias_kernel, micro),
        grid=(blocks,),
        in_specs=specs,
        out_specs=pl.BlockSpec((None, None) + shape[2:], lambda i: (micro, i, 0, 0, 0)),
        out_shape=jax.ShapeDtypeStruct(shape, f32),
        input_output_aliases={} if earlier is None else {7: 0},
        compiler_params=pltpu.CompilerParams(vmem_limit_bytes=VMEM_LIMIT),
        cost_estimate=cost(11),
        name="pair_bias",
    )(*operands)


def two_parts(value):
    high = value.astype(bf16)
    return high, (value - high.astype(f32)).astype(bf16)


def pair_grad_kernel(micro, flag_ref, dist_ref, score_ref, mean_ref, coef_ref, out_ref):
    row_count, columns = dist_ref.shape
    heads = score_ref.shape[1] // row_count
    long_tiles = PROTEIN_ROWS // LANES
    all_tiles = columns // LANES

    @pl.when(pl.program_id(0) == 0)
    def _():
        out_ref[...] = jnp.zeros_like(out_ref)

    def compute(base, first, tiles, batch):
        total = out_ref[...]
        span = slice(first * LANES, (first + tiles) * LANES)
        dist = dist_ref[pl.ds(base, TILE_ROWS), span]
        for start in range(0, TILE_ROWS, batch):
            rows = range(start, start + batch)
            dens = density_rows([dist[row : row + 1] for row in rows], mean_ref, coef_ref, None)
            score = jnp.concatenate(
                [
                    score_ref[first + tile, pl.ds(base + row, heads, stride=row_count), :]
                    for row in rows
                    for tile in range(tiles)
                ],
                axis=1,
            ).astype(bf16)
            far = jnp.concatenate([dist[row : row + 1] for row in rows], axis=1) - CENTRE
            once = score.astype(f32) * far
            stack = jnp.concatenate([score, *two_parts(once), *two_parts(once * far)], axis=0)
            total = total + dot_nt(stack, dens)
        out_ref[...] = total

    def one_tile(tile_index, carry):
        base = pl.multiple_of(tile_index * TILE_ROWS, TILE_ROWS)
        flag = flag_ref[micro, pl.program_id(0) * (row_count // TILE_ROWS) + tile_index]

        @pl.when(flag != 1)
        def _():
            compute(base, 0, long_tiles, 2)

        @pl.when(flag != 0)
        def _():
            compute(base, long_tiles, all_tiles - long_tiles, TILE_ROWS)

        return carry

    lax.fori_loop(0, row_count // TILE_ROWS, one_tile, 0)


def pair_grads(micro, flags, dist, score_cot, mean_wide, coef_wide):
    columns = dist.shape[2]
    blocks = score_cot.shape[1]
    kernels = mean_wide.shape[0]
    heads = score_cot.shape[3] // ROW_BLOCK
    wide = pl.BlockSpec((kernels, LANES), lambda i: (0, 0))
    return pl.pallas_call(
        functools.partial(pair_grad_kernel, micro),
        grid=(blocks,),
        in_specs=[
            pl.BlockSpec(memory_space=pltpu.SMEM),
            pl.BlockSpec((None, ROW_BLOCK, columns), lambda i: (micro, i, 0)),
            pl.BlockSpec((None, None) + score_cot.shape[2:], lambda i: (micro, i, 0, 0, 0)),
            wide,
            wide,
        ],
        out_specs=pl.BlockSpec((5 * heads, kernels), lambda i: (0, 0)),
        out_shape=jax.ShapeDtypeStruct((5 * heads, kernels), f32),
        compiler_params=pltpu.CompilerParams(vmem_limit_bytes=VMEM_LIMIT),
        cost_estimate=cost(14),
        name="pair_grads",
    )(flags, dist, score_cot, mean_wide, coef_wide)


def head_stack(tile):
    lane_head = lax.broadcasted_iota(jnp.int32, (1, LANES), 1) // HEAD_PAD
    return jnp.concatenate(
        [
            jnp.where(lane_head == head, tile, jnp.zeros_like(tile))
            for head in range(LANES // HEAD_PAD)
        ],
        axis=0,
    )


def head_merge(stacked, row_count):
    lane_head = lax.broadcasted_iota(jnp.int32, (1, LANES), 1) // HEAD_PAD
    merged = stacked[:row_count]
    for head in range(1, LANES // HEAD_PAD):
        merged = jnp.where(
            lane_head == head, stacked[head * row_count : (head + 1) * row_count], merged
        )
    return merged


def attend_kernel(scale, query_ref, key_ref, value_ref, bias_ref, prob_ref, out_ref):
    row_count = query_ref.shape[0]
    blocks, tiles = bias_ref.shape[:2]
    heads = LANES // HEAD_PAD
    stack = heads * row_count
    for group in range(query_ref.shape[1] // LANES):
        lanes = slice(group * LANES, (group + 1) * LANES)
        rows = slice(group * stack, (group + 1) * stack)
        scores = dot_nt(head_stack(query_ref[:, lanes]), key_ref[:, lanes]) * scale
        bias = [
            [
                bias_ref[block, tile, head * ROW_BLOCK : (head + 1) * ROW_BLOCK]
                for head in range(group * heads, (group + 1) * heads)
                for block in range(blocks)
            ]
            for tile in range(tiles)
        ]
        scores = scores + jnp.concatenate([jnp.concatenate(b, axis=0) for b in bias], axis=1)
        exps = jnp.exp2(scores - jnp.max(scores, axis=1, keepdims=True))
        probs = (exps * (1.0 / jnp.sum(exps, axis=1, keepdims=True))).astype(bf16)
        prob_ref[rows] = probs
        merged = head_merge(dot_wide(probs, value_ref[:, lanes]), row_count)
        out_ref[:, lanes] = merged.astype(bf16)


def attend(query, both, bias, scale):
    micro_count, row_count, width = query.shape
    columns = both.shape[1]
    wide = PER_STEP * LANES
    groups = width // wide
    heads = PER_STEP * (LANES // HEAD_PAD)
    stack = heads * row_count
    own = pl.BlockSpec((None, row_count, wide), lambda m, g: (m, 0, g))
    whole = pl.BlockSpec((None, columns, wide), lambda m, g: (m, 0, g))
    later = pl.BlockSpec((None, columns, wide), lambda m, g: (m, 0, groups + g))
    return pl.pallas_call(
        functools.partial(attend_kernel, scale),
        grid=(micro_count, groups),
        in_specs=[
            own,
            whole,
            later,
            pl.BlockSpec(
                (None, row_count // ROW_BLOCK, columns // LANES, heads * ROW_BLOCK, LANES),
                lambda m, g: (m, 0, 0, g, 0),
            ),
        ],
        out_specs=[pl.BlockSpec((None, stack, columns), lambda m, g: (m, g, 0)), own],
        out_shape=[
            jax.ShapeDtypeStruct((micro_count, groups * stack, columns), bf16),
            jax.ShapeDtypeStruct((micro_count, row_count, width), bf16),
        ],
        compiler_params=pltpu.CompilerParams(vmem_limit_bytes=VMEM_LIMIT),
        cost_estimate=cost(30),
        name="attend",
    )(query, both, both, bias)


def attend_back_kernel(
    scale,
    query_ref,
    key_ref,
    value_ref,
    cot_ref,
    prob_ref,
    score_ref,
    query_cot_ref,
    key_cot_ref,
    value_cot_ref,
):
    row_count = query_ref.shape[0]
    blocks, tiles = score_ref.shape[:2]
    heads = LANES // HEAD_PAD
    stack = heads * row_count
    for group in range(query_ref.shape[1] // LANES):
        lanes = slice(group * LANES, (group + 1) * LANES)
        rows = slice(group * stack, (group + 1) * stack)
        cot_stack = head_stack(cot_ref[:, lanes])
        low_probs = prob_ref[rows]
        probs = low_probs.astype(f32)
        weighted = probs * dot_nt(cot_stack, value_ref[:, lanes])
        score_cot = weighted - probs * jnp.sum(weighted, axis=1, keepdims=True)
        for head in range(heads):
            to = slice((group * heads + head) * ROW_BLOCK, (group * heads + head + 1) * ROW_BLOCK)
            for block in range(blocks):
                at = head * row_count + block * ROW_BLOCK
                for tile in range(tiles):
                    score_ref[block, tile, to] = score_cot[
                        at : at + ROW_BLOCK, tile * LANES : (tile + 1) * LANES
                    ]
        low = score_cot.astype(bf16)
        merged = head_merge(dot_wide(low, key_ref[:, lanes]), row_count)
        query_cot_ref[:, lanes] = (merged * scale).astype(bf16)
        key_cot = dot_tn(low, head_stack(query_ref[:, lanes])) * scale
        key_cot_ref[:, lanes] = key_cot.astype(bf16)
        value_cot_ref[:, lanes] = dot_tn(low_probs, cot_stack).astype(bf16)


def attend_back(query, both, cot, probs, scale):
    micro_count, row_count, width = query.shape
    columns = both.shape[1]
    block = (
        row_count // ROW_BLOCK,
        columns // LANES,
        PER_STEP * (LANES // HEAD_PAD) * ROW_BLOCK,
        LANES,
    )
    wide = PER_STEP * LANES
    groups = width // wide
    heads = PER_STEP * (LANES // HEAD_PAD)
    stack = heads * row_count
    own = pl.BlockSpec((None, row_count, wide), lambda m, g: (m, 0, g))
    whole = pl.BlockSpec((None, columns, wide), lambda m, g: (m, 0, g))
    later = pl.BlockSpec((None, columns, wide), lambda m, g: (m, 0, groups + g))
    return pl.pallas_call(
        functools.partial(attend_back_kernel, scale),
        grid=(micro_count, groups),
        in_specs=[
            own,
            whole,
            later,
            own,
            pl.BlockSpec((None, stack, columns), lambda m, g: (m, g, 0)),
        ],
        out_specs=[
            pl.BlockSpec((None,) + block, lambda m, g: (m, 0, 0, g, 0)),
            own,
            whole,
            whole,
        ],
        out_shape=[
            jax.ShapeDtypeStruct(
                (micro_count,) + block[:2] + (groups * block[2], LANES), f32
            ),
            jax.ShapeDtypeStruct((micro_count, row_count, width), bf16),
            jax.ShapeDtypeStruct((micro_count, columns, width), bf16),
            jax.ShapeDtypeStruct((micro_count, columns, width), bf16),
        ],
        compiler_params=pltpu.CompilerParams(vmem_limit_bytes=VMEM_LIMIT),
        cost_estimate=cost(35),
        name="attend_back",
    )(query, both, both, cot, probs)


def spans(start, stop, width):
    pieces = []
    at = start
    while at < stop:
        block = at // width
        last = min(stop, (block + 1) * width)
        pieces.append((block, at - block * width, last - block * width, at - start))
        at = last
    return pieces


def roll_matrix(size, shift):
    row = lax.broadcasted_iota(jnp.int32, (size, size), 0) + shift
    row = jnp.where(row >= size, row - size, row)
    column = lax.broadcasted_iota(jnp.int32, (size, size), 1)
    return jnp.where(row == column, 1.0, 0.0).astype(bf16)


def weight_loads(me, mine, other, weights, sems, first):
    core = me & 1
    return [
        pltpu.make_async_copy(
            src.at[i], weights.at[2 * i + (core ^ side)], sems.at[first + 2 * side + i]
        )
        for side, src in enumerate((mine, other))
        for i in range(2)
    ]


def project_kernel(
    at_ref, a0, a1, a2, a3, w0, w1, query_ref, both_ref, rolled_ref, rows, weights, sems
):
    micro_count, group_rows, width = rolled_ref.shape
    tok_rows = group_rows // 4
    wide = query_ref.shape[2]
    block_width = weights.shape[2]
    me = at_ref[0]
    row_copies = [
        pltpu.make_async_copy(src, rows.at[me ^ r], sems.at[r])
        for r, src in enumerate((a0, a1, a2, a3))
    ]
    weight_copies = weight_loads(me, w0, w1, weights, sems, 4)
    for copy in row_copies + weight_copies:
        copy.start()
    for copy in row_copies:
        copy.wait()
    for micro in range(micro_count):
        group = jnp.concatenate(
            [rows[s, micro * tok_rows : (micro + 1) * tok_rows, :] for s in range(4)], axis=0
        )
        turn = roll_matrix(group_rows, at_ref[1 + micro])
        rolled_ref[micro] = dot_wide(turn, group).astype(bf16)
    for copy in weight_copies:
        copy.wait()

    def one(micro, carry):
        own = rows[me, pl.ds(micro * tok_rows, tok_rows), :]
        for block, first, last, offset in spans(0, wide, block_width):
            query_ref[micro, :, offset : offset + last - first] = dot_wide(
                own, weights[block, :, first:last]
            ).astype(bf16)
        group = rolled_ref[micro]
        for block, first, last, offset in spans(wide, 3 * wide, block_width):
            both_ref[micro, :, offset : offset + last - first] = dot_wide(
                group, weights[block, :, first:last]
            ).astype(bf16)
        return carry

    lax.fori_loop(0, micro_count, one, 0)


def project(places, rows, weights, micro_count, wide):
    total_rows, width = rows[0].shape
    tok_rows = total_rows // micro_count
    group_rows = 4 * tok_rows
    block_width = weights[0].shape[2]
    whole = pl.BlockSpec(memory_space=pltpu.VMEM)
    return pl.pallas_call(
        project_kernel,
        in_specs=[pl.BlockSpec(memory_space=pltpu.SMEM)]
        + [pl.BlockSpec(memory_space=pl.ANY)] * 6,
        out_specs=[whole] * 3,
        out_shape=[
            jax.ShapeDtypeStruct((micro_count, tok_rows, wide), bf16),
            jax.ShapeDtypeStruct((micro_count, group_rows, 2 * wide), bf16),
            jax.ShapeDtypeStruct((micro_count, group_rows, width), bf16),
        ],
        scratch_shapes=[
            pltpu.VMEM((4, total_rows, width), bf16),
            pltpu.VMEM((4, width, block_width), bf16),
            pltpu.SemaphoreType.DMA((8,)),
        ],
        compiler_params=pltpu.CompilerParams(vmem_limit_bytes=VMEM_LIMIT),
        cost_estimate=cost(10),
        name="project",
    )(places, *rows, *weights)


def project_back_kernel(
    at_ref,
    query_ref,
    key_ref,
    value_ref,
    rolled_ref,
    own_ref,
    w0,
    w1,
    own_cot_ref,
    group_keep_ref,
    group_give_ref,
    grad_keep_ref,
    grad_give_ref,
    weights,
    stage,
    sems,
):
    micro_count, group_rows, width = rolled_ref.shape
    tok_rows = group_rows // 4
    wide = query_ref.shape[2]
    block_width = weights.shape[2]
    me = at_ref[0]
    weight_copies = weight_loads(me, w0, w1, weights, sems, 0)
    for copy in weight_copies:
        copy.start()
    grad_copies = []
    own_turned = own_ref[...].T
    rolled_turned = rolled_ref[...].reshape(-1, width).T
    for block in range(4):
        low, high = block * block_width, (block + 1) * block_width
        parts = []
        for which, cot_ref in enumerate((query_ref, key_ref, value_ref)):
            first = max(low, which * wide) - which * wide
            last = min(high, (which + 1) * wide) - which * wide
            if first < last:
                left = own_turned if which == 0 else rolled_turned
                right = cot_ref[...].reshape(-1, wide)[:, first:last]
                parts.append(dot_wide(left, right).astype(bf16))
        stage[block] = parts[0] if len(parts) == 1 else jnp.concatenate(parts, axis=1)
        for leaves, target in enumerate((grad_keep_ref, grad_give_ref)):
            copy = pltpu.make_async_copy(
                stage.at[block], target.at[(me ^ block) >> 1], sems.at[4 + block]
            )
            grad_copies.append((((me ^ block) & 1) == leaves, copy))

            @pl.when(((me ^ block) & 1) == leaves)
            def _():
                copy.start()

    for copy in weight_copies:
        copy.wait()

    def one(micro, carry):
        total = None
        for block, first, last, offset in spans(0, wide, block_width):
            part = dot_nt(
                query_ref[micro, :, offset : offset + last - first], weights[block, :, first:last]
            )
            total = part if total is None else total + part
        own_cot_ref[micro] = total
        total = None
        for block, first, last, offset in spans(wide, 3 * wide, block_width):
            source = key_ref if offset < wide else value_ref
            at = offset if offset < wide else offset - wide
            end = at + last - first
            pieces = [(source, at, end, first)]
            if offset < wide < offset + last - first:
                cut = wide - offset
                pieces = [(key_ref, offset, wide, first), (value_ref, 0, end - wide, first + cut)]
            for ref, begin, stop, column in pieces:
                part = dot_nt(
                    ref[micro, :, begin:stop], weights[block, :, column : column + stop - begin]
                )
                total = part if total is None else total + part
        turn = roll_matrix(group_rows, at_ref[1 + micro])
        back = dot_tn(turn, total.astype(bf16)).astype(bf16)
        for s in range(4):
            for leaves, target in enumerate((group_keep_ref, group_give_ref)):

                @pl.when(((me ^ s) & 1) == leaves)
                def _():
                    target[(me ^ s) >> 1, pl.ds(micro * tok_rows, tok_rows), :] = back[
                        s * tok_rows : (s + 1) * tok_rows
                    ]

        return carry

    lax.fori_loop(0, micro_count, one, 0)
    for started, copy in grad_copies:

        @pl.when(started)
        def _():
            copy.wait()


def project_back(places, query_cot, key_cot, value_cot, rolled, own, weights):
    micro_count, group_rows, width = rolled.shape
    tok_rows = group_rows // 4
    block_width = weights[0].shape[2]
    whole = pl.BlockSpec(memory_space=pltpu.VMEM)
    away = pl.BlockSpec(memory_space=pl.ANY)
    return pl.pallas_call(
        project_back_kernel,
        in_specs=[pl.BlockSpec(memory_space=pltpu.SMEM)] + [whole] * 5 + [away] * 2,
        out_specs=[whole, whole, whole, away, away],
        out_shape=[jax.ShapeDtypeStruct((micro_count, tok_rows, width), f32)]
        + [jax.ShapeDtypeStruct((2, micro_count * tok_rows, width), bf16)] * 2
        + [jax.ShapeDtypeStruct((2, width, block_width), bf16)] * 2,
        scratch_shapes=[
            pltpu.VMEM((4, width, block_width), bf16),
            pltpu.VMEM((4, width, block_width), bf16),
            pltpu.SemaphoreType.DMA((8,)),
        ],
        compiler_params=pltpu.CompilerParams(vmem_limit_bytes=VMEM_LIMIT),
        cost_estimate=cost(14),
        name="project_back",
    )(places, query_cot, key_cot, value_cot, rolled, own, *weights)


CHUNKS = 8


def dense_kernel(
    att_ref,
    start_ref,
    cot_ref,
    gain_ref,
    place_ref,
    big_ref,
    out_ref,
    mid_cot_ref,
    att_cot_ref,
    gain_cot_ref,
    grad_ref,
    up_v,
    down_v,
    output_v,
    mid_v,
    normed_v,
    inv_v,
    ffn_v,
    branch_v,
    total_v,
    back_v,
    up_s,
    cot_s,
    gelu_v,
    cot_v,
    up_stage,
    down_stage,
    output_stage,
    zero_v,
    sems,
    grad_sems,
):
    rows, width = start_ref.shape
    own = width // CHUNKS
    third = own // 3
    pair = CHUNKS // 4
    step = rows // 3
    output_copy = pltpu.make_async_copy(
        big_ref.at[:, pl.ds(0, 3), pl.ds(2 * own, third)], output_v, sems.at[8]
    )

    def up_copy(j):
        return pltpu.make_async_copy(big_ref.at[:, j, pl.ds(0, own)], up_v.at[j], sems.at[j])

    def down_copy(j):
        return pltpu.make_async_copy(
            big_ref.at[pl.ds(j * pair, pair), :, pl.ds(own, own)], down_v.at[j], sems.at[4 + j]
        )

    def up_out(j):
        return pltpu.make_async_copy(
            up_stage.at[j], grad_ref.at[:, j, pl.ds(0, own)], grad_sems.at[j]
        )

    def down_out(j):
        return pltpu.make_async_copy(
            down_stage.at[j],
            grad_ref.at[pl.ds(j * pair, pair), :, pl.ds(own, own)],
            grad_sems.at[4 + j],
        )

    output_copy.start()
    for j in range(4):
        up_copy(j).start()
        down_copy(j).start()
    zero_v[...] = jnp.zeros_like(zero_v)
    zero_copy = pltpu.make_async_copy(
        zero_v, grad_ref.at[:, 3, pl.ds(2 * own, third)], grad_sems.at[8]
    )
    zero_copy.start()
    att = dot_nt(att_ref[...], place_ref[...]).astype(bf16)
    branch_v[...] = cot_ref[...].astype(bf16)
    output_copy.wait()
    output_w = output_v[...].reshape(width, width)
    gain = gain_ref[...]
    mid_v[...] = start_ref[...] + dot_wide(att, output_w)
    for part in range(3):
        at = slice(part * step, (part + 1) * step)
        mid = mid_v[at]
        centre = mid - jnp.mean(mid, axis=1, keepdims=True)
        inv_std = lax.rsqrt(jnp.mean(centre * centre, axis=1, keepdims=True) + NORM_EPS)
        normed = centre * inv_std
        normed_v[at] = normed
        inv_v[at] = jnp.broadcast_to(inv_std, (step, LANES))
        ffn_v[at] = (normed * gain).astype(bf16)
    ffn_turned = ffn_v[...].T
    total_v[...] = mid_v[...]
    back_v[...] = jnp.zeros_like(back_v)

    def one(j, carry):
        up_copy(j).wait()
        down_copy(j).wait()
        up_w = up_v[j].reshape(width, width)
        down_w = down_v[j].reshape(width, width)
        up_s[...] = dot_wide(ffn_v[...], up_w)
        cot_s[...] = dot_nt(branch_v[...], down_w)
        gelus, cots = [], []
        for start in range(0, rows, 64):
            at = slice(start, start + 64)
            up = up_s[at]
            square = up * up
            root = math.sqrt(2.0 / math.pi)
            bend = jnp.tanh(up * (root + (root * 0.044715) * square))
            half = 0.5 + 0.5 * bend
            slope = half + up * (0.5 - 0.5 * bend * bend) * (
                root + (root * 3 * 0.044715) * square
            )
            gelus.append((up * half).astype(bf16))
            cots.append((cot_s[at] * slope).astype(bf16))
        gelu = jnp.concatenate(gelus, axis=0)
        cot = jnp.concatenate(cots, axis=0)
        gelu_v[...] = gelu
        cot_v[...] = cot
        total_v[...] += dot_wide(gelu_v[...], down_w)
        back_v[...] += dot_nt(cot_v[...], up_w)
        up_stage[j] = dot_wide(ffn_turned, cot_v[...]).astype(bf16).reshape(up_stage.shape[1:])
        up_out(j).start()
        down_stage[j] = (
            dot_tn(gelu_v[...], branch_v[...]).astype(bf16).reshape(down_stage.shape[1:])
        )
        down_out(j).start()
        return carry

    lax.fori_loop(0, 4, one, 0)
    out_ref[...] = total_v[...].astype(bf16)
    gain_cot = jnp.zeros((1, width), f32)
    for part in range(3):
        at = slice(part * step, (part + 1) * step)
        back = back_v[at]
        normed = normed_v[at]
        gain_cot = gain_cot + jnp.sum(back * normed, axis=0, keepdims=True)
        scaled = back * gain
        mid_cot = cot_ref[at] + inv_v[at][:, :1] * (
            scaled
            - jnp.mean(scaled, axis=1, keepdims=True)
            - normed * jnp.mean(scaled * normed, axis=1, keepdims=True)
        )
        mid_cot_ref[at] = mid_cot
        cot_v[at] = mid_cot.astype(bf16)
    gain_cot_ref[...] = gain_cot
    att_cot = dot_nt(cot_v[...], output_w).astype(bf16)
    att_cot_ref[...] = dot_wide(att_cot, place_ref[...]).astype(bf16)
    output_stage[...] = dot_tn(att, cot_v[...]).astype(bf16).reshape(output_stage.shape)
    output_out = pltpu.make_async_copy(
        output_stage, grad_ref.at[:, pl.ds(0, 3), pl.ds(2 * own, third)], grad_sems.at[9]
    )
    output_out.start()
    for j in range(4):
        up_out(j).wait()
        down_out(j).wait()
    output_out.wait()
    zero_copy.wait()


def dense(attended, start, out_cot, gain, place_heads, big):
    rows, width = start.shape
    wide = attended.shape[1]
    own = width // CHUNKS
    third = own // 3
    pair = CHUNKS // 4
    whole = pl.BlockSpec(memory_space=pltpu.VMEM)
    away = pl.BlockSpec(memory_space=pl.ANY)
    return pl.pallas_call(
        dense_kernel,
        in_specs=[whole] * 5 + [away],
        out_specs=[whole] * 4 + [away],
        out_shape=[
            jax.ShapeDtypeStruct((rows, width), bf16),
            jax.ShapeDtypeStruct((rows, width), f32),
            jax.ShapeDtypeStruct((rows, wide), bf16),
            jax.ShapeDtypeStruct((1, width), f32),
            jax.ShapeDtypeStruct(big.shape, bf16),
        ],
        scratch_shapes=[
            pltpu.VMEM((4, CHUNKS, own, width), bf16),
            pltpu.VMEM((4, pair, 4, own, width), bf16),
            pltpu.VMEM((CHUNKS, 3, third, width), bf16),
            pltpu.VMEM((rows, width), f32),
            pltpu.VMEM((rows, width), f32),
            pltpu.VMEM((rows, LANES), f32),
            pltpu.VMEM((rows, width), bf16),
            pltpu.VMEM((rows, width), bf16),
            pltpu.VMEM((rows, width), f32),
            pltpu.VMEM((rows, width), f32),
            pltpu.VMEM((rows, width), f32),
            pltpu.VMEM((rows, width), f32),
            pltpu.VMEM((rows, width), bf16),
            pltpu.VMEM((rows, width), bf16),
            pltpu.VMEM((4, CHUNKS, own, width), bf16),
            pltpu.VMEM((4, pair, 4, own, width), bf16),
            pltpu.VMEM((CHUNKS, 3, third, width), bf16),
            pltpu.VMEM((CHUNKS, third, width), bf16),
            pltpu.SemaphoreType.DMA((9,)),
            pltpu.SemaphoreType.DMA((10,)),
        ],
        compiler_params=pltpu.CompilerParams(vmem_limit_bytes=VMEM_LIMIT),
        cost_estimate=cost(25),
        name="dense",
    )(attended, start, out_cot, gain, place_heads, big)


def place_matrix(source, piece, padded):
    index = jnp.arange(source, dtype=jnp.int32)
    target = (index // piece) * padded + index % piece
    spots = jnp.arange(source // piece * padded, dtype=jnp.int32)
    return (target[:, None] == spots[None, :]).astype(bf16)


def dot_low(left, right):
    return jnp.dot(left, right, preferred_element_type=f32).astype(bf16)


def roll_rows(value, shift, axis):
    size = value.shape[axis]
    twice = jnp.concatenate([value, value], axis=axis)
    return lax.dynamic_slice_in_dim(twice, shift, size, axis)


def gather_shards(shard):
    return lax.all_gather(shard, "fsdp", axis=0, tiled=True)


def reduce_shards(grad):
    part = lax.psum_scatter(grad, "fsdp", scatter_dimension=0, tiled=True)
    return lax.psum(part.astype(bf16), "seq").astype(f32)[0]


LINE = 4


def place():
    fsdp_index, seq_index = lax.axis_index("fsdp"), lax.axis_index("seq")
    return fsdp_index // 2, fsdp_index % 2, seq_index // 2, seq_index % 2


def flip(value, axis, bit):
    return lax.ppermute(value, axis, [(i, i ^ bit) for i in range(lax.axis_size(axis))])


def along_line(value, step):
    pairs = [
        (z * 2 + y, (z + step) % LINE * 2 + y) for z in range(LINE) for y in range(2)
    ]
    return lax.ppermute(value, "fsdp", pairs)


def line_gather(block, axis=0):
    z = place()[0]
    parts = [block] + [along_line(block, step) for step in range(1, LINE)]
    ring = jnp.stack([parts[-step % LINE] for step in range(LINE)] * 2, axis=axis)
    return lax.dynamic_slice_in_dim(ring, (LINE - z) % LINE, LINE, axis)


def in_line(parts, axis=0):
    z = place()[0]
    return jnp.stack(
        [lax.select_n((z + LINE - at) % LINE, *parts) for at in range(LINE)], axis=axis
    )


def pair_gather(value, bit_axis, bit, own_bit, axis=0):
    other = flip(value, bit_axis, bit)
    return jnp.stack(
        [jnp.where(own_bit == 0, value, other), jnp.where(own_bit == 0, other, value)], axis=axis
    )


def pair_reduce(value, bit_axis, bit, own_bit, axis=0):
    keep, give = pair_split(value, own_bit, axis)
    return add_low(keep, flip(give, bit_axis, bit))


def pair_split(value, own_bit, axis):
    keep = lax.dynamic_index_in_dim(value, own_bit, axis, keepdims=False)
    return keep, lax.dynamic_index_in_dim(value, 1 - own_bit, axis, keepdims=False)


def add_low(left, right):
    return (left.astype(f32) + right.astype(f32)).astype(left.dtype)


def line_reduce(value, *others):
    z = place()[0]
    total = lax.dynamic_index_in_dim(value, z, 0, keepdims=False).astype(f32)
    for step in range(1, LINE):
        give = lax.dynamic_index_in_dim(value, (z + step) % LINE, 0, keepdims=False)
        total = total + after(along_line(give, step), *others).astype(f32)
    return total


def fast_mesh():
    return (lax.axis_size("fsdp"), lax.axis_size("seq")) == (2 * LINE, 4)


def exact_parts(value):
    parts = []
    for _ in range(2):
        part = lax.reduce_precision(value, 8, 7)
        parts.append(part.astype(bf16))
        value = value - part
    return parts + [value.astype(bf16)]


def gather_small(small, stamps):
    if not fast_mesh():
        whole = lax.all_gather(small, "fsdp", axis=0)
        return whole, lax.all_gather(stamps, "fsdp", axis=0), whole
    parts = jnp.concatenate(exact_parts(stamps))
    row = jnp.pad(parts, (0, LANES - parts.shape[0]))[None]
    packed = jnp.concatenate([small, jnp.pad(row, ((0, 15), (0, 0)))], axis=0)
    line = line_gather(packed)
    packed = pair_gather(line, "fsdp", 1, place()[1], 1)
    packed = packed.reshape((2 * LINE,) + packed.shape[2:])
    count = stamps.shape[0]
    row = packed[:, small.shape[0]].astype(f32)
    stamps_all = row[:, :count] + row[:, count : 2 * count] + row[:, 2 * count : 3 * count]
    return packed[:, : small.shape[0]], stamps_all, line


def after(value, *others):
    if not others:
        return value
    return lax.optimization_barrier((value,) + others)[0]


def scatter_groups(value):
    if not fast_mesh():
        return lax.psum_scatter(value, "fsdp", scatter_dimension=0, tiled=True)[0], value
    y, core = place()[1], place()[3]
    half = value.shape[2] // 2
    value = lax.dynamic_slice_in_dim(value, core * half, half, 2)
    value = value.reshape((LINE, 2) + value.shape[1:])
    first = pair_reduce(value, "fsdp", 1, y, 1)
    value = line_reduce(first)
    other = flip(value, "seq", 1)
    value = jnp.concatenate(
        [jnp.where(core == 0, value, other), jnp.where(core == 0, other, value)], axis=1
    )
    return value, first


def gather_big(output_weight, up_weight, down_weight, *others):
    if not fast_mesh():
        up, down, output = (gather_shards(w) for w in (up_weight, down_weight, output_weight))
        width = output.shape[0]
        own = width // CHUNKS
        return join_big(
            up.reshape(CHUNKS, own, 4, width).transpose(0, 2, 1, 3),
            down.reshape(CHUNKS, 4, own, width),
            output.reshape(CHUNKS, own, width),
        )
    seq_index = lax.axis_index("seq")
    own, width = output_weight.shape
    third = own // 3
    quarter = jnp.concatenate(
        [
            lax.dynamic_slice_in_dim(up_weight, seq_index * width, width, 1),
            lax.dynamic_slice_in_dim(down_weight, seq_index * own, own, 0),
            lax.dynamic_slice_in_dim(
                jnp.pad(output_weight, ((0, third), (0, 0))), seq_index * third, third, 0
            ),
        ],
        axis=0,
    )
    big = lax.all_gather(after(quarter, *others), ("fsdp", "seq"), axis=0)
    return big.reshape((CHUNKS, 4) + quarter.shape)


def join_big(up, down, output):
    chunks, own, width = output.shape
    third = own // 3
    output = jnp.pad(output, ((0, 0), (0, third), (0, 0))).reshape(chunks, 4, third, width)
    return jnp.concatenate([up, down, output], axis=2)


def reduce_big(grad):
    chunks, quarters, rows, width = grad.shape
    own = width // CHUNKS
    if not fast_mesh():
        fsdp_count = lax.axis_size("fsdp")
        up = grad[:, :, :own].transpose(0, 2, 1, 3).reshape(fsdp_count, -1, 4 * width)
        down = grad[:, :, own : 2 * own].reshape(fsdp_count, -1, width)
        output = grad[:, :3, 2 * own :].reshape(fsdp_count, -1, width)
        return tuple(reduce_shards(g) for g in (up, down, output))
    total = lax.psum_scatter(
        grad.reshape(chunks * quarters, rows, width),
        ("fsdp", "seq"),
        scatter_dimension=0,
        tiled=True,
    )
    return total[0]


def four_ways(value):
    return value, flip(value, "seq", 1), flip(value, "seq", 2)


def fourth(three, *others):
    if not fast_mesh():
        return three
    value, near, across = three
    across = after(across, *others)
    return value, near, across, flip(across, "seq", 1)


def gather_projections(weight):
    columns = weight.shape[1] // 4
    if not fast_mesh():
        full = gather_shards(weight)
        blocks = [full[:, i * columns : (i + 1) * columns] for i in range(4)]
        return (jnp.stack(blocks[::2]), jnp.stack(blocks[1::2])), weight
    y, core = place()[1], place()[3]
    pair = jnp.stack(
        [
            lax.dynamic_slice_in_dim(weight, (core + 2 * i) * columns, columns, 1)
            for i in range(2)
        ]
    )
    line = line_gather(pair, 1)
    return (line, flip(line, "fsdp", 1)), line


def finish_projections(pair, *others):
    if not fast_mesh():
        return pair
    y = place()[1]
    line, other = pair
    other = after(other, *others)
    pair = jnp.stack(
        [jnp.where(y == 0, line, other), jnp.where(y == 0, other, line)], axis=2
    ).reshape(2, -1, line.shape[-1])
    return pair, flip(pair, "seq", 1)


def gather_group(value):
    if not fast_mesh():
        rows = lax.all_gather(value, "seq", axis=0)
        return tuple(rows[i] for i in range(4))
    return four_ways(value)


def in_order(keep, give):
    return keep[0], give[0], keep[1], give[1]


def reduce_group(keep, give):
    order = jnp.stack(in_order(keep, give))
    return lax.psum_scatter(order, "seq", scatter_dimension=0, tiled=True)[0].astype(f32)


def reduce_projections(keep, give):
    order = jnp.concatenate(in_order(keep, give), axis=1)
    return reduce_shards(order.reshape(lax.axis_size("fsdp"), -1, order.shape[1]))


def gather_finals(value, *others):
    x, core = place()[2:]
    width = value.shape[1]
    own = width // CHUNKS
    other = after(flip(value, "seq", 2), *others)
    total = jnp.stack([jnp.where(x == 0, value, other), jnp.where(x == 0, other, value)])
    total = pair_gather(total, "seq", 1, core, 1).astype(f32)
    total = total.reshape((4,) + value.shape)
    return (
        total[:, :own].transpose(1, 0, 2).reshape(own, -1),
        total[:, own : 2 * own].transpose(1, 0, 2).reshape(own, -1),
        total[:, 2 * own : 3 * own].reshape(-1, width),
        total[:3, 3 * own :].reshape(own, width),
    )


def join_lanes(value, lanes):
    return jnp.concatenate(
        [value[:, at : at + lanes] for at in range(0, value.shape[1], lanes)], axis=0
    )


def line_exchange(give, times, *others):
    z = place()[0]
    rows = give.shape[1]
    total = lax.dynamic_index_in_dim(give, z, 0, keepdims=False).astype(f32)
    parts = [times]
    for step in range(1, LINE):
        piece = lax.dynamic_index_in_dim(give, (z + step) % LINE, 0, keepdims=False)
        other = after(along_line(jnp.concatenate([piece, times], axis=0), step), *others)
        total = total + other[:rows].astype(f32)
        parts.append(other[rows:])
    return total, in_line(parts)


def pair_exchange(grad, times):
    y = place()[1]
    rows, lanes = grad.shape[2:]
    keep = lax.dynamic_index_in_dim(grad, y, 1, keepdims=False)
    give = lax.dynamic_index_in_dim(grad, 1 - y, 1, keepdims=False)
    give = jnp.concatenate([give.reshape(LINE * rows, lanes), times], axis=0)
    other = flip(give, "fsdp", 1)
    keep = add_low(keep, other[: LINE * rows].reshape(keep.shape))
    late = other[LINE * rows :]
    times = jnp.concatenate(
        [jnp.where(y == 0, times, late), jnp.where(y == 0, late, times)], axis=0
    )
    return keep, times


def body(
    hidden_in,
    row_types,
    lengths,
    noise_time,
    coords,
    residue_table,
    atom_table,
    time_weight,
    first_gain,
    query_weight,
    key_weight,
    value_weight,
    output_weight,
    kernel_mean,
    kernel_width,
    pair_weight,
    second_gain,
    up_weight,
    down_weight,
    force_weight,
    layer_cot,
    force_cot,
):
    seq_count = lax.axis_size("seq")
    fsdp_count = lax.axis_size("fsdp")
    seq_index = lax.axis_index("seq")
    micro_count, tok_rows, model_width = hidden_in.shape
    group_rows = tok_rows * seq_count
    own_kernels, head_count = pair_weight.shape
    kernels = own_kernels * fsdp_count
    head_dim = model_width // head_count
    inv_root = head_dim ** (-0.5)
    wide_heads = head_count * HEAD_PAD
    total_rows = micro_count * tok_rows
    residues, own_width = residue_table.shape
    types = residues + atom_table.shape[0]
    offset = seq_index * tok_rows

    small_rows = types + 16
    small = jnp.concatenate(
        [
            residue_table,
            atom_table,
            force_weight,
            first_gain[None],
            second_gain[None],
            jnp.zeros((small_rows - types - 5, own_width), bf16),
        ],
        axis=0,
    )
    small = jnp.pad(small, ((0, 0), (0, LANES - own_width)))
    kernel_rows = jnp.concatenate([pair_weight, kernel_mean[:, None], kernel_width[:, None]], axis=1)
    kernel_rows = jnp.pad(kernel_rows, ((0, 0), (0, LANES - head_count - 2)))
    big = gather_big(output_weight, up_weight, down_weight)
    small_all, stamps_all, small_line = gather_small(
        jnp.concatenate([small, kernel_rows], axis=0), noise_time[:, 0].reshape(-1)
    )
    head_place = place_matrix(model_width, head_dim, HEAD_PAD)
    qkv_weight = jnp.concatenate(
        [dot_low(w, head_place) for w in (query_weight, key_weight, value_weight)], axis=1
    )
    qkv_blocks, qkv_line = gather_projections(qkv_weight)
    kernel_all = small_all[:, small_rows:].reshape(kernels, LANES)
    pair_full = kernel_all[:, :head_count].astype(f32)
    mean_full = kernel_all[:, head_count].astype(f32)
    width_full = kernel_all[:, head_count + 1].astype(f32)
    spread = place_matrix(model_width, own_width, LANES)
    tables = dot_low(
        small_all[:, :small_rows].transpose(1, 0, 2).reshape(small_rows, fsdp_count * LANES),
        spread.T,
    )
    type_table = tables[:types]
    force_wide = tables[types : types + 3].astype(f32)
    gain_one = tables[types + 3].astype(f32)
    gain_two = tables[types + 4].astype(f32)

    coords = after(coords, small_line)
    doc_lengths = lengths[:, 0]
    documents = jnp.arange(doc_lengths.shape[1], dtype=jnp.int32)
    earlier = documents[:, None] <= documents[None, :]
    bounds = jnp.sum(jnp.where(earlier[None], doc_lengths[:, :, None], 0), axis=1)
    first_len = doc_lengths[:, 0]
    all_rows = jnp.arange(group_rows, dtype=jnp.int32)
    key_doc = jnp.sum((all_rows[None, :, None] >= bounds[:, None, :]).astype(jnp.int32), axis=2)
    query_doc = lax.dynamic_slice_in_dim(key_doc, offset, tok_rows, 1)
    query_pos = lax.dynamic_slice_in_dim(coords, offset, tok_rows, 2)
    roll_index = (all_rows[None, :] + first_len[:, None]) % group_rows
    rolled_doc = jnp.sum(
        (roll_index[:, :, None] >= bounds[:, None, :]).astype(jnp.int32), axis=2
    )
    rolled_pos = jnp.stack([roll_rows(coords[m], first_len[m], 1) for m in range(micro_count)])
    same_doc = query_doc[:, :, None] == rolled_doc[:, None, :]
    mask = jnp.where(same_doc, 0.0, -1e30).astype(f32)
    delta = query_pos[:, :, :, None] - rolled_pos[:, :, None, :]
    dist = jnp.sqrt(jnp.sum(delta * delta, axis=1))
    long_row = (query_doc == 1).reshape(micro_count, tok_rows // TILE_ROWS, TILE_ROWS)
    flags = jnp.where(
        jnp.all(long_row, axis=2), 0, jnp.where(jnp.any(long_row, axis=2), 2, 1)
    ).astype(jnp.int32)

    scale_k = 1.0 / (math.sqrt(2.0 * math.pi) * width_full)
    coef = (-0.5 * LOG2E) / (width_full * width_full)
    mean_wide = jnp.broadcast_to(mean_full[:, None], (kernels, LANES))
    coef_wide = jnp.broadcast_to(coef[:, None], (kernels, LANES))
    base_wide = jnp.broadcast_to(jnp.log2(scale_k)[:, None], (kernels, LANES))
    bias_weight = pair_full.T.astype(bf16)
    bias_args = (mask, mean_wide, coef_wide, base_wide, bias_weight)

    doc_hot = (
        query_doc[:, :, None] == jnp.arange(doc_lengths.shape[1], dtype=jnp.int32)
    ).astype(f32)
    type_hot = (
        row_types.reshape(total_rows)[:, None] == jnp.arange(types, dtype=jnp.int32)
    ).astype(bf16)
    time_low = sinus_columns(
        stamps_all, model_width, lax.axis_index("fsdp") * own_width, own_width
    )
    time_proj = dot_wide(time_low.reshape(-1, own_width), time_weight)
    time_proj, time_step = scatter_groups(time_proj.reshape(fsdp_count, -1, model_width))
    bias = pair_bias(0, None, flags, dist, *bias_args)
    bias = pair_bias(1, bias, flags, after(dist, qkv_line, time_step), *bias_args)
    time_proj = time_proj.reshape(micro_count, -1, model_width)
    start_state = (
        hidden_in.astype(f32)
        + dot_wide(type_hot, type_table).reshape(hidden_in.shape)
        + jnp.einsum("min,mnd->mid", doc_hot, time_proj, precision=EXACT)
    ).reshape(total_rows, model_width)
    normed_in, normed_one, inv_one = norm_forward(start_state, gain_one)
    attn_in = normed_in.astype(bf16)

    four = seq_index if fast_mesh() else 0
    places = jnp.concatenate([jnp.full((1,), four, jnp.int32), first_len])
    attn_rows = gather_group(attn_in)
    for micro in range(2, micro_count):
        bias = pair_bias(micro, bias, flags, after(dist, attn_in), *bias_args)
    attn_rows = fourth(attn_rows, bias)
    qkv_blocks = finish_projections(qkv_blocks, bias)
    queries, both, rolled = project(places, attn_rows, qkv_blocks, micro_count, wide_heads)
    probs, attended = attend(queries, both, bias, inv_root * LOG2E)
    forces_cot = force_cot.transpose(1, 0, 2).reshape(3, total_rows)
    out_grad = layer_cot.reshape(total_rows, model_width).astype(f32)
    for axis in range(3):
        out_grad = out_grad + forces_cot[axis][:, None] * force_wide[axis][None, :]
    layer_out, mid_grad, attended_grad, gain_two_grad, big_grad = dense(
        attended.reshape(total_rows, wide_heads),
        start_state,
        out_grad,
        gain_two[None],
        head_place,
        big,
    )
    big_sum = reduce_big(big_grad)
    forces = dot_nt(force_wide.astype(bf16), layer_out)
    forces = forces.reshape(3, micro_count, tok_rows).transpose(1, 0, 2)
    force_w_grad = jnp.dot(forces_cot, layer_out.astype(f32), precision=EXACT)

    score_cot, query_low, key_part, value_part = attend_back(
        queries,
        both,
        attended_grad.reshape(micro_count, tok_rows, wide_heads),
        probs,
        inv_root,
    )
    own_part, group_keep, group_give, qkv_keep, qkv_give = project_back(
        places, query_low, key_part, value_part, rolled, attn_in, qkv_blocks
    )

    def pair_sums(micro, earlier, *others):
        part = pair_grads(
            micro, flags, after(dist, earlier, *others), score_cot, mean_wide, coef_wide
        )
        return part if micro == 0 else earlier + part

    sums = pair_sums(0, group_give)
    if fast_mesh():
        group_other, qkv_other = (flip(v, "seq", 1) for v in (group_give, qkv_give))
        group_near = add_low(group_keep, after(group_other, sums))
        qkv_near = add_low(qkv_keep, after(qkv_other, sums))
        qkv_near = qkv_near.reshape((2, LINE, 2, -1) + qkv_near.shape[2:])
        pair_keep, pair_give = pair_split(qkv_near, place()[1], 2)
        group_other = flip(group_near[1], "seq", 2)
        qkv_other = flip(pair_give, "fsdp", 1)
        sums = pair_sums(1, sums, group_near, pair_give)
        group_sum = group_near[0].astype(f32) + after(group_other, sums).astype(f32)
    else:
        group_sum = reduce_group(group_keep, group_give)
    attn_in_grad = own_part.reshape(total_rows, model_width) + group_sum
    norm_part_one, gain_one_grad = norm_backward(attn_in_grad, normed_one, inv_one, gain_one)
    input_grad = mid_grad + norm_part_one

    input_low = input_grad.astype(bf16)
    type_grad = dot_tn(type_hot, input_low)
    time_cot = jnp.einsum(
        "min,mid->mnd",
        doc_hot.astype(bf16),
        input_low.reshape(micro_count, tok_rows, model_width),
        preferred_element_type=f32,
    ).reshape(-1, model_width)
    small_grad = jnp.concatenate(
        [
            type_grad,
            force_w_grad,
            gain_one_grad[None],
            gain_two_grad,
            jnp.zeros((small_rows - types - 5, model_width), f32),
        ],
        axis=0,
    )
    small_grad = dot_low(small_grad.astype(bf16), spread)
    small_grad = small_grad.reshape(small_rows, fsdp_count, LANES).transpose(1, 0, 2)

    def kernel_grads(sums):
        plain, once, once_low, twice, twice_low = (
            sums[k * head_count : (k + 1) * head_count].T for k in range(5)
        )
        centre = (mean_full - CENTRE)[:, None]
        once = once + once_low
        twice = twice + twice_low - centre * (2.0 * once - centre * plain)
        once = once - centre * plain
        pair_w_grad = plain * scale_k[:, None]
        inv_width = 1.0 / width_full
        mean_grad = jnp.sum(pair_full * once, axis=1) * scale_k * inv_width * inv_width
        width_grad = (
            jnp.sum(pair_full * (twice * (inv_width * inv_width)[:, None] - plain), axis=1)
            * scale_k
            * inv_width
        )
        grad = jnp.concatenate(
            [pair_w_grad, mean_grad[:, None], width_grad[:, None]], axis=1
        ).astype(bf16)
        grad = jnp.pad(grad, ((0, 0), (0, LANES - head_count - 2)))
        return grad.reshape(fsdp_count, own_kernels, LANES)

    if fast_mesh():
        small_other, time_other = (flip(v, "seq", 1) for v in (small_grad, time_cot))
        qkv_pair = add_low(pair_keep, after(qkv_other, small_grad, time_cot))
        qkv_other = flip(qkv_pair[1], "seq", 2)
        small_one, time_one = small_grad + small_other, time_cot + time_other
        for micro in range(2, micro_count):
            sums = pair_sums(micro, sums, qkv_pair, small_one, time_one)
        small_other, time_other = (flip(v, "seq", 2) for v in (small_one, time_one))
        qkv_far = add_low(qkv_pair[0], after(qkv_other, sums))
        kernel_grad = kernel_grads(after(sums, qkv_far))
        for bit in (1, 2):
            kernel_grad = kernel_grad + flip(kernel_grad, "seq", bit)
        small_two = small_one + after(small_other, sums)
        time_two = time_one + after(time_other, sums)
        small_two = jnp.concatenate([small_two, kernel_grad], axis=1)
        small_two = small_two.reshape((LINE, 2) + small_two.shape[1:])
        time_two = join_lanes(time_two.astype(bf16), LANES)
        small_half, time_pair = pair_exchange(small_two, time_two)
        qkv_own = line_reduce(qkv_far, small_half, time_pair).astype(bf16)
        finals = jnp.concatenate([qkv_own, big_sum], axis=0)
        small_sum, time_cots = line_exchange(small_half, time_pair, finals)
        time_cots = time_cots.reshape(
            fsdp_count, model_width // LANES, -1, LANES
        ).transpose(0, 2, 1, 3)
    else:
        for micro in range(1, micro_count):
            sums = pair_sums(micro, sums)
        small_sum = reduce_shards(jnp.concatenate([small_grad, kernel_grads(sums)], axis=1))
        time_cots = lax.all_gather(lax.psum(time_cot, "seq").astype(bf16), "fsdp", axis=0)
        finals = (reduce_projections(qkv_keep, qkv_give),) + big_sum
    row_sum = small_sum[:small_rows, :own_width]
    kernel_sum = small_sum[small_rows:]
    time_sum = dot_tn(time_low.reshape(-1, own_width), time_cots.reshape(-1, model_width))
    if fast_mesh():
        finals = gather_finals(finals, small_sum, time_cots)
    qkv_sum, up_sum, down_sum, output_sum = finals
    qkv_low = join_lanes(qkv_sum.astype(bf16), wide_heads)
    query_sum, key_sum, value_sum = dot_nt(qkv_low, head_place).reshape(3, -1, model_width)
    return (
        layer_out.reshape(hidden_in.shape),
        forces,
        input_grad.reshape(hidden_in.shape),
        row_sum[:residues],
        row_sum[residues:types],
        time_sum,
        row_sum[types + 3],
        query_sum,
        key_sum,
        value_sum,
        output_sum,
        kernel_sum[:, head_count],
        kernel_sum[:, head_count + 1],
        kernel_sum[:, :head_count],
        row_sum[types + 4],
        up_sum,
        down_sum,
        row_sum[types : types + 3],
    )


def solution(mesh):
    rows = ("fsdp", "seq")
    return jax.shard_map(
        body,
        mesh=mesh,
        in_specs=(
            P(None, rows, None),
            P(None, rows),
            P(None, "fsdp", None),
            P(None, "fsdp", None),
            P(None, None, "fsdp"),
            P(None, "fsdp"),
            P(None, "fsdp"),
            P("fsdp", None),
            P("fsdp"),
            P("fsdp", None),
            P("fsdp", None),
            P("fsdp", None),
            P("fsdp", None),
            P("fsdp"),
            P("fsdp"),
            P("fsdp", None),
            P("fsdp"),
            P("fsdp", None),
            P("fsdp", None),
            P(None, "fsdp"),
            P(None, rows, None),
            P(None, None, rows),
        ),
        out_specs=(
            P(None, rows, None),
            P(None, None, rows),
            P(None, rows, None),
            P(None, "fsdp"),
            P(None, "fsdp"),
            P("fsdp", None),
            P("fsdp"),
            P("fsdp", None),
            P("fsdp", None),
            P("fsdp", None),
            P("fsdp", None),
            P("fsdp"),
            P("fsdp"),
            P("fsdp", None),
            P("fsdp"),
            P("fsdp", None),
            P("fsdp", None),
            P(None, "fsdp"),
        ),
        check_vma=False,
    )
```

time: 1180 us -> 389 us (0.33)
  waiting for transfers between devices: 786 us -> 76.4 us
  matrix products: 117 us -> 11.6 us
  blocking collectives: 45 us -> 0 us
  Pallas kernels: 139 us -> 180 us
  starting transfers between devices: 1.11 us -> 38.2 us
    reduce_scatter x9 -> x1, waiting for transfers between devices: 518 us -> 0.02 us  [reduce_big(): lax.psum_scatter(grad.reshape(chunks * quarters, rows, width), ('fsdp', '...]
    all_gather x8 -> x1, waiting for transfers between devices: 226 us -> 0.01 us  [gather_big(): big = lax.all_gather(after(quarter, *others), ('fsdp', 'seq'), axis=0)]
    ppermute x0 -> x37, waiting for transfers between devices: none -> 76.4 us  [the longest x22 54.4 us: flip(): lax.ppermute(value, axis, [(i, i ^ bit) for i in range(lax.axis_size(axis...]
    pallas_call x2 -> x9, Pallas kernels: 73.1 us -> 133 us  [the longest x3 37 us: pair_grads(): pl.pallas_call(functools.partial(pair_grad_kernel, micro), grid=(blocks,)...]
    dot_general x13 -> x5, matrix products: 56.2 us -> 3.82 us  [dot_low(): return jnp.dot(left, right, preferred_element_type=f32).astype(bf16)]
    ppermute x0 -> x37, starting transfers between devices: none -> 38.1 us  [the longest x15 24.3 us: along_line(): return lax.ppermute(value, 'fsdp', pairs)]
    psum x1 -> x0, waiting for transfers between devices: 37.1 us -> none  [reduce_shards(): return lax.psum(part, 'seq').astype(f32)[0]]
    all_gather x1 -> x0, blocking collectives: 33.4 us -> none  [body(): lax.all_gather(jnp.concatenate([small, kernel_rows], axis=0), 'fsdp', axi...]
  transfers between devices with their start and end apart: 18 -> 39, of which waited for: 16 -> 16; matrix products, arithmetic and copies ran while one was open for 12% -> 13% of each run, Pallas kernels for 9% -> 41%
where the time goes in v2:
time: 389 us; the launch traced here: 382 us
  Pallas kernels  180 us (46%)
  waiting for transfers between devices  76.4 us (20%)
  starting transfers between devices  38.2 us (10%)
  other arithmetic  28.4 us (7%)
  local copies, waits for them, and re-layouts  26.2 us (7%)
  between operations  21.6 us (6%)
  matrix products  11.6 us (3%)
    ppermute x22, waiting for transfers between devices, flip(): lax.ppermute(value, axis, [(i, i ^ bit) for i in range(lax.axis_size(axis...  54.4 us
    pallas_call x3, Pallas kernels, pair_grads(): pl.pallas_call(functools.partial(pair_grad_kernel, micro), grid=(blocks,)...  37 us
    pallas_call x3, Pallas kernels, pair_bias(): pl.pallas_call(functools.partial(bias_kernel, micro), grid=(blocks,), in_...  36.8 us
    pallas_call x1, Pallas kernels, attend_back(): pl.pallas_call(functools.partial(attend_back_kernel, scale), grid=(micro_...  26.9 us
    ppermute x15, starting transfers between devices, along_line(): return lax.ppermute(value, 'fsdp', pairs)  24.3 us
    pallas_call x1, Pallas kernels, dense(): pl.pallas_call(dense_kernel, in_specs=[whole] * 5 + [away], out_specs=[wh...  24.3 us
    pallas_call x1, Pallas kernels, project_back(): pl.pallas_call(project_back_kernel, in_specs=[pl.BlockSpec(memory_space=p...  22 us
    ppermute x15, waiting for transfers between devices, along_line(): return lax.ppermute(value, 'fsdp', pairs)  22 us
  transfers between devices with their start and end apart: 39, of which 16 were waited for; matrix products, arithmetic and copies ran while one was open for 13% of the time, Pallas kernels for 41%

profile of v2, /device:TPU:0, one launch (start us, length us, event | category | flops | bytes accessed | tf_op | source)
XLA Modules:
  0.0 382.4 jit_solution(17054088745860643328)
XLA Ops:
  11.0 4.1 %collective-permute-start.1 = (bf16[208,128]{1,0:T(8,128)(2,1)S(1)}, bf16[208,128]{1,0:T(8,128)(2,1)S(1)}, u32[]{:S(2)}, u32[]{:S(2)}) collective-permute-start(bf16[208,128]{1,0:T(8,128)(2,1)S(1)} %fusion.59), channel_id=1, source_target_pairs={{0,16},{4,20},{8,24},{12,28},{16,0},{20,4},{24,8},{28,12},{1,17},{... | collective-permute-start | bytes 159752 | tf_op jit(solution)/shard_map/ppermute | solution.py:885
  20.5 2.9 collective-permute-start.11
  47.5 13.0 %pair_bias.3.rest_0_ = f32[3,4,4,1024,128]{4,3,2,1,0:T(8,128)} custom-call(s32[3,16]{1,0:T(4,128)} %select_select_fusion.flag_ref, f32[3,128,512]{2,1,0:T(8,128)} %sqrt.3.dist_ref, f32[3,128,512]{2,1,0:T(8,128)} %compare_select_fusion.mask_ref, f32[128,128]{1,0:T(8,128)} %broadcast_in_dim.148.mean_ref, f32[128,128]{1,0:T(8,128)} %broadcast_in_dim.150.coef_ref, ...), custom_call_target="tpu_custom_call" | custom-call | flops 440000000 | tf_op jit(solution)/shard_map/pair_bias/pallas_call | solution.py:165
  62.6 4.1 %collective-permute-start.7 = (f32[24,384]{1,0:T(8,128)S(1)}, f32[24,384]{1,0:T(8,128)S(1)}, u32[]{:S(2)}, u32[]{:S(2)}) collective-permute-start(f32[24,384]{1,0:T(8,128)S(1)} %get-tuple-element.233), channel_id=1, source_target_pairs={{0,24},{4,28},{8,0},{12,4},{16,8},{20,12},{24,16},{28,20},{1,25},{... | collective-permute-start | bytes 110600 | tf_op jit(solution)/shard_map/ppermute | solution.py:885
  68.7 4.8 %collective-permute-done.6 = f32[24,384]{1,0:T(8,128)S(1)} collective-permute-done((f32[24,384]{1,0:T(8,128)S(1)}, f32[24,384]{1,0:T(8,128)S(1)}, u32[]{:S(2)}, u32[]{:S(2)}) %collective-permute-start.6) | collective-permute-done | bytes 36896 | tf_op jit(solution)/shard_map/ppermute | solution.py:885
  73.6 11.8 %pair_bias.4.rest_0_ = f32[3,4,4,1024,128]{4,3,2,1,0:T(8,128)} custom-call(s32[3,16]{1,0:T(4,128)} %select_select_fusion.flag_ref, f32[3,128,512]{2,1,0:T(8,128)} %sqrt.3.dist_ref, f32[3,128,512]{2,1,0:T(8,128)} %compare_select_fusion.mask_ref, f32[128,128]{1,0:T(8,128)} %broadcast_in_dim.148.mean_ref, ...), custom_call_target="tpu_custom_call", output_to_operand_aliasing={{}: (7, {})} | custom-call | flops 440000000 | tf_op jit(solution)/shard_map/pair_bias/pallas_call | solution.py:165
  87.2 12.0 %pair_bias.5.bias_ref = f32[3,4,4,1024,128]{4,3,2,1,0:T(8,128)} custom-call(s32[3,16]{1,0:T(4,128)} %select_select_fusion.flag_ref, f32[3,128,512]{2,1,0:T(8,128)} %sqrt.3.dist_ref, f32[3,128,512]{2,1,0:T(8,128)} %compare_select_fusion.mask_ref, f32[128,128]{1,0:T(8,128)} %broadcast_in_dim.148.mean_ref, ...), custom_call_target="tpu_custom_call", output_to_operand_aliasing={{}: (7, {})} | custom-call | flops 440000000 | tf_op jit(solution)/shard_map/pair_bias/pallas_call | solution.py:165
  99.2 7.2 %collective-permute-done.15 = bf16[2,4,96,768]{3,2,1,0:T(8,128)(2,1)S(1)} collective-permute-done((bf16[2,4,96,768]{3,2,1,0:T(8,128)(2,1)S(1)}, bf16[2,4,96,768]{3,2,1,0:T(8,128)(2,1)S(1)}, u32[]{:S(2)}, u32[]{:S(2)}) %collective-permute-start.15) | collective-permute-done | bytes 1179680 | tf_op jit(solution)/shard_map/ppermute | solution.py:878
  109.7 13.1 %collective-permute-done.10.a2 = bf16[384,768]{1,0:T(8,128)(2,1)S(1)} collective-permute-done((bf16[384,768]{1,0:T(8,128)(2,1)S(1)}, bf16[384,768]{1,0:T(8,128)(2,1)S(1)}, u32[]{:S(2)}, u32[]{:S(2)}) %collective-permute-start.10) | collective-permute-done | bytes 589856 | tf_op jit(solution)/shard_map/ppermute | solution.py:878
  127.3 13.2 %project.1 = (bf16[3,128,1024]{2,1,0:T(8,128)(2,1)}, bf16[3,512,2048]{2,1,0:T(8,128)(2,1)}, bf16[3,512,768]{2,1,0:T(8,128)(2,1)}) custom-call(s32[4]{0:T(128)} %pad_add_fusion.at_ref, bf16[384,768]{1,0:T(8,128)(2,1)} %copy-done.6, bf16[384,768]{1,0:T(8,128)(2,1)} %copy-done.18, bf16[384,768]{1,0:T(8,128)(2,1)} %copy-done.17, bf16[384,768]{1,0:T(8,128)(2,1)} %copy-done.19, ...), custom_call_target="tpu_custom_call" | custom-call | flops 400000000 | tf_op jit(solution)/shard_map/project/pallas_call | solution.py:497
  140.5 19.8 %attend.1 = (bf16[3,4096,512]{2,1,0:T(8,128)(2,1)}, bf16[3,128,1024]{2,1,0:T(8,128)(2,1)}) custom-call(bf16[3,128,1024]{2,1,0:T(8,128)(2,1)} %get-tuple-element.65.query_ref, bf16[3,512,2048]{2,1,0:T(8,128)(2,1)} %get-tuple-element.66.key_ref.value_ref, bf16[3,512,2048]{2,1,0:T(8,128)(2,1)} %get-tuple-element.66.key_ref.value_ref, ...), custom_call_target="tpu_custom_call" | custom-call | flops 1200000000 | tf_op jit(solution)/shard_map/attend/pallas_call | solution.py:311
  160.3 24.3 %dense.1 = (bf16[384,768]{1,0:T(8,128)(2,1)}, f32[384,768]{1,0:T(8,128)}, bf16[384,1024]{1,0:T(8,128)(2,1)}, f32[1,768]{1,0:T(1,128)}, bf16[8,4,224,768]{3,2,1,0:T(8,128)(2,1)}) custom-call(bf16[384,1024]{1,0:T(8,128)(2,1)} %bitcast.343, f32[384,768]{1,0:T(8,128)} %bitcast.318, f32[384,768]{1,0:T(8,128)} %fusion.20.cot_ref, ...), custom_call_target="tpu_custom_call" | custom-call | flops 1000000000 | tf_op jit(solution)/shard_map/dense/pallas_call | solution.py:804
  184.6 26.9 %attend_back.1 = (f32[3,4,4,1024,128]{4,3,2,1,0:T(8,128)}, bf16[3,128,1024]{2,1,0:T(8,128)(2,1)}, bf16[3,512,1024]{2,1,0:T(8,128)(2,1)}, bf16[3,512,1024]{2,1,0:T(8,128)(2,1)}) custom-call(bf16[3,128,1024]{2,1,0:T(8,128)(2,1)} %get-tuple-element.65.query_ref, bf16[3,512,2048]{2,1,0:T(8,128)(2,1)} %get-tuple-element.66.key_ref.value_ref, ...), custom_call_target="tpu_custom_call" | custom-call | flops 1400000000 | tf_op jit(solution)/shard_map/attend_back/pallas_call | solution.py:390
  211.5 22.0 %project_back.1 = (f32[3,128,768]{2,1,0:T(8,128)}, bf16[2,384,768]{2,1,0:T(8,128)(2,1)}, bf16[2,384,768]{2,1,0:T(8,128)(2,1)}, bf16[2,768,768]{2,1,0:T(8,128)(2,1)}, bf16[2,768,768]{2,1,0:T(8,128)(2,1)}) custom-call(s32[4]{0:T(128)} %pad_add_fusion.at_ref, bf16[3,128,1024]{2,1,0:T(8,128)(2,1)} %get-tuple-element.72.query_ref, ...), custom_call_target="tpu_custom_call" | custom-call | flops 560000000 | tf_op jit(solution)/shard_map/project_back/pallas_call | solution.py:620
  234.7 13.5 %pair_grads.3 = f32[160,128]{1,0:T(8,128)} custom-call(s32[3,16]{1,0:T(4,128)} %select_select_fusion.flag_ref, f32[3,128,512]{2,1,0:T(8,128)} %sqrt.3.dist_ref, f32[3,4,4,1024,128]{4,3,2,1,0:T(8,128)} %get-tuple-element.80.score_ref, f32[128,128]{1,0:T(8,128)} %broadcast_in_dim.148.mean_ref, f32[128,128]{1,0:T(8,128)} %broadcast_in_dim.150.coef_ref), custom_call_target="tpu_custom_call" | custom-call | flops 560000000 | tf_op jit(solution)/shard_map/pair_grads/pallas_call | solution.py:237
  254.2 11.9 %pair_grads.4 = f32[160,128]{1,0:T(8,128)} custom-call(s32[3,16]{1,0:T(4,128)} %select_select_fusion.flag_ref, f32[3,128,512]{2,1,0:T(8,128)} %sqrt.3.dist_ref, f32[3,4,4,1024,128]{4,3,2,1,0:T(8,128)} %get-tuple-element.80.score_ref, f32[128,128]{1,0:T(8,128)} %broadcast_in_dim.148.mean_ref, f32[128,128]{1,0:T(8,128)} %broadcast_in_dim.150.coef_ref), custom_call_target="tpu_custom_call" | custom-call | flops 560000000 | tf_op jit(solution)/shard_map/pair_grads/pallas_call | solution.py:237
  273.0 3.0 collective-permute-start.20
  276.9 16.0 %collective-permute-done.22 = bf16[2,4,96,768]{3,2,1,0:T(8,128)(2,1)} collective-permute-done((bf16[2,4,96,768]{3,2,1,0:T(8,128)(2,1)}, bf16[2,4,96,768]{3,2,1,0:T(8,128)(2,1)}, u32[]{:S(2)}, u32[]{:S(2)}) %collective-permute-start.22) | collective-permute-done | bytes 1179680 | tf_op jit(solution)/shard_map/ppermute | solution.py:878
  301.1 11.6 %pair_grads.5 = f32[160,128]{1,0:T(8,128)} custom-call(s32[3,16]{1,0:T(4,128)} %select_select_fusion.flag_ref, f32[3,128,512]{2,1,0:T(8,128)} %sqrt.3.dist_ref, f32[3,4,4,1024,128]{4,3,2,1,0:T(8,128)} %get-tuple-element.80.score_ref, f32[128,128]{1,0:T(8,128)} %broadcast_in_dim.148.mean_ref, f32[128,128]{1,0:T(8,128)} %broadcast_in_dim.150.coef_ref), custom_call_target="tpu_custom_call" | custom-call | flops 560000000 | tf_op jit(solution)/shard_map/pair_grads/pallas_call | solution.py:237
  318.0 6.1 %collective-permute-done.21 = bf16[8,176,128]{2,1,0:T(8,128)(2,1)} collective-permute-done((bf16[8,176,128]{2,1,0:T(8,128)(2,1)S(1)}, bf16[8,176,128]{2,1,0:T(8,128)(2,1)}, u32[]{:S(2)}, u32[]{:S(2)}) %collective-permute-start.21) | collective-permute-done | bytes 360480 | tf_op jit(solution)/shard_map/ppermute | solution.py:878
  331.2 5.8 %collective-permute-done.28 = bf16[912,128]{1,0:T(8,128)(2,1)S(1)} collective-permute-done((bf16[912,128]{1,0:T(8,128)(2,1)S(1)}, bf16[912,128]{1,0:T(8,128)(2,1)S(1)}, u32[]{:S(2)}, u32[]{:S(2)}) %collective-permute-start.28) | collective-permute-done | bytes 233504 | tf_op jit(solution)/shard_map/ppermute | solution.py:878
  337.1 2.7 collective-permute-done.32
  339.8 6.9 %collective-permute-done.31 = bf16[96,768]{1,0:T(8,128)(2,1)S(1)} collective-permute-done((bf16[96,768]{1,0:T(8,128)(2,1)S(1)}, bf16[96,768]{1,0:T(8,128)(2,1)S(1)}, u32[]{:S(2)}, u32[]{:S(2)}) %collective-permute-start.31) | collective-permute-done | bytes 147488 | tf_op jit(solution)/shard_map/ppermute | solution.py:885
  354.9 4.9 %collective-permute-done.34 = bf16[480,128]{1,0:T(8,128)(2,1)S(1)} collective-permute-done((bf16[480,128]{1,0:T(8,128)(2,1)S(1)}, bf16[480,128]{1,0:T(8,128)(2,1)S(1)}, u32[]{:S(2)}, u32[]{:S(2)}) %collective-permute-start.34) | collective-permute-done | bytes 122912 | tf_op jit(solution)/shard_map/ppermute | solution.py:885
  (381 shorter events, 99.2 us)
Async XLA Ops:
  7.3 153.0 %all-gather.3.cloned.1.call-start = ((), (), s32[]{:S(2)}) async-start(), calls=%async_computation.2 | async-start | bytes 11354112 | tf_op jit(solution)/shard_map/all_gather | solution.py:1006
  10.1 336.9 %reduce-scatter.2.cloned.1.call-start = ((), (), s32[]{:S(2)}) async-start(), calls=%async_computation.1 | async-start | bytes 11354112 | tf_op jit(solution)/shard_map/reduce_scatter | solution.py:1026
  11.0 22.5 %collective-permute-start.1 = (bf16[208,128]{1,0:T(8,128)(2,1)S(1)}, bf16[208,128]{1,0:T(8,128)(2,1)S(1)}, u32[]{:S(2)}, u32[]{:S(2)}) collective-permute-start(bf16[208,128]{1,0:T(8,128)(2,1)S(1)} %fusion.59), channel_id=1, source_target_pairs={{0,16},{4,20},{8,24},{12,28},{16,0},{20,4},{24,8},{28,12},{1,17},{... | collective-permute-start | bytes 159752 | tf_op jit(solution)/shard_map/ppermute | solution.py:885
  15.1 18.3 %collective-permute-start = (bf16[208,128]{1,0:T(8,128)(2,1)S(1)}, bf16[208,128]{1,0:T(8,128)(2,1)S(1)}, u32[]{:S(2)}, u32[]{:S(2)}) collective-permute-start(bf16[208,128]{1,0:T(8,128)(2,1)S(1)} %fusion.59), channel_id=1, source_target_pairs={{0,24},{4,28},{8,0},{12,4},{16,8},{20,12},{24,16},{28,20},{1,25},{... | collective-permute-start | bytes 159752 | tf_op jit(solution)/shard_map/ppermute | solution.py:885
  16.4 17.1 %collective-permute-start.2 = (bf16[208,128]{1,0:T(8,128)(2,1)S(1)}, bf16[208,128]{1,0:T(8,128)(2,1)S(1)}, u32[]{:S(2)}, u32[]{:S(2)}) collective-permute-start(bf16[208,128]{1,0:T(8,128)(2,1)S(1)} %fusion.59), channel_id=1, source_target_pairs={{0,8},{4,12},{8,16},{12,20},{16,24},{20,28},{24,0},{28,4},{1,9},{5... | collective-permute-start | bytes 159752 | tf_op jit(solution)/shard_map/ppermute | solution.py:885
  19.4 41.2 %collective-permute-start.12 = (bf16[2,96,768]{2,1,0:T(8,128)(2,1)S(1)}, bf16[2,96,768]{2,1,0:T(8,128)(2,1)S(1)}, u32[]{:S(2)}, u32[]{:S(2)}) collective-permute-start(bf16[2,96,768]{2,1,0:T(8,128)(2,1)S(1)} %pad_maximum_fusion.8), channel_id=1, source_target_pairs={{0,16},{4,20},{8,24},{12,28},{16,0},{20,4},{24,8},{28,12},{1,17},{... | collective-permute-start | bytes 884744 | tf_op jit(solution)/shard_map/ppermute | solution.py:885
  20.5 40.0 %collective-permute-start.11 = (bf16[2,96,768]{2,1,0:T(8,128)(2,1)S(1)}, bf16[2,96,768]{2,1,0:T(8,128)(2,1)S(1)}, u32[]{:S(2)}, u32[]{:S(2)}) collective-permute-start(bf16[2,96,768]{2,1,0:T(8,128)(2,1)S(1)} %pad_maximum_fusion.8), channel_id=1, source_target_pairs={{0,24},{4,28},{8,0},{12,4},{16,8},{20,12},{24,16},{28,20},{1,25},{... | collective-permute-start | bytes 884744 | tf_op jit(solution)/shard_map/ppermute | solution.py:885
  33.4 27.3 %collective-permute-start.13 = (bf16[2,96,768]{2,1,0:T(8,128)(2,1)S(1)}, bf16[2,96,768]{2,1,0:T(8,128)(2,1)S(1)}, u32[]{:S(2)}, u32[]{:S(2)}) collective-permute-start(bf16[2,96,768]{2,1,0:T(8,128)(2,1)S(1)} %pad_maximum_fusion.8), channel_id=1, source_target_pairs={{0,8},{4,12},{8,16},{12,20},{16,24},{20,28},{24,0},{28,4},{1,9},{5... | collective-permute-start | bytes 884744 | tf_op jit(solution)/shard_map/ppermute | solution.py:885
  40.6 20.2 %collective-permute-start.4 = (f32[4,24,384]{2,1,0:T(8,128)S(1)}, f32[4,24,384]{2,1,0:T(8,128)}, u32[]{:S(2)}, u32[]{:S(2)}) collective-permute-start(f32[4,24,384]{2,1,0:T(8,128)S(1)} %dynamic-slice_bitcast_fusion.6), channel_id=1, source_target_pairs={{0,4},{4,0},{8,12},{12,8},{16,20},{20,16},{24,28},{28,24},{1,5},{5... | collective-permute-start | bytes 442376 | tf_op jit(solution)/shard_map/ppermute | solution.py:878
  67.3 39.1 %collective-permute-start.15 = (bf16[2,4,96,768]{3,2,1,0:T(8,128)(2,1)S(1)}, bf16[2,4,96,768]{3,2,1,0:T(8,128)(2,1)S(1)}, u32[]{:S(2)}, u32[]{:S(2)}) collective-permute-start(bf16[2,4,96,768]{3,2,1,0:T(8,128)(2,1)S(1)} %constant_dynamic-slice_fusion.3), channel_id=1, source_target_pairs={{0,4},{4,0},{8,12},{12,8},{16,20},{20,16},{24,28},{28,24},{1,5},{5... | collective-permute-start | bytes 3538952 | tf_op jit(solution)/shard_map/ppermute | solution.py:878
  106.9 18.0 %collective-permute-start.16 = (bf16[2,768,768]{2,1,0:T(8,128)(2,1)S(1)}, bf16[2,768,768]{2,1,0:T(8,128)(2,1)S(1)}, u32[]{:S(2)}, u32[]{:S(2)}) collective-permute-start(bf16[2,768,768]{2,1,0:T(8,128)(2,1)S(1)} %bitcast.319), channel_id=1, source_target_pairs={{0,1},{1,0},{2,3},{3,2},{4,5},{5,4},{6,7},{7,6},{8,9},{9,8},{10,11... | collective-permute-start | bytes 7077896 | tf_op jit(solution)/shard_map/ppermute | solution.py:878
  107.3 15.5 %collective-permute-start.10 = (bf16[384,768]{1,0:T(8,128)(2,1)S(1)}, bf16[384,768]{1,0:T(8,128)(2,1)S(1)}, u32[]{:S(2)}, u32[]{:S(2)}) collective-permute-start(bf16[384,768]{1,0:T(8,128)(2,1)S(1)} %multiply_convert_fusion.a0.own_ref), channel_id=1, source_target_pairs={{0,2},{1,3},{2,0},{3,1},{4,6},{5,7},{6,4},{7,5},{8,10},{9,11},{10,... | collective-permute-start | bytes 1769480 | tf_op jit(solution)/shard_map/ppermute | solution.py:878
  109.7 15.2 %collective-permute-start.9 = (bf16[384,768]{1,0:T(8,128)(2,1)S(1)}, bf16[384,768]{1,0:T(8,128)(2,1)S(1)}, u32[]{:S(2)}, u32[]{:S(2)}) collective-permute-start(bf16[384,768]{1,0:T(8,128)(2,1)S(1)} %multiply_convert_fusion.a0.own_ref), channel_id=1, source_target_pairs={{0,1},{1,0},{2,3},{3,2},{4,5},{5,4},{6,7},{7,6},{8,9},{9,8},{10,11... | collective-permute-start | bytes 1769480 | tf_op jit(solution)/shard_map/ppermute | solution.py:878
  233.5 16.4 %collective-permute-start.19 = (bf16[2,768,768]{2,1,0:T(8,128)(2,1)}, bf16[2,768,768]{2,1,0:T(8,128)(2,1)}, u32[]{:S(2)}, u32[]{:S(2)}) collective-permute-start(bf16[2,768,768]{2,1,0:T(8,128)(2,1)} %get-tuple-element.83), channel_id=1, source_target_pairs={{0,1},{1,0},{2,3},{3,2},{4,5},{5,4},{6,7},{7,6},{8,9},{9,8},{10,11... | collective-permute-start | bytes 7077896 | tf_op jit(solution)/shard_map/ppermute | solution.py:878
  234.1 15.1 %collective-permute-start.17 = (bf16[2,384,768]{2,1,0:T(8,128)(2,1)}, bf16[2,384,768]{2,1,0:T(8,128)(2,1)S(1)}, u32[]{:S(2)}, u32[]{:S(2)}) collective-permute-start(bf16[2,384,768]{2,1,0:T(8,128)(2,1)} %get-tuple-element.78), channel_id=1, source_target_pairs={{0,1},{1,0},{2,3},{3,2},{4,5},{5,4},{6,7},{7,6},{8,9},{9,8},{10,11... | collective-permute-start | bytes 3538952 | tf_op jit(solution)/shard_map/ppermute | solution.py:878
  249.5 18.1 %collective-permute-start.18 = (bf16[384,768]{1,0:T(8,128)(2,1)S(1)}, bf16[384,768]{1,0:T(8,128)(2,1)S(1)}, u32[]{:S(2)}, u32[]{:S(2)}) collective-permute-start(bf16[384,768]{1,0:T(8,128)(2,1)S(1)} %slice_bitcast_fusion.4), channel_id=1, source_target_pairs={{0,2},{1,3},{2,0},{3,1},{4,6},{5,7},{6,4},{7,5},{8,10},{9,11},{10,... | collective-permute-start | bytes 1769480 | tf_op jit(solution)/shard_map/ppermute | solution.py:878
  254.2 38.7 %collective-permute-start.22 = (bf16[2,4,96,768]{3,2,1,0:T(8,128)(2,1)}, bf16[2,4,96,768]{3,2,1,0:T(8,128)(2,1)}, u32[]{:S(2)}, u32[]{:S(2)}) collective-permute-start(bf16[2,4,96,768]{3,2,1,0:T(8,128)(2,1)} %dynamic-slice_bitcast_fusion), channel_id=1, source_target_pairs={{0,4},{4,0},{8,12},{12,8},{16,20},{20,16},{24,28},{28,24},{1,5},{5... | collective-permute-start | bytes 3538952 | tf_op jit(solution)/shard_map/ppermute | solution.py:878
  273.0 26.0 %collective-permute-start.20 = (bf16[8,176,128]{2,1,0:T(8,128)(2,1)}, bf16[8,176,128]{2,1,0:T(8,128)(2,1)}, u32[]{:S(2)}, u32[]{:S(2)}) collective-permute-start(bf16[8,176,128]{2,1,0:T(8,128)(2,1)} %bitcast.315), channel_id=1, source_target_pairs={{0,1},{1,0},{2,3},{3,2},{4,5},{5,4},{6,7},{7,6},{8,9},{9,8},{10,11... | collective-permute-start | bytes 1081352 | tf_op jit(solution)/shard_map/ppermute | solution.py:878
  294.5 22.6 %collective-permute-start.24 = (bf16[4,96,768]{2,1,0:T(8,128)(2,1)S(1)}, bf16[4,96,768]{2,1,0:T(8,128)(2,1)S(1)}, u32[]{:S(2)}, u32[]{:S(2)}) collective-permute-start(bf16[4,96,768]{2,1,0:T(8,128)(2,1)S(1)} %slice_bitcast_fusion.2), channel_id=1, source_target_pairs={{0,2},{1,3},{2,0},{3,1},{4,6},{5,7},{6,4},{7,5},{8,10},{9,11},{10,... | collective-permute-start | bytes 1769480 | tf_op jit(solution)/shard_map/ppermute | solution.py:878
  297.9 18.5 %collective-permute-start.27 = (f32[24,768]{1,0:T(8,128)S(1)}, f32[24,768]{1,0:T(8,128)S(1)}, u32[]{:S(2)}, u32[]{:S(2)}) collective-permute-start(f32[24,768]{1,0:T(8,128)S(1)} %add.450), channel_id=1, source_target_pairs={{0,2},{1,3},{2,0},{3,1},{4,6},{5,7},{6,4},{7,5},{8,10},{9,11},{10,... | collective-permute-start | bytes 221192 | tf_op jit(solution)/shard_map/ppermute | solution.py:878
  300.1 24.0 %collective-permute-start.21 = (bf16[8,176,128]{2,1,0:T(8,128)(2,1)S(1)}, bf16[8,176,128]{2,1,0:T(8,128)(2,1)}, u32[]{:S(2)}, u32[]{:S(2)}) collective-permute-start(bf16[8,176,128]{2,1,0:T(8,128)(2,1)S(1)} %fusion.122), channel_id=1, source_target_pairs={{0,2},{1,3},{2,0},{3,1},{4,6},{5,7},{6,4},{7,5},{8,10},{9,11},{10,... | collective-permute-start | bytes 1081352 | tf_op jit(solution)/shard_map/ppermute | solution.py:878
  327.4 12.4 %collective-permute-start.32 = (bf16[96,768]{1,0:T(8,128)(2,1)S(1)}, bf16[96,768]{1,0:T(8,128)(2,1)S(1)}, u32[]{:S(2)}, u32[]{:S(2)}) collective-permute-start(bf16[96,768]{1,0:T(8,128)(2,1)S(1)} %get-tuple-element.217), channel_id=1, source_target_pairs={{0,24},{4,28},{8,0},{12,4},{16,8},{20,12},{24,16},{28,20},{1,25},{... | collective-permute-start | bytes 442376 | tf_op jit(solution)/shard_map/ppermute | solution.py:885
  329.5 17.3 %collective-permute-start.31 = (bf16[96,768]{1,0:T(8,128)(2,1)S(1)}, bf16[96,768]{1,0:T(8,128)(2,1)S(1)}, u32[]{:S(2)}, u32[]{:S(2)}) collective-permute-start(bf16[96,768]{1,0:T(8,128)(2,1)S(1)} %get-tuple-element.218), channel_id=1, source_target_pairs={{0,16},{4,20},{8,24},{12,28},{16,0},{20,4},{24,8},{28,12},{1,17},{... | collective-permute-start | bytes 442376 | tf_op jit(solution)/shard_map/ppermute | solution.py:885
  348.0 13.7 %collective-permute-start.35 = (bf16[320,768]{1,0:T(8,128)(2,1)S(1)}, bf16[320,768]{1,0:T(8,128)(2,1)S(1)}, u32[]{:S(2)}, u32[]{:S(2)}) collective-permute-start(bf16[320,768]{1,0:T(8,128)(2,1)S(1)} %pad_maximum_fusion.4), channel_id=1, source_target_pairs={{0,2},{1,3},{2,0},{3,1},{4,6},{5,7},{6,4},{7,5},{8,10},{9,11},{10,... | collective-permute-start | bytes 1474568 | tf_op jit(solution)/shard_map/ppermute | solution.py:878
  (82 other events, 781.1 us)
Sparse Core Ops, SparseCore 0:
  11.0 115.7 all-gather.2
  184.7 155.6 reduce-scatter.1

commit v3 on v2

--- a/solution.py
+++ b/solution.py
@@ -447,7 +447,23 @@
 
 
 def project_kernel(
-    at_ref, a0, a1, a2, a3, w0, w1, query_ref, both_ref, rolled_ref, rows, weights, sems
+    at_ref,
+    a0,
+    a1,
+    a2,
+    a3,
+    w0,
+    w1,
+    query_out,
+    both_out,
+    rolled_out,
+    rows,
+    weights,
+    query_ref,
+    both_ref,
+    rolled_ref,
+    sems,
+    out_sems,
 ):
     micro_count, group_rows, width = rolled_ref.shape
     tok_rows = group_rows // 4
@@ -469,6 +485,15 @@
         )
         turn = roll_matrix(group_rows, at_ref[1 + micro])
         rolled_ref[micro] = dot_wide(turn, group).astype(bf16)
+
+    def leave(micro):
+        return [
+            pltpu.make_async_copy(ref.at[micro], out.at[micro], out_sems.at[3 * micro + i])
+            for i, (ref, out) in enumerate(
+                ((query_ref, query_out), (both_ref, both_out), (rolled_ref, rolled_out))
+            )
+        ]
+
     for copy in weight_copies:
         copy.wait()
 
@@ -483,9 +508,14 @@
             both_ref[micro, :, offset : offset + last - first] = dot_wide(
                 group, weights[block, :, first:last]
             ).astype(bf16)
+        for copy in leave(micro):
+            copy.start()
         return carry
 
     lax.fori_loop(0, micro_count, one, 0)
+    for micro in range(micro_count):
+        for copy in leave(micro):
+            copy.wait()
 
 
 def project(places, rows, weights, micro_count, wide):
@@ -493,12 +523,11 @@
     tok_rows = total_rows // micro_count
     group_rows = 4 * tok_rows
     block_width = weights[0].shape[2]
-    whole = pl.BlockSpec(memory_space=pltpu.VMEM)
     return pl.pallas_call(
         project_kernel,
         in_specs=[pl.BlockSpec(memory_space=pltpu.SMEM)]
         + [pl.BlockSpec(memory_space=pl.ANY)] * 6,
-        out_specs=[whole] * 3,
+        out_specs=[pl.BlockSpec(memory_space=pl.ANY)] * 3,
         out_shape=[
             jax.ShapeDtypeStruct((micro_count, tok_rows, wide), bf16),
             jax.ShapeDtypeStruct((micro_count, group_rows, 2 * wide), bf16),
@@ -507,7 +536,11 @@
         scratch_shapes=[
             pltpu.VMEM((4, total_rows, width), bf16),
             pltpu.VMEM((4, width, block_width), bf16),
+            pltpu.VMEM((micro_count, tok_rows, wide), bf16),
+            pltpu.VMEM((micro_count, group_rows, 2 * wide), bf16),
+            pltpu.VMEM((micro_count, group_rows, width), bf16),
             pltpu.SemaphoreType.DMA((8,)),
+            pltpu.SemaphoreType.DMA((3 * micro_count,)),
         ],
         compiler_params=pltpu.CompilerParams(vmem_limit_bytes=VMEM_LIMIT),
         cost_estimate=cost(10),

time: 389 us -> 387 us (level)
  transfers between devices with their start and end apart: 39 -> 39, of which waited for: 16 -> 17; matrix products, arithmetic and copies ran while one was open for 13% -> 13% of each run, Pallas kernels for 41% -> 41%
where the time goes in v3:
time: 387 us; the launch traced here: 380 us
  Pallas kernels  182 us (47%)
  waiting for transfers between devices  74.6 us (19%)
  starting transfers between devices  35.4 us (9%)
  other arithmetic  28.5 us (7%)
  local copies, waits for them, and re-layouts  26.4 us (7%)
  between operations  21.6 us (6%)
  matrix products  11.6 us (3%)
    ppermute x22, waiting for transfers between devices, flip(): lax.ppermute(value, axis, [(i, i ^ bit) for i in range(lax.axis_size(axis...  52.6 us
    pallas_call x3, Pallas kernels, pair_grads(): pl.pallas_call(functools.partial(pair_grad_kernel, micro), grid=(blocks,)...  38.7 us
    pallas_call x3, Pallas kernels, pair_bias(): pl.pallas_call(functools.partial(bias_kernel, micro), grid=(blocks,), in_...  38.6 us
    pallas_call x1, Pallas kernels, attend_back(): pl.pallas_call(functools.partial(attend_back_kernel, scale), grid=(micro_...  27 us
    pallas_call x1, Pallas kernels, dense(): pl.pallas_call(dense_kernel, in_specs=[whole] * 5 + [away], out_specs=[wh...  24.3 us
    ppermute x15, starting transfers between devices, along_line(): return lax.ppermute(value, 'fsdp', pairs)  23.5 us
    pallas_call x1, Pallas kernels, project_back(): pl.pallas_call(project_back_kernel, in_specs=[pl.BlockSpec(memory_space=p...  22 us
    ppermute x15, waiting for transfers between devices, along_line(): return lax.ppermute(value, 'fsdp', pairs)  21.9 us
  transfers between devices with their start and end apart: 39, of which 17 were waited for; matrix products, arithmetic and copies ran while one was open for 13% of the time, Pallas kernels for 41%

profile of v3, /device:TPU:0, one launch (start us, length us, event | category | flops | bytes accessed | tf_op | source)
XLA Modules:
  0.0 379.9 jit_solution(11796920477303531289)
XLA Ops:
  11.0 4.1 %collective-permute-start.1 = (bf16[208,128]{1,0:T(8,128)(2,1)S(1)}, bf16[208,128]{1,0:T(8,128)(2,1)S(1)}, u32[]{:S(2)}, u32[]{:S(2)}) collective-permute-start(bf16[208,128]{1,0:T(8,128)(2,1)S(1)} %fusion.59), channel_id=1, source_target_pairs={{0,16},{4,20},{8,24},{12,28},{16,0},{20,4},{24,8},{28,12},{1,17},{... | collective-permute-start | bytes 159752 | tf_op jit(solution)/shard_map/ppermute | solution.py:918
  20.5 2.9 collective-permute-start.11
  47.5 13.7 %pair_bias.3.rest_0_ = f32[3,4,4,1024,128]{4,3,2,1,0:T(8,128)} custom-call(s32[3,16]{1,0:T(4,128)} %select_select_fusion.flag_ref, f32[3,128,512]{2,1,0:T(8,128)} %sqrt.3.dist_ref, f32[3,128,512]{2,1,0:T(8,128)} %compare_select_fusion.mask_ref, f32[128,128]{1,0:T(8,128)} %broadcast_in_dim.148.mean_ref, f32[128,128]{1,0:T(8,128)} %broadcast_in_dim.150.coef_ref, ...), custom_call_target="tpu_custom_call" | custom-call | flops 440000000 | tf_op jit(solution)/shard_map/pair_bias/pallas_call | solution.py:165
  63.7 2.9 collective-permute-start.7
  68.6 4.5 %collective-permute-done.6 = f32[24,384]{1,0:T(8,128)S(1)} collective-permute-done((f32[24,384]{1,0:T(8,128)S(1)}, f32[24,384]{1,0:T(8,128)S(1)}, u32[]{:S(2)}, u32[]{:S(2)}) %collective-permute-start.6) | collective-permute-done | bytes 36896 | tf_op jit(solution)/shard_map/ppermute | solution.py:918
  73.2 11.4 %pair_bias.4.rest_0_ = f32[3,4,4,1024,128]{4,3,2,1,0:T(8,128)} custom-call(s32[3,16]{1,0:T(4,128)} %select_select_fusion.flag_ref, f32[3,128,512]{2,1,0:T(8,128)} %sqrt.3.dist_ref, f32[3,128,512]{2,1,0:T(8,128)} %compare_select_fusion.mask_ref, f32[128,128]{1,0:T(8,128)} %broadcast_in_dim.148.mean_ref, ...), custom_call_target="tpu_custom_call", output_to_operand_aliasing={{}: (7, {})} | custom-call | flops 440000000 | tf_op jit(solution)/shard_map/pair_bias/pallas_call | solution.py:165
  86.5 13.5 %pair_bias.5.bias_ref = f32[3,4,4,1024,128]{4,3,2,1,0:T(8,128)} custom-call(s32[3,16]{1,0:T(4,128)} %select_select_fusion.flag_ref, f32[3,128,512]{2,1,0:T(8,128)} %sqrt.3.dist_ref, f32[3,128,512]{2,1,0:T(8,128)} %compare_select_fusion.mask_ref, f32[128,128]{1,0:T(8,128)} %broadcast_in_dim.148.mean_ref, ...), custom_call_target="tpu_custom_call", output_to_operand_aliasing={{}: (7, {})} | custom-call | flops 440000000 | tf_op jit(solution)/shard_map/pair_bias/pallas_call | solution.py:165
  100.0 5.8 %collective-permute-done.15 = bf16[2,4,96,768]{3,2,1,0:T(8,128)(2,1)S(1)} collective-permute-done((bf16[2,4,96,768]{3,2,1,0:T(8,128)(2,1)S(1)}, bf16[2,4,96,768]{3,2,1,0:T(8,128)(2,1)S(1)}, u32[]{:S(2)}, u32[]{:S(2)}) %collective-permute-start.15) | collective-permute-done | bytes 1179680 | tf_op jit(solution)/shard_map/ppermute | solution.py:911
  109.1 13.1 %collective-permute-done.10.a2 = bf16[384,768]{1,0:T(8,128)(2,1)S(1)} collective-permute-done((bf16[384,768]{1,0:T(8,128)(2,1)S(1)}, bf16[384,768]{1,0:T(8,128)(2,1)S(1)}, u32[]{:S(2)}, u32[]{:S(2)}) %collective-permute-start.10) | collective-permute-done | bytes 589856 | tf_op jit(solution)/shard_map/ppermute | solution.py:911
  127.1 11.5 %project.1 = (bf16[3,128,1024]{2,1,0:T(8,128)(2,1)}, bf16[3,512,2048]{2,1,0:T(8,128)(2,1)}, bf16[3,512,768]{2,1,0:T(8,128)(2,1)}) custom-call(s32[4]{0:T(128)} %pad_add_fusion.at_ref, bf16[384,768]{1,0:T(8,128)(2,1)} %copy-done.6, bf16[384,768]{1,0:T(8,128)(2,1)} %copy-done.18, bf16[384,768]{1,0:T(8,128)(2,1)} %copy-done.17, bf16[384,768]{1,0:T(8,128)(2,1)} %copy-done.19, ...), custom_call_target="tpu_custom_call" | custom-call | flops 400000000 | tf_op jit(solution)/shard_map/project/pallas_call | solution.py:526
  138.6 19.8 %attend.1 = (bf16[3,4096,512]{2,1,0:T(8,128)(2,1)}, bf16[3,128,1024]{2,1,0:T(8,128)(2,1)}) custom-call(bf16[3,128,1024]{2,1,0:T(8,128)(2,1)} %get-tuple-element.65.query_ref, bf16[3,512,2048]{2,1,0:T(8,128)(2,1)} %get-tuple-element.66.key_ref.value_ref, bf16[3,512,2048]{2,1,0:T(8,128)(2,1)} %get-tuple-element.66.key_ref.value_ref, ...), custom_call_target="tpu_custom_call" | custom-call | flops 1200000000 | tf_op jit(solution)/shard_map/attend/pallas_call | solution.py:311
  158.4 24.3 %dense.1 = (bf16[384,768]{1,0:T(8,128)(2,1)}, f32[384,768]{1,0:T(8,128)}, bf16[384,1024]{1,0:T(8,128)(2,1)}, f32[1,768]{1,0:T(1,128)}, bf16[8,4,224,768]{3,2,1,0:T(8,128)(2,1)}) custom-call(bf16[384,1024]{1,0:T(8,128)(2,1)} %bitcast.343, f32[384,768]{1,0:T(8,128)} %bitcast.318, f32[384,768]{1,0:T(8,128)} %fusion.20.cot_ref, ...), custom_call_target="tpu_custom_call" | custom-call | flops 1000000000 | tf_op jit(solution)/shard_map/dense/pallas_call | solution.py:837
  182.7 27.0 %attend_back.1 = (f32[3,4,4,1024,128]{4,3,2,1,0:T(8,128)}, bf16[3,128,1024]{2,1,0:T(8,128)(2,1)}, bf16[3,512,1024]{2,1,0:T(8,128)(2,1)}, bf16[3,512,1024]{2,1,0:T(8,128)(2,1)}) custom-call(bf16[3,128,1024]{2,1,0:T(8,128)(2,1)} %get-tuple-element.65.query_ref, bf16[3,512,2048]{2,1,0:T(8,128)(2,1)} %get-tuple-element.66.key_ref.value_ref, ...), custom_call_target="tpu_custom_call" | custom-call | flops 1400000000 | tf_op jit(solution)/shard_map/attend_back/pallas_call | solution.py:390
  209.7 22.0 %project_back.1 = (f32[3,128,768]{2,1,0:T(8,128)}, bf16[2,384,768]{2,1,0:T(8,128)(2,1)}, bf16[2,384,768]{2,1,0:T(8,128)(2,1)}, bf16[2,768,768]{2,1,0:T(8,128)(2,1)}, bf16[2,768,768]{2,1,0:T(8,128)(2,1)}) custom-call(s32[4]{0:T(128)} %pad_add_fusion.at_ref, bf16[3,128,1024]{2,1,0:T(8,128)(2,1)} %get-tuple-element.72.query_ref, ...), custom_call_target="tpu_custom_call" | custom-call | flops 560000000 | tf_op jit(solution)/shard_map/project_back/pallas_call | solution.py:653
  232.9 14.2 %pair_grads.3 = f32[160,128]{1,0:T(8,128)} custom-call(s32[3,16]{1,0:T(4,128)} %select_select_fusion.flag_ref, f32[3,128,512]{2,1,0:T(8,128)} %sqrt.3.dist_ref, f32[3,4,4,1024,128]{4,3,2,1,0:T(8,128)} %get-tuple-element.80.score_ref, f32[128,128]{1,0:T(8,128)} %broadcast_in_dim.148.mean_ref, f32[128,128]{1,0:T(8,128)} %broadcast_in_dim.150.coef_ref), custom_call_target="tpu_custom_call" | custom-call | flops 560000000 | tf_op jit(solution)/shard_map/pair_grads/pallas_call | solution.py:237
  253.1 11.4 %pair_grads.4 = f32[160,128]{1,0:T(8,128)} custom-call(s32[3,16]{1,0:T(4,128)} %select_select_fusion.flag_ref, f32[3,128,512]{2,1,0:T(8,128)} %sqrt.3.dist_ref, f32[3,4,4,1024,128]{4,3,2,1,0:T(8,128)} %get-tuple-element.80.score_ref, f32[128,128]{1,0:T(8,128)} %broadcast_in_dim.148.mean_ref, f32[128,128]{1,0:T(8,128)} %broadcast_in_dim.150.coef_ref), custom_call_target="tpu_custom_call" | custom-call | flops 560000000 | tf_op jit(solution)/shard_map/pair_grads/pallas_call | solution.py:237
  274.6 16.5 %collective-permute-done.22 = bf16[2,4,96,768]{3,2,1,0:T(8,128)(2,1)} collective-permute-done((bf16[2,4,96,768]{3,2,1,0:T(8,128)(2,1)}, bf16[2,4,96,768]{3,2,1,0:T(8,128)(2,1)}, u32[]{:S(2)}, u32[]{:S(2)}) %collective-permute-start.22) | collective-permute-done | bytes 1179680 | tf_op jit(solution)/shard_map/ppermute | solution.py:911
  298.9 13.1 %pair_grads.5 = f32[160,128]{1,0:T(8,128)} custom-call(s32[3,16]{1,0:T(4,128)} %select_select_fusion.flag_ref, f32[3,128,512]{2,1,0:T(8,128)} %sqrt.3.dist_ref, f32[3,4,4,1024,128]{4,3,2,1,0:T(8,128)} %get-tuple-element.80.score_ref, f32[128,128]{1,0:T(8,128)} %broadcast_in_dim.148.mean_ref, f32[128,128]{1,0:T(8,128)} %broadcast_in_dim.150.coef_ref), custom_call_target="tpu_custom_call" | custom-call | flops 560000000 | tf_op jit(solution)/shard_map/pair_grads/pallas_call | solution.py:237
  316.2 5.4 %collective-permute-done.21 = bf16[8,176,128]{2,1,0:T(8,128)(2,1)} collective-permute-done((bf16[8,176,128]{2,1,0:T(8,128)(2,1)S(1)}, bf16[8,176,128]{2,1,0:T(8,128)(2,1)}, u32[]{:S(2)}, u32[]{:S(2)}) %collective-permute-start.21) | collective-permute-done | bytes 360480 | tf_op jit(solution)/shard_map/ppermute | solution.py:911
  324.0 3.1 collective-permute-start.32
  329.5 5.7 %collective-permute-done.28 = bf16[912,128]{1,0:T(8,128)(2,1)S(1)} collective-permute-done((bf16[912,128]{1,0:T(8,128)(2,1)S(1)}, bf16[912,128]{1,0:T(8,128)(2,1)S(1)}, u32[]{:S(2)}, u32[]{:S(2)}) %collective-permute-start.28) | collective-permute-done | bytes 233504 | tf_op jit(solution)/shard_map/ppermute | solution.py:911
  337.7 6.5 %collective-permute-done.31 = bf16[96,768]{1,0:T(8,128)(2,1)S(1)} collective-permute-done((bf16[96,768]{1,0:T(8,128)(2,1)S(1)}, bf16[96,768]{1,0:T(8,128)(2,1)S(1)}, u32[]{:S(2)}, u32[]{:S(2)}) %collective-permute-start.31) | collective-permute-done | bytes 147488 | tf_op jit(solution)/shard_map/ppermute | solution.py:918
  347.0 2.8 collective-permute-start.33
  352.4 5.0 %collective-permute-done.34 = bf16[480,128]{1,0:T(8,128)(2,1)S(1)} collective-permute-done((bf16[480,128]{1,0:T(8,128)(2,1)S(1)}, bf16[480,128]{1,0:T(8,128)(2,1)S(1)}, u32[]{:S(2)}, u32[]{:S(2)}) %collective-permute-start.34) | collective-permute-done | bytes 122912 | tf_op jit(solution)/shard_map/ppermute | solution.py:918
  (381 shorter events, 98.2 us)
Async XLA Ops:
  7.3 151.1 %all-gather.3.cloned.1.call-start = ((), (), s32[]{:S(2)}) async-start(), calls=%async_computation.2 | async-start | bytes 11354112 | tf_op jit(solution)/shard_map/all_gather | solution.py:1039
  10.1 334.2 %reduce-scatter.2.cloned.1.call-start = ((), (), s32[]{:S(2)}) async-start(), calls=%async_computation.1 | async-start | bytes 11354112 | tf_op jit(solution)/shard_map/reduce_scatter | solution.py:1059
  11.0 22.5 %collective-permute-start.1 = (bf16[208,128]{1,0:T(8,128)(2,1)S(1)}, bf16[208,128]{1,0:T(8,128)(2,1)S(1)}, u32[]{:S(2)}, u32[]{:S(2)}) collective-permute-start(bf16[208,128]{1,0:T(8,128)(2,1)S(1)} %fusion.59), channel_id=1, source_target_pairs={{0,16},{4,20},{8,24},{12,28},{16,0},{20,4},{24,8},{28,12},{1,17},{... | collective-permute-start | bytes 159752 | tf_op jit(solution)/shard_map/ppermute | solution.py:918
  15.1 18.3 %collective-permute-start = (bf16[208,128]{1,0:T(8,128)(2,1)S(1)}, bf16[208,128]{1,0:T(8,128)(2,1)S(1)}, u32[]{:S(2)}, u32[]{:S(2)}) collective-permute-start(bf16[208,128]{1,0:T(8,128)(2,1)S(1)} %fusion.59), channel_id=1, source_target_pairs={{0,24},{4,28},{8,0},{12,4},{16,8},{20,12},{24,16},{28,20},{1,25},{... | collective-permute-start | bytes 159752 | tf_op jit(solution)/shard_map/ppermute | solution.py:918
  16.4 17.1 %collective-permute-start.2 = (bf16[208,128]{1,0:T(8,128)(2,1)S(1)}, bf16[208,128]{1,0:T(8,128)(2,1)S(1)}, u32[]{:S(2)}, u32[]{:S(2)}) collective-permute-start(bf16[208,128]{1,0:T(8,128)(2,1)S(1)} %fusion.59), channel_id=1, source_target_pairs={{0,8},{4,12},{8,16},{12,20},{16,24},{20,28},{24,0},{28,4},{1,9},{5... | collective-permute-start | bytes 159752 | tf_op jit(solution)/shard_map/ppermute | solution.py:918
  19.4 41.9 %collective-permute-start.12 = (bf16[2,96,768]{2,1,0:T(8,128)(2,1)S(1)}, bf16[2,96,768]{2,1,0:T(8,128)(2,1)S(1)}, u32[]{:S(2)}, u32[]{:S(2)}) collective-permute-start(bf16[2,96,768]{2,1,0:T(8,128)(2,1)S(1)} %pad_maximum_fusion.8), channel_id=1, source_target_pairs={{0,16},{4,20},{8,24},{12,28},{16,0},{20,4},{24,8},{28,12},{1,17},{... | collective-permute-start | bytes 884744 | tf_op jit(solution)/shard_map/ppermute | solution.py:918
  20.5 40.8 %collective-permute-start.11 = (bf16[2,96,768]{2,1,0:T(8,128)(2,1)S(1)}, bf16[2,96,768]{2,1,0:T(8,128)(2,1)S(1)}, u32[]{:S(2)}, u32[]{:S(2)}) collective-permute-start(bf16[2,96,768]{2,1,0:T(8,128)(2,1)S(1)} %pad_maximum_fusion.8), channel_id=1, source_target_pairs={{0,24},{4,28},{8,0},{12,4},{16,8},{20,12},{24,16},{28,20},{1,25},{... | collective-permute-start | bytes 884744 | tf_op jit(solution)/shard_map/ppermute | solution.py:918
  33.4 28.0 %collective-permute-start.13 = (bf16[2,96,768]{2,1,0:T(8,128)(2,1)S(1)}, bf16[2,96,768]{2,1,0:T(8,128)(2,1)S(1)}, u32[]{:S(2)}, u32[]{:S(2)}) collective-permute-start(bf16[2,96,768]{2,1,0:T(8,128)(2,1)S(1)} %pad_maximum_fusion.8), channel_id=1, source_target_pairs={{0,8},{4,12},{8,16},{12,20},{16,24},{20,28},{24,0},{28,4},{1,9},{5... | collective-permute-start | bytes 884744 | tf_op jit(solution)/shard_map/ppermute | solution.py:918
  40.6 20.9 %collective-permute-start.4 = (f32[4,24,384]{2,1,0:T(8,128)S(1)}, f32[4,24,384]{2,1,0:T(8,128)}, u32[]{:S(2)}, u32[]{:S(2)}) collective-permute-start(f32[4,24,384]{2,1,0:T(8,128)S(1)} %dynamic-slice_bitcast_fusion.6), channel_id=1, source_target_pairs={{0,4},{4,0},{8,12},{12,8},{16,20},{20,16},{24,28},{28,24},{1,5},{5... | collective-permute-start | bytes 442376 | tf_op jit(solution)/shard_map/ppermute | solution.py:911
  66.7 39.1 %collective-permute-start.15 = (bf16[2,4,96,768]{3,2,1,0:T(8,128)(2,1)S(1)}, bf16[2,4,96,768]{3,2,1,0:T(8,128)(2,1)S(1)}, u32[]{:S(2)}, u32[]{:S(2)}) collective-permute-start(bf16[2,4,96,768]{3,2,1,0:T(8,128)(2,1)S(1)} %constant_dynamic-slice_fusion.3), channel_id=1, source_target_pairs={{0,4},{4,0},{8,12},{12,8},{16,20},{20,16},{24,28},{28,24},{1,5},{5... | collective-permute-start | bytes 3538952 | tf_op jit(solution)/shard_map/ppermute | solution.py:911
  106.3 18.6 %collective-permute-start.16 = (bf16[2,768,768]{2,1,0:T(8,128)(2,1)S(1)}, bf16[2,768,768]{2,1,0:T(8,128)(2,1)S(1)}, u32[]{:S(2)}, u32[]{:S(2)}) collective-permute-start(bf16[2,768,768]{2,1,0:T(8,128)(2,1)S(1)} %bitcast.319), channel_id=1, source_target_pairs={{0,1},{1,0},{2,3},{3,2},{4,5},{5,4},{6,7},{7,6},{8,9},{9,8},{10,11... | collective-permute-start | bytes 7077896 | tf_op jit(solution)/shard_map/ppermute | solution.py:911
  106.7 15.5 %collective-permute-start.10 = (bf16[384,768]{1,0:T(8,128)(2,1)S(1)}, bf16[384,768]{1,0:T(8,128)(2,1)S(1)}, u32[]{:S(2)}, u32[]{:S(2)}) collective-permute-start(bf16[384,768]{1,0:T(8,128)(2,1)S(1)} %multiply_convert_fusion.a0.own_ref), channel_id=1, source_target_pairs={{0,2},{1,3},{2,0},{3,1},{4,6},{5,7},{6,4},{7,5},{8,10},{9,11},{10,... | collective-permute-start | bytes 1769480 | tf_op jit(solution)/shard_map/ppermute | solution.py:911
  109.0 15.2 %collective-permute-start.9 = (bf16[384,768]{1,0:T(8,128)(2,1)S(1)}, bf16[384,768]{1,0:T(8,128)(2,1)S(1)}, u32[]{:S(2)}, u32[]{:S(2)}) collective-permute-start(bf16[384,768]{1,0:T(8,128)(2,1)S(1)} %multiply_convert_fusion.a0.own_ref), channel_id=1, source_target_pairs={{0,1},{1,0},{2,3},{3,2},{4,5},{5,4},{6,7},{7,6},{8,9},{9,8},{10,11... | collective-permute-start | bytes 1769480 | tf_op jit(solution)/shard_map/ppermute | solution.py:911
  231.7 16.7 %collective-permute-start.19 = (bf16[2,768,768]{2,1,0:T(8,128)(2,1)}, bf16[2,768,768]{2,1,0:T(8,128)(2,1)}, u32[]{:S(2)}, u32[]{:S(2)}) collective-permute-start(bf16[2,768,768]{2,1,0:T(8,128)(2,1)} %get-tuple-element.83), channel_id=1, source_target_pairs={{0,1},{1,0},{2,3},{3,2},{4,5},{5,4},{6,7},{7,6},{8,9},{9,8},{10,11... | collective-permute-start | bytes 7077896 | tf_op jit(solution)/shard_map/ppermute | solution.py:911
  231.9 16.0 %collective-permute-start.17 = (bf16[2,384,768]{2,1,0:T(8,128)(2,1)}, bf16[2,384,768]{2,1,0:T(8,128)(2,1)S(1)}, u32[]{:S(2)}, u32[]{:S(2)}) collective-permute-start(bf16[2,384,768]{2,1,0:T(8,128)(2,1)} %get-tuple-element.78), channel_id=1, source_target_pairs={{0,1},{1,0},{2,3},{3,2},{4,5},{5,4},{6,7},{7,6},{8,9},{9,8},{10,11... | collective-permute-start | bytes 3538952 | tf_op jit(solution)/shard_map/ppermute | solution.py:911
  248.3 18.0 %collective-permute-start.18 = (bf16[384,768]{1,0:T(8,128)(2,1)S(1)}, bf16[384,768]{1,0:T(8,128)(2,1)S(1)}, u32[]{:S(2)}, u32[]{:S(2)}) collective-permute-start(bf16[384,768]{1,0:T(8,128)(2,1)S(1)} %slice_bitcast_fusion.4), channel_id=1, source_target_pairs={{0,2},{1,3},{2,0},{3,1},{4,6},{5,7},{6,4},{7,5},{8,10},{9,11},{10,... | collective-permute-start | bytes 1769480 | tf_op jit(solution)/shard_map/ppermute | solution.py:911
  253.1 38.1 %collective-permute-start.22 = (bf16[2,4,96,768]{3,2,1,0:T(8,128)(2,1)}, bf16[2,4,96,768]{3,2,1,0:T(8,128)(2,1)}, u32[]{:S(2)}, u32[]{:S(2)}) collective-permute-start(bf16[2,4,96,768]{3,2,1,0:T(8,128)(2,1)} %dynamic-slice_bitcast_fusion), channel_id=1, source_target_pairs={{0,4},{4,0},{8,12},{12,8},{16,20},{20,16},{24,28},{28,24},{1,5},{5... | collective-permute-start | bytes 3538952 | tf_op jit(solution)/shard_map/ppermute | solution.py:911
  271.7 25.6 %collective-permute-start.20 = (bf16[8,176,128]{2,1,0:T(8,128)(2,1)}, bf16[8,176,128]{2,1,0:T(8,128)(2,1)}, u32[]{:S(2)}, u32[]{:S(2)}) collective-permute-start(bf16[8,176,128]{2,1,0:T(8,128)(2,1)} %bitcast.315), channel_id=1, source_target_pairs={{0,1},{1,0},{2,3},{3,2},{4,5},{5,4},{6,7},{7,6},{8,9},{9,8},{10,11... | collective-permute-start | bytes 1081352 | tf_op jit(solution)/shard_map/ppermute | solution.py:911
  292.8 22.5 %collective-permute-start.24 = (bf16[4,96,768]{2,1,0:T(8,128)(2,1)S(1)}, bf16[4,96,768]{2,1,0:T(8,128)(2,1)S(1)}, u32[]{:S(2)}, u32[]{:S(2)}) collective-permute-start(bf16[4,96,768]{2,1,0:T(8,128)(2,1)S(1)} %slice_bitcast_fusion.2), channel_id=1, source_target_pairs={{0,2},{1,3},{2,0},{3,1},{4,6},{5,7},{6,4},{7,5},{8,10},{9,11},{10,... | collective-permute-start | bytes 1769480 | tf_op jit(solution)/shard_map/ppermute | solution.py:911
  295.7 18.9 %collective-permute-start.27 = (f32[24,768]{1,0:T(8,128)S(1)}, f32[24,768]{1,0:T(8,128)S(1)}, u32[]{:S(2)}, u32[]{:S(2)}) collective-permute-start(f32[24,768]{1,0:T(8,128)S(1)} %add.450), channel_id=1, source_target_pairs={{0,2},{1,3},{2,0},{3,1},{4,6},{5,7},{6,4},{7,5},{8,10},{9,11},{10,... | collective-permute-start | bytes 221192 | tf_op jit(solution)/shard_map/ppermute | solution.py:911
  298.4 23.2 %collective-permute-start.21 = (bf16[8,176,128]{2,1,0:T(8,128)(2,1)S(1)}, bf16[8,176,128]{2,1,0:T(8,128)(2,1)}, u32[]{:S(2)}, u32[]{:S(2)}) collective-permute-start(bf16[8,176,128]{2,1,0:T(8,128)(2,1)S(1)} %fusion.122), channel_id=1, source_target_pairs={{0,2},{1,3},{2,0},{3,1},{4,6},{5,7},{6,4},{7,5},{8,10},{9,11},{10,... | collective-permute-start | bytes 1081352 | tf_op jit(solution)/shard_map/ppermute | solution.py:911
  324.0 13.7 %collective-permute-start.32 = (bf16[96,768]{1,0:T(8,128)(2,1)S(1)}, bf16[96,768]{1,0:T(8,128)(2,1)S(1)}, u32[]{:S(2)}, u32[]{:S(2)}) collective-permute-start(bf16[96,768]{1,0:T(8,128)(2,1)S(1)} %get-tuple-element.217), channel_id=1, source_target_pairs={{0,24},{4,28},{8,0},{12,4},{16,8},{20,12},{24,16},{28,20},{1,25},{... | collective-permute-start | bytes 442376 | tf_op jit(solution)/shard_map/ppermute | solution.py:918
  327.0 17.1 %collective-permute-start.31 = (bf16[96,768]{1,0:T(8,128)(2,1)S(1)}, bf16[96,768]{1,0:T(8,128)(2,1)S(1)}, u32[]{:S(2)}, u32[]{:S(2)}) collective-permute-start(bf16[96,768]{1,0:T(8,128)(2,1)S(1)} %get-tuple-element.218), channel_id=1, source_target_pairs={{0,16},{4,20},{8,24},{12,28},{16,0},{20,4},{24,8},{28,12},{1,17},{... | collective-permute-start | bytes 442376 | tf_op jit(solution)/shard_map/ppermute | solution.py:918
  345.4 13.8 %collective-permute-start.35 = (bf16[320,768]{1,0:T(8,128)(2,1)S(1)}, bf16[320,768]{1,0:T(8,128)(2,1)S(1)}, u32[]{:S(2)}, u32[]{:S(2)}) collective-permute-start(bf16[320,768]{1,0:T(8,128)(2,1)S(1)} %pad_maximum_fusion.4), channel_id=1, source_target_pairs={{0,2},{1,3},{2,0},{3,1},{4,6},{5,7},{6,4},{7,5},{8,10},{9,11},{10,... | collective-permute-start | bytes 1474568 | tf_op jit(solution)/shard_map/ppermute | solution.py:911
  (82 other events, 773.4 us)
Sparse Core Ops, SparseCore 0:
  11.0 115.7 all-gather.2
  182.8 155.4 reduce-scatter.1
